TPU v7x, 32 devices: a whole 2x2x4 slice. The times are simulated.
32 devices in a mesh: member: 2 (over x), lat: 16 (over z, y, core).
Axes of the slice: x: 2, y: 2, z: 4, core: 2. Of those that a mesh axis runs over, the one named last changes fastest.
Arguments:
- state: float32 [256, 32, 1152], P('member', 'lat'), parts along dimension 0, may hold values from -6 to 6
- vertical_mix: float32 [8, 16, 16], replicated, may hold values from -1.5 to 1.5
- coupling: float32 [4, 8], replicated, may hold values from -2 to 2
- fractions: float32 [16, 1152], replicated, may hold values from 0.25 to 1
- weight_index: int32 [64], P(('member', 'lat')), parts along dimension 0, may hold values from 0 to 15
- band_bounds: int32 [17], replicated, may hold values from 0 to 32, as said below
- polar_mask: int32 [32], replicated, may hold values from 0 to 1, as said below
Outputs:
- state_out: float32 [256, 32, 1152], P(('member', 'lat')), parts along dimension 0
- ocean: float32 [4, 192, 1152], P(None, ('member', 'lat')), parts along dimension 1
There are 2 independent parts, one for each index of `member`. A program takes and returns all parts, laid end to end along the dimension named above; an argument that names none is the same for every part. Nothing has to cross between parts.
Inputs may be any that keep to these rules, and one draw needn't show every extreme that they name: `band_bounds`: starts at 0, ends at 32; entry o lies between o * 2 - 2/2 and o * 2 + 2/2 - 1; some owner's slots hold exactly 6 rows. `polar_mask`: 0 outside the first and the last 5 rows; 1 on rows 4 and 27.
All inputs are finite; a program needn't handle non-finite values.
Results may differ from a plain program's by a relative error of at most 0.00007.
Values sent between devices are 32-bit elements; how exact they have to be, the bound alone decides.
No kernel may reach another device: no remote copies, remote signals or barrier semaphores. Data moves between devices by JAX's collectives and lax.ppermute only.
A program may use at most 64 MiB of HBM per device.

v0:
```python
import jax
import jax.numpy as jnp
from jax import lax
from jax.sharding import PartitionSpec as P

COSCUT = 0.5
HIGHEST = lax.Precision.HIGHEST


def extended(cells, sides, width):
    for axis, dim in sides:
        count = lax.axis_size(axis)
        ends = count - 1
        head = lax.slice_in_dim(cells, 0, width, axis=dim)
        tail = lax.slice_in_dim(cells, cells.shape[dim] - width, cells.shape[dim], axis=dim)
        cells = jnp.concatenate(
            [
                lax.ppermute(tail, axis, [(i, (i + 1) % count) for i in range(ends)]),
                cells,
                lax.ppermute(head, axis, [((i + 1) % count, i) for i in range(ends)]),
            ],
            axis=dim,
        )
    return cells


def transform_table(lon_count):
    half_count = lon_count // 2
    sample = jnp.arange(lon_count, dtype=jnp.int32)
    column = jnp.arange(lon_count, dtype=jnp.int32)
    wavenumber = jnp.where(column <= half_count, column, column - half_count)
    phase_angle = (sample[:, None] * wavenumber[None, :] % lon_count).astype(jnp.float32) * (
        2.0 * jnp.pi / lon_count
    )
    dft_table = jnp.where(column[None, :] <= half_count, jnp.cos(phase_angle), jnp.sin(phase_angle))
    inverse_weight = (
        jnp.where((column == 0) | (column == half_count), 1.0, 2.0).astype(jnp.float32) / lon_count
    )
    return (dft_table, wavenumber, inverse_weight)


def row_damping(global_rows, mask_rows, lat_count, wavenumber, lon_count):
    latitude = jnp.pi * ((global_rows.astype(jnp.float32) + 0.5) / lat_count - 0.5)
    cos_square = jnp.cos(latitude) ** 2
    sin_square = jnp.sin(jnp.pi * wavenumber.astype(jnp.float32) / lon_count) ** 2
    damping = cos_square[:, None] / jnp.maximum(
        cos_square[:, None], COSCUT**2 * sin_square[None, :]
    )
    return jnp.where(mask_rows[:, None] == 1, damping, 1.0)


def polar_filter(fields, global_rows, mask_rows, lat_count):
    lon_count = fields.shape[-1]
    dft_table, wavenumber, inverse_weight = transform_table(lon_count)
    filter_gain = (
        row_damping(global_rows, mask_rows, lat_count, wavenumber, lon_count)
        * inverse_weight[None, :]
    )
    spectrum = jnp.einsum("arn,nk->ark", fields, dft_table, precision=HIGHEST)
    smoothed = jnp.einsum("ark,nk->arn", spectrum * filter_gain[None], dft_table, precision=HIGHEST)
    return jnp.where(mask_rows[None, :, None] == 1, smoothed, fields)


def body(state, vertical_mix, coupling, fractions, weight_index, band_bounds, polar_mask):
    field_count, level_count = (vertical_mix.shape[0], vertical_mix.shape[1])
    stack_count, row_count, lon_count = state.shape
    lat_count = polar_mask.shape[0]
    owner_index = lax.axis_index("lat")
    columns = state.reshape(field_count, level_count, row_count * lon_count)
    mixed_state = jnp.einsum("fkl,flc->fkc", vertical_mix, columns, precision=HIGHEST)
    bottom = mixed_state[:, level_count - 1]
    wind_speed = jnp.sqrt(bottom[0] ** 2 + bottom[1] ** 2 + 1.0)
    surface_flux = wind_speed[None, :] * jnp.dot(coupling, bottom, precision=HIGHEST)
    onehot = (
        weight_index[:, None] == jnp.arange(fractions.shape[0], dtype=jnp.int32)[None, :]
    ).astype(jnp.float32)
    row_fraction = jnp.dot(onehot, fractions, precision=HIGHEST)
    weighted = surface_flux.reshape(-1, row_count, lon_count) * row_fraction[None]
    stacked = mixed_state.reshape(stack_count, row_count, lon_count)
    global_rows = owner_index * row_count + jnp.arange(row_count, dtype=jnp.int32)
    mask_rows = lax.dynamic_slice_in_dim(polar_mask, owner_index * row_count, row_count)

    def apply_filter(values):
        return polar_filter(values, global_rows, mask_rows, lat_count)

    def keep_values(values):
        return values

    filtered = lax.cond(jnp.any(mask_rows == 1), apply_filter, keep_values, stacked)
    state_out = lax.all_to_all(filtered, "lat", split_axis=0, concat_axis=1, tiled=True)
    nearby = extended(weighted, (("lat", 1),), row_count)
    padded = jnp.concatenate(
        [nearby, jnp.zeros((nearby.shape[0], row_count, lon_count), jnp.float32)], axis=1
    )
    half_rows = row_count // 2
    band_start = band_bounds[owner_index] - half_rows
    band_length = band_bounds[owner_index + 1] - band_bounds[owner_index] + 2 * half_rows + 1
    local_start = band_start - (owner_index - 1) * row_count
    picked = lax.dynamic_slice_in_dim(padded, local_start, 3 * row_count, 1)
    valid_slot = jnp.arange(3 * row_count, dtype=jnp.int32) < band_length
    ocean = jnp.where(valid_slot[None, :, None], picked, 0.0)
    return (state_out, ocean)


def solution(mesh):
    return jax.shard_map(
        body,
        mesh=mesh,
        in_specs=(P("member", "lat", None), P(), P(), P(), P(("member", "lat")), P(), P()),
        out_specs=(P(("member", "lat"), None, None), P(None, ("member", "lat"), None)),
        check_vma=False,
    )
```

profile of v0, /device:TPU:15, one launch (start us, length us, event | category | flops | bytes accessed | tf_op | source)
XLA Modules:
  0.0 105.5 jit_solution(4231373884959775416)
XLA Ops:
  0.6 0.0 copy-start
  0.6 1.4 %compare_reduce_fusion = (pred[]{:T(512)}, s32[2]{0:T(128)S(1)}) fusion(s32[32]{0:T(128)} %param.15, s32[]{:T(128)S(6)} %select_n.67), kind=kLoop, calls=%fused_computation.59 | loop fusion | flops 3 | bytes 21 | tf_op jit(solution)/shard_map/reduce_or | solution.py:89
  2.7 0.0 copy-start.1
  2.7 2.3 %reshape.146 = f32[8,16,2304]{2,1,0:T(8,128)S(1)} reshape(f32[128,2,1152]{2,1,0:T(2,128)} %param.9) | data formatting | bytes 2359296 | tf_op jit(solution)/shard_map/reshape | solution.py:69
  5.0 1.1 %fusion.48 = f32[8,16,2304]{2,1,0:T(8,128)S(1)} fusion(f32[8,16,16]{2,1,0:T(8,128)S(1)} %copy-done.1, f32[8,16,2304]{2,1,0:T(8,128)S(1)} %reshape.146), kind=kOutput, calls=%fused_computation.65 | convolution fusion | flops 56623104 | bytes 2367488 | tf_op jit(solution)/shard_map/fkl,flc->fkc/dot_general | solution.py:70
  6.1 0.7 reshape.147
  6.8 1.1 %conditional.1 = (f32[128,2,1152]{2,0,1:T(8,128)}) conditional(s32[]{:T(128)} %convert_element_type.19, (f32[128,2,1152]{2,1,0:T(2,128)S(1)}) %tuple.18, (s32[2]{0:T(128)S(1)}, f32[128,2,1152]{2,1,0:T(2,128)S(1)}, s32[]{:T(128)}, s32[2]{0:T(128)S(1)}) %tuple.14), branch_computations={%region_1.0_spmd, %region_2.3_spmd} | conditional | flops 8180886528 | bytes 5952434 | solution.py:89
  6.8 1.1 %copy.18 = f32[128,2,1152]{2,0,1:T(8,128)} copy(f32[128,2,1152]{2,1,0:T(2,128)S(1)} %get-tuple-element.29) | data formatting | bytes 2359296 | tf_op jit(solution)/shard_map/reshape | solution.py:79
  7.9 3.2 %copy.15 = f32[128,2,1152]{2,1,0:T(2,128)} copy(f32[128,2,1152]{2,0,1:T(8,128)} %get-tuple-element.36) | data formatting | bytes 2359296 | tf_op jit(solution)/shard_map/cond | solution.py:89
  11.1 63.6 %all-to-all-start = ((f32[128,2,1152]{2,1,0:T(2,128)}), f32[128,2,1152]{2,1,0:T(2,128)S(1)}, u32[]{:S(2)}, u32[]{:S(2)}) async-start(f32[128,2,1152]{2,1,0:T(2,128)} %copy.15), calls=%async_computation | async-start | bytes 2359296 | tf_op jit(solution)/shard_map/all_to_all | solution.py:90
  74.7 0.1 slice.18
  74.8 0.1 sqrt_reduce_fusion
  74.9 0.2 fusion.43
  75.1 0.2 convolution_multiply_fusion
  75.3 2.3 %collective-permute-start.1 = (f32[4,2,1152]{2,0,1:T(4,128)S(1)}, f32[4,2,1152]{2,0,1:T(4,128)S(1)}, u32[]{:S(2)}, u32[]{:S(2)}) collective-permute-start(f32[4,2,1152]{2,0,1:T(4,128)S(1)} %broadcast_multiply_fusion), channel_id=1, source_target_pairs={{1,0},{2,1},{3,2},{4,3},{5,4},{6,5},{7,6},{8,7},{9,8},{10,9},{11,1... | collective-permute-start | bytes 110600 | tf_op jit(solution)/shard_map/ppermute | solution.py:20
  77.6 4.2 %collective-permute-start = (f32[4,2,1152]{2,0,1:T(4,128)S(1)}, f32[4,2,1152]{2,0,1:T(4,128)S(1)}, u32[]{:S(2)}, u32[]{:S(2)}) collective-permute-start(f32[4,2,1152]{2,0,1:T(4,128)S(1)} %broadcast_multiply_fusion), channel_id=1, source_target_pairs={{0,1},{1,2},{2,3},{3,4},{4,5},{5,6},{6,7},{7,8},{8,9},{9,10},{10,1... | collective-permute-start | bytes 110600 | tf_op jit(solution)/shard_map/ppermute | solution.py:18
  81.8 0.6 fusion.47
  84.4 0.1 pad_dynamic-slice_fusion.3
  84.5 18.4 %collective-permute-done.1 = f32[4,2,1152]{2,0,1:T(4,128)S(1)} collective-permute-done((f32[4,2,1152]{2,0,1:T(4,128)S(1)}, f32[4,2,1152]{2,0,1:T(4,128)S(1)}, u32[]{:S(2)}, u32[]{:S(2)}) %collective-permute-start.1) | collective-permute-done | bytes 36896 | tf_op jit(solution)/shard_map/ppermute | solution.py:20
  102.8 0.0 collective-permute-done
  102.8 0.7 fusion.39
  103.6 0.0 all-to-all-done
  103.6 0.1 copy.16
  103.7 1.8 %all_to_all.16 = f32[8,32,1152]{2,1,0:T(8,128)} reshape(f32[8,16,2,1152]{3,2,1,0:T(2,128)S(1)} %copy.16) | data formatting | bytes 2359296 | tf_op jit(solution)/shard_map/all_to_all | solution.py:90
  (12 shorter events, 0.0 us)
Async XLA Ops:
  0.6 74.2 %copy-start = (f32[16,1152]{1,0:T(8,128)S(1)}, f32[16,1152]{1,0:T(8,128)}, u32[]{:S(2)}) copy-start(f32[16,1152]{1,0:T(8,128)} %param.12) | copy-start | bytes 221188
  2.7 2.3 %copy-start.1 = (f32[8,16,16]{2,1,0:T(8,128)S(1)}, f32[8,16,16]{2,1,0:T(8,128)}, u32[]{:S(2)}) copy-start(f32[8,16,16]{2,1,0:T(8,128)} %param.10) | copy-start | bytes 24580
  11.1 63.7 %copy-start.4 = (s32[2]{0:T(128)S(1)}, s32[2]{0:T(128)}, u32[]{:S(2)}) copy-start(s32[2]{0:T(128)} %param.13) | copy-start | bytes 28
  11.1 64.0 %copy-start.2 = (f32[4,8]{1,0:T(4,128)S(1)}, f32[4,8]{1,0:T(4,128)}, u32[]{:S(2)}) copy-start(f32[4,8]{1,0:T(4,128)} %param.11) | copy-start | bytes 388
  11.1 70.7 %copy-start.3 = (s32[17]{0:T(128)S(1)}, s32[17]{0:T(128)}, u32[]{:S(2)}) copy-start(s32[17]{0:T(128)} %param.14) | copy-start | bytes 208
  11.1 92.4 %all-to-all-start = ((f32[128,2,1152]{2,1,0:T(2,128)}), f32[128,2,1152]{2,1,0:T(2,128)S(1)}, u32[]{:S(2)}, u32[]{:S(2)}) async-start(f32[128,2,1152]{2,1,0:T(2,128)} %copy.15), calls=%async_computation | async-start | bytes 2359296 | tf_op jit(solution)/shard_map/all_to_all | solution.py:90
  75.3 27.5 %collective-permute-start.1 = (f32[4,2,1152]{2,0,1:T(4,128)S(1)}, f32[4,2,1152]{2,0,1:T(4,128)S(1)}, u32[]{:S(2)}, u32[]{:S(2)}) collective-permute-start(f32[4,2,1152]{2,0,1:T(4,128)S(1)} %broadcast_multiply_fusion), channel_id=1, source_target_pairs={{1,0},{2,1},{3,2},{4,3},{5,4},{6,5},{7,6},{8,7},{9,8},{10,9},{11,1... | collective-permute-start | bytes 110600 | tf_op jit(solution)/shard_map/ppermute | solution.py:20
  77.6 25.2 %collective-permute-start = (f32[4,2,1152]{2,0,1:T(4,128)S(1)}, f32[4,2,1152]{2,0,1:T(4,128)S(1)}, u32[]{:S(2)}, u32[]{:S(2)}) collective-permute-start(f32[4,2,1152]{2,0,1:T(4,128)S(1)} %broadcast_multiply_fusion), channel_id=1, source_target_pairs={{0,1},{1,2},{2,3},{3,4},{4,5},{5,6},{6,7},{7,8},{8,9},{9,10},{10,1... | collective-permute-start | bytes 110600 | tf_op jit(solution)/shard_map/ppermute | solution.py:18
where the time goes:
time: 106 us
  starting transfers between devices  70 us (66%)
  waiting for transfers between devices  18.4 us (17%)
  local copies, waits for them, and re-layouts  9.98 us (9%)
  between operations  3.41 us (3%)
  other arithmetic  2.21 us (2%)
  matrix products  1.51 us (1%)
    all_to_all x1, starting transfers between devices, body(): lax.all_to_all(filtered, 'lat', split_axis=0, concat_axis=1, tiled=True)  63.6 us
    ppermute x1, waiting for transfers between devices, extended(): lax.ppermute(head, axis, [((i + 1) % count, i) for i in range(ends)])  18.4 us
    ppermute x1, starting transfers between devices, extended(): lax.ppermute(tail, axis, [(i, (i + 1) % count) for i in range(ends)])  4.19 us
    cond x1, local copies, waits for them, and re-layouts, body(): lax.cond(jnp.any(mask_rows == 1), apply_filter, keep_values, stacked)  3.21 us
    reshape x1, local copies, waits for them, and re-layouts, body(): columns = state.reshape(field_count, level_count, row_count * lon_count)  2.28 us
    ppermute x1, starting transfers between devices, extended(): lax.ppermute(head, axis, [((i + 1) % count, i) for i in range(ends)])  2.27 us
  transfers between devices with their start and end apart: 3, of which 1 were waited for; matrix products, arithmetic and copies ran while one was open for 2% of the time, Pallas kernels for 0%

commit v1 on v0

v1 whole, which is shorter than its diff:
```python
import functools

import jax
import jax.numpy as jnp
import numpy as np
from jax import lax
from jax.experimental import pallas as pl
from jax.experimental.pallas import tpu as pltpu
from jax.sharding import PartitionSpec as P

COSCUT = 0.5
LANES = 128
ORDER = (12, 8, 4, 2, 13, 9, 5, 1, 14, 10, 6, 3, 15, 11, 7)
F32 = jnp.float32
BF16 = jnp.bfloat16


def split_product(left, right, dims=(((1,), (0,)), ((), ()))):
    high = left.astype(BF16)
    low = (left - high.astype(F32)).astype(BF16)
    dot = functools.partial(lax.dot_general, dimension_numbers=dims, preferred_element_type=F32)
    return dot(high, right[0]) + (dot(high, right[1]) + dot(low, right[0]))


def halves(values):
    high = values.astype(BF16)
    return high, (values - high.astype(F32)).astype(BF16)


def np_halves(values):
    values = np.asarray(values, np.float32)
    high = values.astype(jnp.bfloat16)
    return np.stack([high, (values - high.astype(np.float32)).astype(jnp.bfloat16)])


def transform_tables(lon_count):
    radix = lon_count // LANES
    b = np.arange(LANES)[:, None]
    k2 = np.arange(LANES)[None, :]
    steps = []
    for k in range(1, radix // 2 + 1):
        angle = 2 * np.pi * ((b * (k + radix * k2)) % lon_count) / lon_count
        c, s = np.cos(angle), np.sin(angle)
        steps.append(np.block([[c, -s], [s, c]]))
    half = LANES // 2
    angle0 = 2 * np.pi * ((b * k2) % LANES) / LANES
    first = np.concatenate(
        [np.cos(angle0[:, : half + 1]), np.sin(angle0[:, 1:half])], axis=1
    )
    wave0 = np.concatenate([np.arange(half + 1), np.arange(1, half)]) * radix
    scale0 = np.where(wave0 * 2 % lon_count == 0, 1.0, 2.0) / lon_count
    waves = [np.concatenate([wave0, np.zeros(LANES)])]
    scales = [np.concatenate([scale0, np.zeros(LANES)])]
    for k in range(1, radix // 2 + 1):
        one = k + radix * np.arange(LANES)
        waves.append(np.concatenate([one, one]))
        scales.append(np.full(2 * LANES, 2.0 / lon_count))
    limit = COSCUT**2 * np.sin(np.pi * np.stack(waves) / lon_count) ** 2
    return (
        np_halves(np.stack(steps)),
        np_halves(first),
        limit.astype(np.float32),
        np.stack(scales).astype(np.float32),
    )


def row_cos_square(lat_count):
    latitude = np.pi * ((np.arange(lat_count) + 0.5) / lat_count - 0.5)
    return (np.cos(latitude) ** 2).astype(np.float32)


def filtered(fields, cos_square, step_table, first_table, limit, scale):
    radix = fields.shape[1] // LANES
    half = radix // 2
    parts = [fields[:, a * LANES : (a + 1) * LANES] for a in range(radix)]
    sums = [parts[a] + parts[radix - a] for a in range(1, half + 1)]
    gaps = [parts[a] - parts[radix - a] for a in range(1, half + 1)]
    back = (((1,), (1,)), ((), ()))

    def gain(k, width):
        return (
            cos_square / jnp.maximum(cos_square, limit[k : k + 1, :width]) * scale[k : k + 1, :width]
        )

    total = parts[0]
    for value in sums:
        total = total + value
    pair = (first_table[0], first_table[1])
    spectrum = split_product(total, pair) * gain(0, LANES)
    base = split_product(spectrum, pair, back)
    cosines, sines = [], []
    for k in range(1, half + 1):
        real, imag = parts[0], None
        for a in range(1, half + 1):
            angle = 2 * np.pi * (a * k % radix) / radix
            real = real + float(np.cos(angle)) * sums[a - 1]
            term = float(-np.sin(angle)) * gaps[a - 1]
            imag = term if imag is None else imag + term
        pair = (step_table[0, k - 1], step_table[1, k - 1])
        spectrum = split_product(jnp.concatenate([real, imag], axis=1), pair) * gain(k, 2 * LANES)
        series = split_product(spectrum, pair, back)
        cosines.append(series[:, :LANES])
        sines.append(series[:, LANES:])
    whole = base
    for value in cosines:
        whole = whole + value
    out = [whole]
    lower, upper = [], []
    for a in range(1, half + 1):
        even, odd = base, None
        for k in range(1, half + 1):
            angle = 2 * np.pi * (a * k % radix) / radix
            even = even + float(np.cos(angle)) * cosines[k - 1]
            term = float(np.sin(angle)) * sines[k - 1]
            odd = term if odd is None else odd + term
        lower.append(even - odd)
        upper.append(even + odd)
    return jnp.concatenate(out + lower + upper[::-1], axis=1)


def mix_kernel(masks, swap, state_ref, mix_ref, mask_ref, cos_ref, steps_ref, first_ref, limit_ref, scale_ref, *refs):
    out_refs, (load_ref, sem) = refs[:-2], refs[-2:]
    levels = mix_ref.shape[1]
    rows, lon = state_ref.shape[1:]
    part = out_refs[0].shape[1]
    split = levels // part
    me = lax.axis_index("lat")
    chip = me // split
    core = lax.rem(me, split)
    fields = [jnp.bitwise_xor(chip, mask) if swap else mask for mask in masks]
    copies = [
        pltpu.make_async_copy(
            state_ref.at[pl.ds(field * levels, levels)], load_ref.at[i], sem.at[i]
        )
        for i, field in enumerate(fields)
    ]
    for copy in copies:
        copy.start()
    for i, field in enumerate(fields):
        weights = jnp.concatenate(
            [
                mix_ref[field, pl.ds(pl.multiple_of((jnp.bitwise_xor(core, c) if swap else c) * part, part), part), :]
                for c in range(split)
            ],
            axis=0,
        )
        copies[i].wait()
        for r in range(rows):
            mixed = split_product(weights, halves(load_ref[i, :, r, :]))
            for c in range(split):
                out_refs[i * split + c][r] = mixed[c * part : (c + 1) * part]
    active = [mask_ref[me * rows + r] == 1 for r in range(rows)]

    @pl.when(functools.reduce(jnp.logical_or, active))
    def _():
        height = len(out_refs) * part
        fields = jnp.concatenate([ref[r] for r in range(rows) for ref in out_refs], axis=0)
        cos_square = jnp.concatenate(
            [jnp.full((height, 1), cos_ref[me * rows + r], F32) for r in range(rows)], axis=0
        )
        smooth = filtered(fields, cos_square, steps_ref, first_ref, limit_ref, scale_ref)
        for r in range(rows):

            @pl.when(active[r])
            def _():
                for i, ref in enumerate(out_refs):
                    start = r * height + i * part
                    ref[r] = smooth[start : start + part]


def mix(state, vertical_mix, polar_mask, tables, masks, part, swap):
    stack_count, rows, lon = state.shape
    levels = vertical_mix.shape[1]
    outs = len(masks) * (levels // part)
    vmem = pl.BlockSpec(memory_space=pltpu.VMEM)
    smem = pl.BlockSpec(memory_space=pltpu.SMEM)
    return pl.pallas_call(
        functools.partial(mix_kernel, masks, swap),
        out_shape=[jax.ShapeDtypeStruct((rows, part, lon), F32)] * outs,
        in_specs=[pl.BlockSpec(memory_space=pl.ANY), vmem, smem, smem, vmem, vmem, vmem, vmem],
        out_specs=[vmem] * outs,
        scratch_shapes=[
            pltpu.VMEM((len(masks), levels, rows, lon), F32),
            pltpu.SemaphoreType.DMA((len(masks),)),
        ],
        compiler_params=pltpu.CompilerParams(vmem_limit_bytes=40 << 20),
        name="mix",
    )(state, vertical_mix, polar_mask, *tables)


def flux_kernel(state_ref, mix_ref, coupling_ref, fractions_ref, index_ref, out_ref):
    fields, levels, _ = mix_ref.shape
    rows = state_ref.shape[1]
    for r in range(rows):
        bottom = jnp.concatenate(
            [
                split_product(
                    mix_ref[f, levels - 8 : levels, :],
                    halves(state_ref[f * levels : (f + 1) * levels, r, :]),
                )[7:8]
                for f in range(fields)
            ],
            axis=0,
        )
        speed = jnp.sqrt(bottom[0:1] * bottom[0:1] + bottom[1:2] * bottom[1:2] + 1.0)
        flux = jnp.dot(
            coupling_ref[...], bottom, precision=lax.Precision.HIGHEST, preferred_element_type=F32
        )
        out_ref[r] = speed * flux * fractions_ref[pl.ds(index_ref[r], 1), :]


def surface_flux(state, vertical_mix, coupling, fractions, weight_index):
    vmem = pl.BlockSpec(memory_space=pltpu.VMEM)
    return pl.pallas_call(
        flux_kernel,
        out_shape=jax.ShapeDtypeStruct((state.shape[1], coupling.shape[0], state.shape[2]), F32),
        in_specs=[vmem] * 4 + [pl.BlockSpec(memory_space=pltpu.SMEM)],
        out_specs=vmem,
        compiler_params=pltpu.CompilerParams(vmem_limit_bytes=40 << 20),
        name="flux",
    )(state, vertical_mix, coupling, fractions, weight_index)


def ocean_kernel(lat_count, bounds_ref, left_ref, own_ref, right_ref, out_ref):
    rows = own_ref.shape[0]
    slots = out_ref.shape[0]
    half = rows // 2
    me = lax.axis_index("lat")
    start = bounds_ref[me] - half
    length = bounds_ref[me + 1] - bounds_ref[me] + 2 * half + 1
    shift = start - (me - 1) * rows
    near = [ref[r] for ref in (left_ref, own_ref, right_ref) for r in range(rows)]
    for s in range(slots):
        row = start + s
        valid = (s < length) & (row >= 0) & (row < lat_count)
        picked = jnp.zeros_like(near[0])
        for p, value in enumerate(near):
            picked = jnp.where(valid & (shift + s == p), value, picked)
        out_ref[s] = picked


def ocean_slots(weighted, band_bounds, lat_count, device_count):
    rows, flux_count, lon = weighted.shape
    ends = device_count - 1
    left = lax.ppermute(weighted, "lat", [(i, i + 1) for i in range(ends)])
    right = lax.ppermute(weighted, "lat", [(i + 1, i) for i in range(ends)])
    vmem = pl.BlockSpec(memory_space=pltpu.VMEM)
    slots = pl.pallas_call(
        functools.partial(ocean_kernel, lat_count),
        out_shape=jax.ShapeDtypeStruct((3 * rows, flux_count, lon), F32),
        in_specs=[pl.BlockSpec(memory_space=pltpu.SMEM)] + [vmem] * 3,
        out_specs=vmem,
        name="ocean",
    )(band_bounds, left, weighted, right)
    return jnp.transpose(slots, (1, 0, 2))


def place_kernel(*refs):
    in_refs, out_ref = refs[:-1], refs[-1]
    rows = in_refs[0].shape[0]
    me = lax.axis_index("lat")
    for m, ref in enumerate(in_refs):
        start = jnp.bitwise_xor(me, m) * rows
        for r in range(rows):
            out_ref[:, pl.ds(start + r, 1), :] = ref[r][:, None, :]


def place(blocks, lat_count):
    rows, part, lon = blocks[0].shape
    vmem = pl.BlockSpec(memory_space=pltpu.VMEM)
    return pl.pallas_call(
        place_kernel,
        out_shape=jax.ShapeDtypeStruct((part, lat_count, lon), F32),
        in_specs=[vmem] * len(blocks),
        out_specs=vmem,
        compiler_params=pltpu.CompilerParams(vmem_limit_bytes=40 << 20),
        name="place",
    )(*blocks)


def body(device_count, state, vertical_mix, coupling, fractions, weight_index, band_bounds, polar_mask):
    field_count, level_count = vertical_mix.shape[:2]
    stack_count, row_count, lon_count = state.shape
    lat_count = polar_mask.shape[0]
    part = stack_count // device_count
    steps, first, limit, scale = transform_tables(lon_count)
    tables = (row_cos_square(lat_count), steps, first, limit, scale)
    weighted = surface_flux(state, vertical_mix, coupling, fractions, weight_index)
    if part % 8 == 0 and device_count == len(ORDER) + 1:
        split = level_count // part
        blocks = mix(state, vertical_mix, polar_mask, tables, tuple(range(field_count)), part, True)
        received = {0: blocks[0]}
        for m in reversed(ORDER):
            received[m] = lax.ppermute(
                blocks[m], "lat", [(i, i ^ m) for i in range(device_count)]
            )
        state_out = place([received[m] for m in range(device_count)], lat_count)
    else:
        mixed = mix(
            state, vertical_mix, polar_mask, tables, tuple(range(field_count)), level_count, False
        )
        stacked = jnp.concatenate(mixed, axis=1)
        moved = lax.all_to_all(stacked, "lat", split_axis=1, concat_axis=0, tiled=True)
        state_out = jnp.transpose(moved, (1, 0, 2))
    ocean = ocean_slots(weighted, band_bounds, lat_count, device_count)
    return (state_out, ocean)


def solution(mesh):
    return jax.shard_map(
        functools.partial(body, mesh.shape["lat"]),
        mesh=mesh,
        in_specs=(P("member", "lat", None), P(), P(), P(), P(("member", "lat")), P(), P()),
        out_specs=(P(("member", "lat"), None, None), P(None, ("member", "lat"), None)),
        check_vma=False,
    )
```

time: 106 us -> 63.4 us (0.60)
  the two profiles are of different devices: /device:TPU:15 before, /device:TPU:0 now
where the time goes in v1:
time: 63.4 us; the launch traced here: 63.2 us
  starting transfers between devices  33.5 us (53%)
  Pallas kernels  16.2 us (26%)
  waiting for transfers between devices  8.26 us (13%)
  local copies, waits for them, and re-layouts  4.36 us (7%)
  between operations  0.77 us (1%)
    ppermute x15, starting transfers between devices, body(): lax.ppermute(blocks[m], 'lat', [(i, i ^ m) for i in range(device_count)])  29.9 us
    pallas_call x1, Pallas kernels, mix(): pl.pallas_call(functools.partial(mix_kernel, masks, swap), out_shape=[jax...  8.61 us
    ppermute x15, waiting for transfers between devices, body(): lax.ppermute(blocks[m], 'lat', [(i, i ^ m) for i in range(device_count)])  8.25 us
    pallas_call x1, Pallas kernels, surface_flux(): pl.pallas_call(flux_kernel, out_shape=jax.ShapeDtypeStruct((state.shape[1...  4.67 us
    unnamed x28, local copies, waits for them, and re-layouts  4.36 us
    ppermute x1, starting transfers between devices, ocean_slots(): left = lax.ppermute(weighted, 'lat', [(i, i + 1) for i in range(ends)])  2.36 us
    pallas_call x1, Pallas kernels, ocean_slots(): pl.pallas_call(functools.partial(ocean_kernel, lat_count), out_shape=jax....  1.53 us
    pallas_call x1, Pallas kernels, place(): pl.pallas_call(place_kernel, out_shape=jax.ShapeDtypeStruct((part, lat_co...  1.42 us
  transfers between devices with their start and end apart: 17, of which 3 were waited for; matrix products, arithmetic and copies ran while one was open for 0% of the time, Pallas kernels for 16%

profile of v1, /device:TPU:0, one launch (start us, length us, event | category | flops | bytes accessed | tf_op | source)
XLA Modules:
  0.0 63.2 jit_solution(12176794690165008077)
XLA Ops:
  0.7 1.3 %copy-done = f32[128,2,1152]{2,1,0:T(2,128)S(1)} copy-done((f32[128,2,1152]{2,1,0:T(2,128)S(1)}, f32[128,2,1152]{2,1,0:T(2,128)}, u32[]{:S(2)}) %copy-start) | copy-done | bytes 1179672
  2.8 0.9 %copy-done.4 = f32[16,1152]{1,0:T(8,128)S(1)} copy-done((f32[16,1152]{1,0:T(8,128)S(1)}, f32[16,1152]{1,0:T(8,128)}, u32[]{:S(2)}) %copy-start.4) | copy-done | bytes 73752
  5.0 4.7 %flux.1.own_ref = f32[2,4,1152]{2,1,0:T(4,128)S(1)} custom-call(f32[128,2,1152]{2,1,0:T(2,128)S(1)} %copy-done, f32[8,16,16]{2,1,0:T(8,128)S(1)} %copy-done.2, f32[4,8]{1,0:T(4,128)S(1)} %copy-done.8, f32[16,1152]{1,0:T(8,128)S(1)} %copy-done.4, s32[2]{0:T(128)S(1)} %copy-done.9), custom_call_target="tpu_custom_call" | custom-call | tf_op jit(solution)/shard_map/flux/pallas_call | solution.py:214
  9.7 2.4 %collective-permute-start.15 = (f32[2,4,1152]{2,1,0:T(4,128)S(1)}, f32[2,4,1152]{2,1,0:T(4,128)S(1)}, u32[]{:S(2)}, u32[]{:S(2)}) collective-permute-start(f32[2,4,1152]{2,1,0:T(4,128)S(1)} %flux.1.own_ref), channel_id=1, source_target_pairs={{0,1},{1,2},{2,3},{3,4},{4,5},{5,6},{6,7},{7,8},{8,9},{9,10},{10,1... | collective-permute-start | bytes 110600 | tf_op jit(solution)/shard_map/ppermute | solution.py:245
  12.0 1.3 %collective-permute-start.16 = (f32[2,4,1152]{2,1,0:T(4,128)S(1)}, f32[2,4,1152]{2,1,0:T(4,128)S(1)}, u32[]{:S(2)}, u32[]{:S(2)}) collective-permute-start(f32[2,4,1152]{2,1,0:T(4,128)S(1)} %flux.1.own_ref), channel_id=1, source_target_pairs={{1,0},{2,1},{3,2},{4,3},{5,4},{6,5},{7,6},{8,7},{9,8},{10,9},{11,1... | collective-permute-start | bytes 110600 | tf_op jit(solution)/shard_map/ppermute | solution.py:246
  13.4 8.6 %mix.1 = (f32[2,8,1152]{2,1,0:T(8,128)S(1)}, f32[2,8,1152]{2,1,0:T(8,128)S(1)}, f32[2,8,1152]{2,1,0:T(8,128)S(1)}, f32[2,8,1152]{2,1,0:T(8,128)S(1)}, f32[2,8,11...) custom-call(f32[128,2,1152]{2,1,0:T(2,128)S(1)} %copy-done, ...), custom_call_target="tpu_custom_call" | custom-call | tf_op jit(solution)/shard_map/mix/pallas_call | solution.py:177
  22.0 3.3 %collective-permute-start = (f32[2,8,1152]{2,1,0:T(8,128)S(1)}, f32[2,8,1152]{2,1,0:T(8,128)S(1)}, u32[]{:S(2)}, u32[]{:S(2)}) collective-permute-start(f32[2,8,1152]{2,1,0:T(8,128)S(1)} %get-tuple-element.19), channel_id=1, source_target_pairs={{0,1},{1,0},{2,3},{3,2},{4,5},{5,4},{6,7},{7,6},{8,9},{9,8},{10,11... | collective-permute-start | bytes 221192 | tf_op jit(solution)/shard_map/ppermute | solution.py:294
  25.4 1.6 %collective-permute-start.1 = (f32[2,8,1152]{2,1,0:T(8,128)S(1)}, f32[2,8,1152]{2,1,0:T(8,128)S(1)}, u32[]{:S(2)}, u32[]{:S(2)}) collective-permute-start(f32[2,8,1152]{2,1,0:T(8,128)S(1)} %get-tuple-element.20), channel_id=1, source_target_pairs={{0,2},{1,3},{2,0},{3,1},{4,6},{5,7},{6,4},{7,5},{8,10},{9,11},{10,... | collective-permute-start | bytes 221192 | tf_op jit(solution)/shard_map/ppermute | solution.py:294
  27.0 1.5 %collective-permute-start.10 = (f32[2,8,1152]{2,1,0:T(8,128)S(1)}, f32[2,8,1152]{2,1,0:T(8,128)S(1)}, u32[]{:S(2)}, u32[]{:S(2)}) collective-permute-start(f32[2,8,1152]{2,1,0:T(8,128)S(1)} %get-tuple-element.29), channel_id=1, source_target_pairs={{0,11},{1,10},{2,9},{3,8},{4,15},{5,14},{6,13},{7,12},{8,3},{9,2},... | collective-permute-start | bytes 221192 | tf_op jit(solution)/shard_map/ppermute | solution.py:294
  28.5 2.2 %collective-permute-start.11 = (f32[2,8,1152]{2,1,0:T(8,128)S(1)}, f32[2,8,1152]{2,1,0:T(8,128)S(1)}, u32[]{:S(2)}, u32[]{:S(2)}) collective-permute-start(f32[2,8,1152]{2,1,0:T(8,128)S(1)} %get-tuple-element.30), channel_id=1, source_target_pairs={{0,12},{1,13},{2,14},{3,15},{4,8},{5,9},{6,10},{7,11},{8,4},{9,5},... | collective-permute-start | bytes 221192 | tf_op jit(solution)/shard_map/ppermute | solution.py:294
  30.7 1.3 %collective-permute-start.12 = (f32[2,8,1152]{2,1,0:T(8,128)S(1)}, f32[2,8,1152]{2,1,0:T(8,128)S(1)}, u32[]{:S(2)}, u32[]{:S(2)}) collective-permute-start(f32[2,8,1152]{2,1,0:T(8,128)S(1)} %get-tuple-element.31), channel_id=1, source_target_pairs={{0,13},{1,12},{2,15},{3,14},{4,9},{5,8},{6,11},{7,10},{8,5},{9,4},... | collective-permute-start | bytes 221192 | tf_op jit(solution)/shard_map/ppermute | solution.py:294
  32.0 1.7 %collective-permute-start.13 = (f32[2,8,1152]{2,1,0:T(8,128)S(1)}, f32[2,8,1152]{2,1,0:T(8,128)S(1)}, u32[]{:S(2)}, u32[]{:S(2)}) collective-permute-start(f32[2,8,1152]{2,1,0:T(8,128)S(1)} %get-tuple-element.32), channel_id=1, source_target_pairs={{0,14},{1,15},{2,12},{3,13},{4,10},{5,11},{6,8},{7,9},{8,6},{9,7},... | collective-permute-start | bytes 221192 | tf_op jit(solution)/shard_map/ppermute | solution.py:294
  33.8 2.8 %collective-permute-start.14 = (f32[2,8,1152]{2,1,0:T(8,128)S(1)}, f32[2,8,1152]{2,1,0:T(8,128)S(1)}, u32[]{:S(2)}, u32[]{:S(2)}) collective-permute-start(f32[2,8,1152]{2,1,0:T(8,128)S(1)} %get-tuple-element.33), channel_id=1, source_target_pairs={{0,15},{1,14},{2,13},{3,12},{4,11},{5,10},{6,9},{7,8},{8,7},{9,6},... | collective-permute-start | bytes 221192 | tf_op jit(solution)/shard_map/ppermute | solution.py:294
  36.5 1.1 %collective-permute-done.10.refs_11_ = f32[2,8,1152]{2,1,0:T(8,128)S(1)} collective-permute-done((f32[2,8,1152]{2,1,0:T(8,128)S(1)}, f32[2,8,1152]{2,1,0:T(8,128)S(1)}, u32[]{:S(2)}, u32[]{:S(2)}) %collective-permute-start.10) | collective-permute-done | bytes 73760 | tf_op jit(solution)/shard_map/ppermute | solution.py:294
  37.7 2.3 %collective-permute-start.2 = (f32[2,8,1152]{2,1,0:T(8,128)S(1)}, f32[2,8,1152]{2,1,0:T(8,128)S(1)}, u32[]{:S(2)}, u32[]{:S(2)}) collective-permute-start(f32[2,8,1152]{2,1,0:T(8,128)S(1)} %get-tuple-element.21), channel_id=1, source_target_pairs={{0,3},{1,2},{2,1},{3,0},{4,7},{5,6},{6,5},{7,4},{8,11},{9,10},{10,... | collective-permute-start | bytes 221192 | tf_op jit(solution)/shard_map/ppermute | solution.py:294
  39.9 2.6 %collective-permute-start.3 = (f32[2,8,1152]{2,1,0:T(8,128)S(1)}, f32[2,8,1152]{2,1,0:T(8,128)S(1)}, u32[]{:S(2)}, u32[]{:S(2)}) collective-permute-start(f32[2,8,1152]{2,1,0:T(8,128)S(1)} %get-tuple-element.22), channel_id=1, source_target_pairs={{0,4},{1,5},{2,6},{3,7},{4,0},{5,1},{6,2},{7,3},{8,12},{9,13},{10,... | collective-permute-start | bytes 221192 | tf_op jit(solution)/shard_map/ppermute | solution.py:294
  42.6 1.0 %collective-permute-start.4 = (f32[2,8,1152]{2,1,0:T(8,128)S(1)}, f32[2,8,1152]{2,1,0:T(8,128)S(1)}, u32[]{:S(2)}, u32[]{:S(2)}) collective-permute-start(f32[2,8,1152]{2,1,0:T(8,128)S(1)} %get-tuple-element.23), channel_id=1, source_target_pairs={{0,5},{1,4},{2,7},{3,6},{4,1},{5,0},{6,3},{7,2},{8,13},{9,12},{10,... | collective-permute-start | bytes 221192 | tf_op jit(solution)/shard_map/ppermute | solution.py:294
  43.6 3.0 %collective-permute-start.5 = (f32[2,8,1152]{2,1,0:T(8,128)S(1)}, f32[2,8,1152]{2,1,0:T(8,128)S(1)}, u32[]{:S(2)}, u32[]{:S(2)}) collective-permute-start(f32[2,8,1152]{2,1,0:T(8,128)S(1)} %get-tuple-element.24), channel_id=1, source_target_pairs={{0,6},{1,7},{2,4},{3,5},{4,2},{5,3},{6,0},{7,1},{8,14},{9,15},{10,... | collective-permute-start | bytes 221192 | tf_op jit(solution)/shard_map/ppermute | solution.py:294
  47.5 1.8 %collective-permute-start.7 = (f32[2,8,1152]{2,1,0:T(8,128)S(1)}, f32[2,8,1152]{2,1,0:T(8,128)S(1)}, u32[]{:S(2)}, u32[]{:S(2)}) collective-permute-start(f32[2,8,1152]{2,1,0:T(8,128)S(1)} %get-tuple-element.26), channel_id=1, source_target_pairs={{0,8},{1,9},{2,10},{3,11},{4,12},{5,13},{6,14},{7,15},{8,0},{9,1},... | collective-permute-start | bytes 221192 | tf_op jit(solution)/shard_map/ppermute | solution.py:294
  50.1 3.0 %collective-permute-start.9 = (f32[2,8,1152]{2,1,0:T(8,128)S(1)}, f32[2,8,1152]{2,1,0:T(8,128)S(1)}, u32[]{:S(2)}, u32[]{:S(2)}) collective-permute-start(f32[2,8,1152]{2,1,0:T(8,128)S(1)} %get-tuple-element.28), channel_id=1, source_target_pairs={{0,10},{1,11},{2,8},{3,9},{4,14},{5,15},{6,12},{7,13},{8,2},{9,3},... | collective-permute-start | bytes 221192 | tf_op jit(solution)/shard_map/ppermute | solution.py:294
  53.1 1.5 %ocean.1 = f32[6,4,1152]{2,1,0:T(4,128)} custom-call(s32[17]{0:T(128)} %bounds_ref.1, f32[2,4,1152]{2,1,0:T(4,128)} %copy-done.12, f32[2,4,1152]{2,1,0:T(4,128)} %copy-done.3, f32[2,4,1152]{2,1,0:T(4,128)} %copy-done.13), custom_call_target="tpu_custom_call" | custom-call | tf_op jit(solution)/shard_map/ocean/pallas_call | solution.py:248
  54.6 4.4 %collective-permute-done.8.refs_9_ = f32[2,8,1152]{2,1,0:T(8,128)S(1)} collective-permute-done((f32[2,8,1152]{2,1,0:T(8,128)S(1)}, f32[2,8,1152]{2,1,0:T(8,128)S(1)}, u32[]{:S(2)}, u32[]{:S(2)}) %collective-permute-start.8) | collective-permute-done | bytes 73760 | tf_op jit(solution)/shard_map/ppermute | solution.py:294
  59.1 2.6 %collective-permute-done.9.refs_10_ = f32[2,8,1152]{2,1,0:T(8,128)S(1)} collective-permute-done((f32[2,8,1152]{2,1,0:T(8,128)S(1)}, f32[2,8,1152]{2,1,0:T(8,128)S(1)}, u32[]{:S(2)}, u32[]{:S(2)}) %collective-permute-start.9) | collective-permute-done | bytes 73760 | tf_op jit(solution)/shard_map/ppermute | solution.py:294
  61.7 1.4 %place.1 = f32[8,32,1152]{2,1,0:T(8,128)} custom-call(f32[2,8,1152]{2,1,0:T(8,128)S(1)} %get-tuple-element.18.refs_0_, f32[2,8,1152]{2,1,0:T(8,128)S(1)} %collective-permute-done.refs_1_, f32[2,8,1152]{2,1,0:T(8,128)S(1)} %collective-permute-done.1.refs_2_, f32[2,8,1152]{2,1,0:T(8,128)S(1)} %collective-permute-done.2.refs_3_, ...), custom_call_target="tpu_custom_call" | custom-call | tf_op jit(solution)/shard_map/place/pallas_call | solution.py:271
  (42 shorter events, 3.9 us)
Async XLA Ops:
  0.6 12.7 %copy-start.11 = (f32[32]{0:T(128)S(1)}, f32[32]{0:T(128)}, u32[]{:S(2)}) copy-start(f32[32]{0:T(128)} %constant.10.clone.cos_ref) | copy-start | bytes 388
  5.0 8.4 %copy-start.6 = (f32[5,256]{1,0:T(8,128)S(1)}, f32[5,256]{1,0:T(8,128)}, u32[]{:S(2)}) copy-start(f32[5,256]{1,0:T(8,128)} %constant.13.clone.limit_ref) | copy-start | bytes 15364
  5.0 8.4 %copy-start.7 = (f32[5,256]{1,0:T(8,128)S(1)}, f32[5,256]{1,0:T(8,128)}, u32[]{:S(2)}) copy-start(f32[5,256]{1,0:T(8,128)} %constant.14.clone.scale_ref) | copy-start | bytes 15364
  5.0 8.4 %copy-start.10 = (s32[32]{0:T(128)S(1)}, s32[32]{0:T(128)}, u32[]{:S(2)}) copy-start(s32[32]{0:T(128)} %mask_ref.1) | copy-start | bytes 388
  9.7 12.4 %copy-start.3 = (f32[2,4,1152]{2,1,0:T(4,128)}, f32[2,4,1152]{2,1,0:T(4,128)S(1)}, u32[]{:S(2)}) copy-start(f32[2,4,1152]{2,1,0:T(4,128)S(1)} %flux.1.own_ref) | copy-start | bytes 110596
  9.7 18.9 %collective-permute-start.15 = (f32[2,4,1152]{2,1,0:T(4,128)S(1)}, f32[2,4,1152]{2,1,0:T(4,128)S(1)}, u32[]{:S(2)}, u32[]{:S(2)}) collective-permute-start(f32[2,4,1152]{2,1,0:T(4,128)S(1)} %flux.1.own_ref), channel_id=1, source_target_pairs={{0,1},{1,2},{2,3},{3,4},{4,5},{5,6},{6,7},{7,8},{8,9},{9,10},{10,1... | collective-permute-start | bytes 110600 | tf_op jit(solution)/shard_map/ppermute | solution.py:245
  12.0 18.7 %collective-permute-start.16 = (f32[2,4,1152]{2,1,0:T(4,128)S(1)}, f32[2,4,1152]{2,1,0:T(4,128)S(1)}, u32[]{:S(2)}, u32[]{:S(2)}) collective-permute-start(f32[2,4,1152]{2,1,0:T(4,128)S(1)} %flux.1.own_ref), channel_id=1, source_target_pairs={{1,0},{2,1},{3,2},{4,3},{5,4},{6,5},{7,6},{8,7},{9,8},{10,9},{11,1... | collective-permute-start | bytes 110600 | tf_op jit(solution)/shard_map/ppermute | solution.py:246
  22.0 10.0 %collective-permute-start = (f32[2,8,1152]{2,1,0:T(8,128)S(1)}, f32[2,8,1152]{2,1,0:T(8,128)S(1)}, u32[]{:S(2)}, u32[]{:S(2)}) collective-permute-start(f32[2,8,1152]{2,1,0:T(8,128)S(1)} %get-tuple-element.19), channel_id=1, source_target_pairs={{0,1},{1,0},{2,3},{3,2},{4,5},{5,4},{6,7},{7,6},{8,9},{9,8},{10,11... | collective-permute-start | bytes 221192 | tf_op jit(solution)/shard_map/ppermute | solution.py:294
  25.4 8.4 %collective-permute-start.1 = (f32[2,8,1152]{2,1,0:T(8,128)S(1)}, f32[2,8,1152]{2,1,0:T(8,128)S(1)}, u32[]{:S(2)}, u32[]{:S(2)}) collective-permute-start(f32[2,8,1152]{2,1,0:T(8,128)S(1)} %get-tuple-element.20), channel_id=1, source_target_pairs={{0,2},{1,3},{2,0},{3,1},{4,6},{5,7},{6,4},{7,5},{8,10},{9,11},{10,... | collective-permute-start | bytes 221192 | tf_op jit(solution)/shard_map/ppermute | solution.py:294
  27.0 10.7 %collective-permute-start.10 = (f32[2,8,1152]{2,1,0:T(8,128)S(1)}, f32[2,8,1152]{2,1,0:T(8,128)S(1)}, u32[]{:S(2)}, u32[]{:S(2)}) collective-permute-start(f32[2,8,1152]{2,1,0:T(8,128)S(1)} %get-tuple-element.29), channel_id=1, source_target_pairs={{0,11},{1,10},{2,9},{3,8},{4,15},{5,14},{6,13},{7,12},{8,3},{9,2},... | collective-permute-start | bytes 221192 | tf_op jit(solution)/shard_map/ppermute | solution.py:294
  28.5 24.6 %copy-start.12 = (f32[2,4,1152]{2,1,0:T(4,128)}, f32[2,4,1152]{2,1,0:T(4,128)S(1)}, u32[]{:S(2)}) copy-start(f32[2,4,1152]{2,1,0:T(4,128)S(1)} %collective-permute-done.15.left_ref) | copy-start | bytes 110596
  28.5 11.4 %collective-permute-start.11 = (f32[2,8,1152]{2,1,0:T(8,128)S(1)}, f32[2,8,1152]{2,1,0:T(8,128)S(1)}, u32[]{:S(2)}, u32[]{:S(2)}) collective-permute-start(f32[2,8,1152]{2,1,0:T(8,128)S(1)} %get-tuple-element.30), channel_id=1, source_target_pairs={{0,12},{1,13},{2,14},{3,15},{4,8},{5,9},{6,10},{7,11},{8,4},{9,5},... | collective-permute-start | bytes 221192 | tf_op jit(solution)/shard_map/ppermute | solution.py:294
  30.7 22.4 %copy-start.13 = (f32[2,4,1152]{2,1,0:T(4,128)}, f32[2,4,1152]{2,1,0:T(4,128)S(1)}, u32[]{:S(2)}) copy-start(f32[2,4,1152]{2,1,0:T(4,128)S(1)} %collective-permute-done.16.right_ref) | copy-start | bytes 110596
  30.7 11.8 %collective-permute-start.12 = (f32[2,8,1152]{2,1,0:T(8,128)S(1)}, f32[2,8,1152]{2,1,0:T(8,128)S(1)}, u32[]{:S(2)}, u32[]{:S(2)}) collective-permute-start(f32[2,8,1152]{2,1,0:T(8,128)S(1)} %get-tuple-element.31), channel_id=1, source_target_pairs={{0,13},{1,12},{2,15},{3,14},{4,9},{5,8},{6,11},{7,10},{8,5},{9,4},... | collective-permute-start | bytes 221192 | tf_op jit(solution)/shard_map/ppermute | solution.py:294
  32.0 11.5 %collective-permute-start.13 = (f32[2,8,1152]{2,1,0:T(8,128)S(1)}, f32[2,8,1152]{2,1,0:T(8,128)S(1)}, u32[]{:S(2)}, u32[]{:S(2)}) collective-permute-start(f32[2,8,1152]{2,1,0:T(8,128)S(1)} %get-tuple-element.32), channel_id=1, source_target_pairs={{0,14},{1,15},{2,12},{3,13},{4,10},{5,11},{6,8},{7,9},{8,6},{9,7},... | collective-permute-start | bytes 221192 | tf_op jit(solution)/shard_map/ppermute | solution.py:294
  33.8 12.9 %collective-permute-start.14 = (f32[2,8,1152]{2,1,0:T(8,128)S(1)}, f32[2,8,1152]{2,1,0:T(8,128)S(1)}, u32[]{:S(2)}, u32[]{:S(2)}) collective-permute-start(f32[2,8,1152]{2,1,0:T(8,128)S(1)} %get-tuple-element.33), channel_id=1, source_target_pairs={{0,15},{1,14},{2,13},{3,12},{4,11},{5,10},{6,9},{7,8},{8,7},{9,6},... | collective-permute-start | bytes 221192 | tf_op jit(solution)/shard_map/ppermute | solution.py:294
  37.7 9.8 %collective-permute-start.2 = (f32[2,8,1152]{2,1,0:T(8,128)S(1)}, f32[2,8,1152]{2,1,0:T(8,128)S(1)}, u32[]{:S(2)}, u32[]{:S(2)}) collective-permute-start(f32[2,8,1152]{2,1,0:T(8,128)S(1)} %get-tuple-element.21), channel_id=1, source_target_pairs={{0,3},{1,2},{2,1},{3,0},{4,7},{5,6},{6,5},{7,4},{8,11},{9,10},{10,... | collective-permute-start | bytes 221192 | tf_op jit(solution)/shard_map/ppermute | solution.py:294
  39.9 9.3 %collective-permute-start.3 = (f32[2,8,1152]{2,1,0:T(8,128)S(1)}, f32[2,8,1152]{2,1,0:T(8,128)S(1)}, u32[]{:S(2)}, u32[]{:S(2)}) collective-permute-start(f32[2,8,1152]{2,1,0:T(8,128)S(1)} %get-tuple-element.22), channel_id=1, source_target_pairs={{0,4},{1,5},{2,6},{3,7},{4,0},{5,1},{6,2},{7,3},{8,12},{9,13},{10,... | collective-permute-start | bytes 221192 | tf_op jit(solution)/shard_map/ppermute | solution.py:294
  42.6 7.6 %collective-permute-start.4 = (f32[2,8,1152]{2,1,0:T(8,128)S(1)}, f32[2,8,1152]{2,1,0:T(8,128)S(1)}, u32[]{:S(2)}, u32[]{:S(2)}) collective-permute-start(f32[2,8,1152]{2,1,0:T(8,128)S(1)} %get-tuple-element.23), channel_id=1, source_target_pairs={{0,5},{1,4},{2,7},{3,6},{4,1},{5,0},{6,3},{7,2},{8,13},{9,12},{10,... | collective-permute-start | bytes 221192 | tf_op jit(solution)/shard_map/ppermute | solution.py:294
  43.6 11.1 %collective-permute-start.5 = (f32[2,8,1152]{2,1,0:T(8,128)S(1)}, f32[2,8,1152]{2,1,0:T(8,128)S(1)}, u32[]{:S(2)}, u32[]{:S(2)}) collective-permute-start(f32[2,8,1152]{2,1,0:T(8,128)S(1)} %get-tuple-element.24), channel_id=1, source_target_pairs={{0,6},{1,7},{2,4},{3,5},{4,2},{5,3},{6,0},{7,1},{8,14},{9,15},{10,... | collective-permute-start | bytes 221192 | tf_op jit(solution)/shard_map/ppermute | solution.py:294
  46.6 8.0 %collective-permute-start.6 = (f32[2,8,1152]{2,1,0:T(8,128)S(1)}, f32[2,8,1152]{2,1,0:T(8,128)S(1)}, u32[]{:S(2)}, u32[]{:S(2)}) collective-permute-start(f32[2,8,1152]{2,1,0:T(8,128)S(1)} %get-tuple-element.25), channel_id=1, source_target_pairs={{0,7},{1,6},{2,5},{3,4},{4,3},{5,2},{6,1},{7,0},{8,15},{9,14},{10,... | collective-permute-start | bytes 221192 | tf_op jit(solution)/shard_map/ppermute | solution.py:294
  47.5 7.2 %collective-permute-start.7 = (f32[2,8,1152]{2,1,0:T(8,128)S(1)}, f32[2,8,1152]{2,1,0:T(8,128)S(1)}, u32[]{:S(2)}, u32[]{:S(2)}) collective-permute-start(f32[2,8,1152]{2,1,0:T(8,128)S(1)} %get-tuple-element.26), channel_id=1, source_target_pairs={{0,8},{1,9},{2,10},{3,11},{4,12},{5,13},{6,14},{7,15},{8,0},{9,1},... | collective-permute-start | bytes 221192 | tf_op jit(solution)/shard_map/ppermute | solution.py:294
  49.3 9.8 %collective-permute-start.8 = (f32[2,8,1152]{2,1,0:T(8,128)S(1)}, f32[2,8,1152]{2,1,0:T(8,128)S(1)}, u32[]{:S(2)}, u32[]{:S(2)}) collective-permute-start(f32[2,8,1152]{2,1,0:T(8,128)S(1)} %get-tuple-element.27), channel_id=1, source_target_pairs={{0,9},{1,8},{2,11},{3,10},{4,13},{5,12},{6,15},{7,14},{8,1},{9,0},... | collective-permute-start | bytes 221192 | tf_op jit(solution)/shard_map/ppermute | solution.py:294
  50.1 11.6 %collective-permute-start.9 = (f32[2,8,1152]{2,1,0:T(8,128)S(1)}, f32[2,8,1152]{2,1,0:T(8,128)S(1)}, u32[]{:S(2)}, u32[]{:S(2)}) collective-permute-start(f32[2,8,1152]{2,1,0:T(8,128)S(1)} %get-tuple-element.28), channel_id=1, source_target_pairs={{0,10},{1,11},{2,8},{3,9},{4,14},{5,15},{6,12},{7,13},{8,2},{9,3},... | collective-permute-start | bytes 221192 | tf_op jit(solution)/shard_map/ppermute | solution.py:294
  (7 other events, 21.1 us)

commit v2 on v1

v2 whole, which is shorter than its diff:
```python
import functools

import jax
import jax.numpy as jnp
import numpy as np
from jax import lax
from jax.experimental import pallas as pl
from jax.experimental.pallas import tpu as pltpu
from jax.sharding import PartitionSpec as P

COSCUT = 0.5
LANES = 128
SUBLANES = 8
DIRECT = 6
BUNDLES = (5, 7, 3, 4, 1, 2)
F32 = jnp.float32
BF16 = jnp.bfloat16
NORMAL = (((1,), (0,)), ((), ()))
TRANSPOSED = (((1,), (1,)), ((), ()))
VMEM_LIMIT = 48 << 20


def halves(values):
    high = values.astype(BF16)
    return high, (values - high.astype(F32)).astype(BF16)


def split_product(left, right, dims=NORMAL):
    dot = functools.partial(lax.dot_general, dimension_numbers=dims, preferred_element_type=F32)
    return dot(left[0], right[0]) + (dot(left[0], right[1]) + dot(left[1], right[0]))


def np_halves(values):
    values = np.asarray(values, np.float32)
    high = values.astype(jnp.bfloat16)
    return np.stack([high, (values - high.astype(np.float32)).astype(jnp.bfloat16)])


def transform_tables(lon_count, lat_count):
    radix = lon_count // LANES
    steps = radix // 2
    b = np.arange(LANES)[:, None]
    k2 = np.arange(LANES)[None, :]
    table = np.zeros((steps * 2 * LANES + LANES, 2 * LANES))
    for k in range(1, steps + 1):
        angle = 2 * np.pi * ((b * (k + radix * k2)) % lon_count) / lon_count
        c, s = np.cos(angle), np.sin(angle)
        table[(k - 1) * 2 * LANES : k * 2 * LANES] = np.block([[c, -s], [s, c]])
    half = LANES // 2
    angle = 2 * np.pi * ((b * k2) % LANES) / LANES
    table[steps * 2 * LANES :, :LANES] = np.concatenate(
        [np.cos(angle[:, : half + 1]), np.sin(angle[:, 1:half])], axis=1
    )
    wave = np.zeros((steps + 1, 2 * LANES))
    scale = np.full((steps + 1, 2 * LANES), 2.0 / lon_count)
    wave[0, :LANES] = np.concatenate([np.arange(half + 1), np.arange(1, half)]) * radix
    scale[0, [0, half]] = 1.0 / lon_count
    for k in range(1, steps + 1):
        wave[k] = np.tile(k + radix * np.arange(LANES), 2)
    limit = COSCUT**2 * np.sin(np.pi * wave / lon_count) ** 2
    latitude = np.pi * ((np.arange(lat_count) + 0.5) / lat_count - 0.5)
    square = np.repeat(np.cos(latitude)[:, None] ** 2, 2 * LANES, axis=1)
    rows = np.concatenate([limit, scale, square])
    rows = np.pad(rows, ((0, -len(rows) % SUBLANES), (0, 0)))
    return np_halves(table), rows.astype(np.float32)


def filtered(fields, squares, table_ref, row_ref):
    radix = fields.shape[1] // LANES
    half = radix // 2
    height = fields.shape[0] // len(squares)
    parts = [fields[:, a * LANES : (a + 1) * LANES] for a in range(radix)]
    sums = [parts[a] + parts[radix - a] for a in range(1, half + 1)]
    gaps = [parts[a] - parts[radix - a] for a in range(1, half + 1)]

    def pair(k):
        if k == 0:
            rows, width = slice(half * 2 * LANES, half * 2 * LANES + LANES), LANES
        else:
            rows, width = slice((k - 1) * 2 * LANES, k * 2 * LANES), 2 * LANES
        return table_ref[0, rows, :width], table_ref[1, rows, :width]

    def gain(k, width):
        limit = row_ref[k : k + 1, :LANES]
        scale = row_ref[half + 1 + k : half + 2 + k, :LANES]
        groups = [
            jnp.broadcast_to(square / jnp.maximum(square, limit) * scale, (height, LANES))
            for square in squares
        ]
        groups = jnp.concatenate(groups, axis=0)
        return groups if width == LANES else jnp.concatenate([groups, groups], axis=1)

    total = parts[0]
    for value in sums:
        total = total + value
    spectrum = split_product(halves(total), pair(0)) * gain(0, LANES)
    base = split_product(halves(spectrum), pair(0), TRANSPOSED)
    cosines, sines = [], []
    for k in range(1, half + 1):
        real, imag = parts[0], None
        for a in range(1, half + 1):
            angle = 2 * np.pi * (a * k % radix) / radix
            real = real + float(np.cos(angle)) * sums[a - 1]
            term = float(-np.sin(angle)) * gaps[a - 1]
            imag = term if imag is None else imag + term
        both = jnp.concatenate([real, imag], axis=1)
        spectrum = split_product(halves(both), pair(k)) * gain(k, 2 * LANES)
        series = split_product(halves(spectrum), pair(k), TRANSPOSED)
        cosines.append(series[:, :LANES])
        sines.append(series[:, LANES:])
    whole = base
    for value in cosines:
        whole = whole + value
    lower, upper = [], []
    for a in range(1, half + 1):
        even, odd = base, None
        for k in range(1, half + 1):
            angle = 2 * np.pi * (a * k % radix) / radix
            even = even + float(np.cos(angle)) * cosines[k - 1]
            term = float(np.sin(angle)) * sines[k - 1]
            odd = term if odd is None else odd + term
        lower.append(even - odd)
        upper.append(even + odd)
    return jnp.concatenate([whole] + lower + upper[::-1], axis=1)


def filter_blocks(rows, out_refs, mask_ref, table_ref, row_ref, table_copy):
    part = out_refs[0].shape[1]
    height = len(out_refs) * part
    radix = out_refs[0].shape[2] // LANES
    first_square = 2 * (radix // 2 + 1)
    active = [mask_ref[row] == 1 for row in rows]
    table_copy.wait()

    @pl.when(functools.reduce(jnp.logical_or, active))
    def _():
        fields = jnp.concatenate([ref[r] for r in range(len(rows)) for ref in out_refs], axis=0)
        squares = [row_ref[pl.ds(first_square + row, 1), :][:, :LANES] for row in rows]
        smooth = filtered(fields, squares, table_ref, row_ref)
        for r in range(len(rows)):

            @pl.when(active[r])
            def _():
                for i, ref in enumerate(out_refs):
                    start = r * height + i * part
                    ref[r] = smooth[start : start + part]


def field_rows(ref, start, count, r, rows, radix):
    step = rows * radix
    return jnp.concatenate(
        [ref[pl.ds(start * step + t * rows + r, count, stride=step), :] for t in range(radix)], axis=1
    )


def first_kernel(
    rows, split, mask, state_ref, mix_ref, mask_hbm, table_hbm, row_hbm, *refs
):
    out_refs = refs[:split]
    load, weights_ref, mask_ref, table_ref, row_ref, sems = refs[split:]
    levels = mix_ref.shape[1]
    part = levels // split
    radix = out_refs[0].shape[2] // LANES
    span = levels * rows * radix
    me = lax.axis_index("lat")
    field = jnp.bitwise_xor(me // split, mask)
    core = lax.rem(me, split)
    copies = [
        pltpu.make_async_copy(state_ref.at[pl.ds(pl.multiple_of(field * span, span), span)], load, sems.at[0]),
        pltpu.make_async_copy(mix_ref.at[field], weights_ref, sems.at[1]),
        pltpu.make_async_copy(mask_hbm, mask_ref, sems.at[2]),
        pltpu.make_async_copy(row_hbm, row_ref, sems.at[3]),
        pltpu.make_async_copy(table_hbm, table_ref, sems.at[4]),
    ]
    for copy in copies:
        copy.start()
    copies[1].wait()
    copies[0].wait()
    weights = halves(
        jnp.concatenate(
            [
                weights_ref[pl.ds(pl.multiple_of(jnp.bitwise_xor(core, c) * part, part), part), :]
                for c in range(split)
            ],
            axis=0,
        )
    )
    for r in range(rows):
        mixed = split_product(weights, halves(field_rows(load, 0, levels, r, rows, radix)))
        for c in range(split):
            out_refs[c][r] = mixed[c * part : (c + 1) * part]
    copies[2].wait()
    copies[3].wait()
    filter_blocks([me * rows + r for r in range(rows)], out_refs, mask_ref, table_ref, row_ref, copies[4])


def first_blocks(view, vertical_mix, polar_mask, tables, lon, rows, split, mask):
    table, row_table = tables
    levels = vertical_mix.shape[1]
    part = levels // split
    hbm = pl.BlockSpec(memory_space=pltpu.HBM)
    return pl.pallas_call(
        functools.partial(first_kernel, rows, split, mask),
        out_shape=[jax.ShapeDtypeStruct((rows, part, lon), F32)] * split,
        in_specs=[hbm] * 5,
        out_specs=[pl.BlockSpec(memory_space=pltpu.VMEM)] * split,
        scratch_shapes=[
            pltpu.VMEM((levels * rows * lon // LANES, LANES), F32),
            pltpu.VMEM(vertical_mix.shape[1:], F32),
            pltpu.SMEM(polar_mask.shape, jnp.int32),
            pltpu.VMEM(table.shape, BF16),
            pltpu.VMEM(row_table.shape, F32),
            pltpu.SemaphoreType.DMA((5,)),
        ],
        compiler_params=pltpu.CompilerParams(vmem_limit_bytes=VMEM_LIMIT),
        name="first_blocks",
    )(view, vertical_mix, polar_mask, table, row_table)


def spread(values, groups, width, count):
    lane = lax.broadcasted_iota(jnp.int32, (width, width * count), 1)
    repeat = (lax.rem(lane, width) == lax.broadcasted_iota(jnp.int32, lane.shape, 0)).astype(BF16)
    lane_group = lax.broadcasted_iota(jnp.int32, (1, width * count), 1) // width
    keep = jnp.concatenate(
        [
            jnp.broadcast_to((lane_group == group).astype(F32), (height, width * count))
            for group, height in groups
        ],
        axis=0,
    )
    return [
        (jnp.dot(value, repeat, preferred_element_type=F32) * keep).astype(BF16) for value in halves(values)
    ]


def rest_kernel(
    rows,
    split,
    masks,
    own_hbm,
    *refs,
):
    sources = [own_hbm]
    if split > 1:
        sources.append(refs[0])
        refs = refs[1:]
    (mix_ref, mask_hbm, coupling_ref, fractions_ref, index_ref, table_hbm, row_hbm) = refs[:7]
    out_refs = refs[7 : 7 + len(masks)]
    flux_ref = refs[7 + len(masks)]
    load, mask_ref, table_ref, row_ref, sems = refs[8 + len(masks) :]
    fields, levels, _ = mix_ref.shape
    part = levels // split
    radix = out_refs[0].shape[2] // LANES
    me = lax.axis_index("lat")
    chip = me // split
    core = lax.rem(me, split)
    copies = [pltpu.make_async_copy(ref, load.at[i], sems.at[i]) for i, ref in enumerate(sources)]
    mask_copy = pltpu.make_async_copy(mask_hbm, mask_ref, sems.at[2])
    row_copy = pltpu.make_async_copy(row_hbm, row_ref, sems.at[3])
    table_copy = pltpu.make_async_copy(table_hbm, table_ref, sems.at[4])
    for copy in copies + [mask_copy, row_copy, table_copy]:
        copy.start()
    chosen = [jnp.bitwise_xor(chip, mask) if split > 1 else mask for mask in masks]
    level_start = pl.multiple_of(core * part, part)
    blocks = [mix_ref[field, pl.ds(level_start, part), :] for field in chosen]
    blocks += [mix_ref[f, levels - 1 : levels, :] for f in range(fields)]
    groups = [(field, part) for field in chosen] + [(f, 1) for f in range(fields)]
    high, low = (spread(jnp.concatenate(blocks, axis=0), groups, levels, fields))
    height = len(masks) * part
    for i, copy in enumerate(copies):
        copy.wait()
        for r in range(rows):
            right = halves(field_rows(load.at[i], 0, fields * levels, r, rows, radix))
            mixed = split_product((high, low), right)
            place = r if split == 1 else jnp.bitwise_xor(core, i) * rows + r
            for j, ref in enumerate(out_refs):
                ref[place] = mixed[j * part : (j + 1) * part]
            if i == 0:
                bottom = mixed[height:]
                speed = jnp.sqrt(bottom[0:1] * bottom[0:1] + bottom[1:2] * bottom[1:2] + 1.0)
                flux = split_product(halves(coupling_ref[...]), halves(bottom))
                flux_ref[r] = speed * flux * fractions_ref[pl.ds(index_ref[r], 1), :]
    mask_copy.wait()
    row_copy.wait()
    filter_blocks(
        [chip * split * rows + r for r in range(rows * split)],
        out_refs,
        mask_ref,
        table_ref,
        row_ref,
        table_copy,
    )


def rest_blocks(
    views, vertical_mix, polar_mask, coupling, fractions, weight_index, tables, lon, rows, masks
):
    split = len(views)
    table, row_table = tables
    levels = vertical_mix.shape[1]
    part = levels // split
    hbm = pl.BlockSpec(memory_space=pltpu.HBM)
    vmem = pl.BlockSpec(memory_space=pltpu.VMEM)
    smem = pl.BlockSpec(memory_space=pltpu.SMEM)
    *blocks, weighted = pl.pallas_call(
        functools.partial(rest_kernel, rows, split, masks),
        out_shape=[jax.ShapeDtypeStruct((rows * split, part, lon), F32)] * len(masks)
        + [jax.ShapeDtypeStruct((rows, coupling.shape[0], lon), F32)],
        in_specs=[hbm] * split + [vmem, hbm, vmem, vmem, smem, hbm, hbm],
        out_specs=[vmem] * (len(masks) + 1),
        scratch_shapes=[
            pltpu.VMEM((split,) + views[0].shape, F32),
            pltpu.SMEM(polar_mask.shape, jnp.int32),
            pltpu.VMEM(table.shape, BF16),
            pltpu.VMEM(row_table.shape, F32),
            pltpu.SemaphoreType.DMA((5,)),
        ],
        compiler_params=pltpu.CompilerParams(vmem_limit_bytes=VMEM_LIMIT),
        name="rest_blocks",
    )(*views, vertical_mix, polar_mask, coupling, fractions, weight_index, table, row_table)
    return blocks, weighted


def ocean_kernel(lat_count, bounds_ref, left_ref, own_ref, right_ref, out_ref):
    rows = own_ref.shape[0]
    slots = out_ref.shape[0]
    half = rows // 2
    me = lax.axis_index("lat")
    start = bounds_ref[me] - half
    length = bounds_ref[me + 1] - bounds_ref[me] + 2 * half + 1
    shift = start - (me - 1) * rows
    near = [ref[r] for ref in (left_ref, own_ref, right_ref) for r in range(rows)]
    for s in range(slots):
        row = start + s
        valid = (s < length) & (row >= 0) & (row < lat_count)
        picked = jnp.zeros_like(near[0])
        for p, value in enumerate(near):
            picked = jnp.where(valid & (shift + s == p), value, picked)
        out_ref[s] = picked


def ocean_slots(weighted, band_bounds, lat_count, device_count):
    rows, flux_count, lon = weighted.shape
    ends = device_count - 1
    left = lax.ppermute(weighted, "lat", [(i, i + 1) for i in range(ends)])
    right = lax.ppermute(weighted, "lat", [(i + 1, i) for i in range(ends)])
    vmem = pl.BlockSpec(memory_space=pltpu.VMEM)
    slots = pl.pallas_call(
        functools.partial(ocean_kernel, lat_count),
        out_shape=jax.ShapeDtypeStruct((3 * rows, flux_count, lon), F32),
        in_specs=[pl.BlockSpec(memory_space=pltpu.SMEM)] + [vmem] * 3,
        out_specs=vmem,
        name="ocean",
    )(band_bounds, left, weighted, right)
    return jnp.transpose(slots, (1, 0, 2))


def place_kernel(split, masks, direct, *refs):
    in_refs, out_ref, buffer, sems = refs[:-3], refs[-3], refs[-2], refs[-1]
    part, lon = in_refs[0].shape[1:]
    rows = in_refs[len(masks)].shape[0]
    radix = lon // LANES
    chip_rows = rows * split
    tile = radix * SUBLANES
    me = lax.axis_index("lat")
    chip = me // split
    core = lax.rem(me, split)
    group_span = out_ref.shape[0] // part

    def put(ref, index, row):
        start = row // SUBLANES * tile + lax.rem(row, SUBLANES)
        for t in range(radix):
            buffer[pl.ds(start + t * SUBLANES, part, stride=group_span), :] = ref[
                index, :, t * LANES : (t + 1) * LANES
            ]

    for i, mask in enumerate(masks):
        base = jnp.bitwise_xor(chip, mask) * chip_rows
        for r in range(chip_rows):
            put(in_refs[i], r, base + r)
    base = jnp.bitwise_xor(chip, direct) * chip_rows
    for c in range(split):
        for r in range(rows):
            put(in_refs[len(masks) + c], r, base + jnp.bitwise_xor(core, c) * rows + r)
    copy = pltpu.make_async_copy(buffer, out_ref, sems.at[0])
    copy.start()
    copy.wait()


def place(bundles, masks, direct_blocks, direct, lat_count):
    part, lon = bundles[0].shape[1:]
    size = part * lat_count * lon // LANES
    vmem = pl.BlockSpec(memory_space=pltpu.VMEM)
    out = pl.pallas_call(
        functools.partial(place_kernel, len(direct_blocks), masks, direct),
        out_shape=jax.ShapeDtypeStruct((size, LANES), F32),
        in_specs=[vmem] * (len(bundles) + len(direct_blocks)),
        out_specs=pl.BlockSpec(memory_space=pltpu.HBM),
        scratch_shapes=[pltpu.VMEM((size, LANES), F32), pltpu.SemaphoreType.DMA((1,))],
        compiler_params=pltpu.CompilerParams(vmem_limit_bytes=VMEM_LIMIT),
        name="place",
    )(*bundles, *direct_blocks)
    tiles = out.reshape(part, lat_count // SUBLANES, lon // LANES, SUBLANES, LANES)
    return tiles.transpose(0, 1, 3, 2, 4).reshape(part, lat_count, lon)


def body(device_count, state, vertical_mix, coupling, fractions, weight_index, band_bounds, polar_mask):
    field_count, level_count = vertical_mix.shape[:2]
    stack_count, row_count, lon_count = state.shape
    lat_count = polar_mask.shape[0]
    part = stack_count // device_count
    tables = transform_tables(lon_count, lat_count)
    radix = lon_count // LANES
    view = state.reshape(stack_count, row_count, radix, LANES).transpose(0, 2, 1, 3).reshape(-1, LANES)
    surface = (coupling, fractions, weight_index, tables, lon_count, row_count)

    def exchange(block, mask):
        return lax.ppermute(block, "lat", [(i, i ^ mask) for i in range(device_count)])

    if part == SUBLANES and level_count == 2 * part and field_count == len(BUNDLES) + 2:
        split = 2
        sibling = exchange(view, 1)
        near, far = first_blocks(
            view, vertical_mix, polar_mask, tables, lon_count, row_count, split, DIRECT
        )
        direct = [exchange(near, DIRECT * split), exchange(far, DIRECT * split + 1)]
        masks = BUNDLES + (0,)
        blocks, weighted = rest_blocks((view, sibling), vertical_mix, polar_mask, *surface, masks)
        moved = [exchange(block, mask * split) for block, mask in zip(blocks, BUNDLES)]
        state_out = place(moved + [blocks[-1]], masks, direct, DIRECT, lat_count)
    else:
        masks = tuple(range(field_count))
        blocks, weighted = rest_blocks((view,), vertical_mix, polar_mask, *surface, masks)
        stacked = jnp.concatenate(blocks, axis=1)
        moved = lax.all_to_all(stacked, "lat", split_axis=1, concat_axis=0, tiled=True)
        state_out = jnp.transpose(moved, (1, 0, 2))
    ocean = ocean_slots(weighted, band_bounds, lat_count, device_count)
    return (state_out, ocean)


def solution(mesh):
    return jax.shard_map(
        functools.partial(body, mesh.shape["lat"]),
        mesh=mesh,
        in_specs=(P("member", "lat", None), P(), P(), P(), P(("member", "lat")), P(), P()),
        out_specs=(P(("member", "lat"), None, None), P(None, ("member", "lat"), None)),
        check_vma=False,
    )
```

time: 63.4 us -> 49.1 us (0.77)
  starting transfers between devices: 33.5 us -> 24.8 us
  Pallas kernels: 16.2 us -> 9.59 us
  local copies, waits for them, and re-layouts: 4.36 us -> 6.05 us
  waiting for transfers between devices: 8.26 us -> 7.53 us
    ppermute x15 -> x9, starting transfers between devices: 29.9 us -> 20 us  [exchange(): lax.ppermute(block, 'lat', [(i, i ^ mask) for i in range(device_count)])]
    pallas_call x3, Pallas kernels: 14.7 us -> 8.07 us  [the longest x1 4.53 us: rest_blocks(): pl.pallas_call(functools.partial(rest_kernel, rows, split, masks), out_sh...]
    transpose x0 -> x1, local copies, waits for them, and re-layouts: none -> 2.64 us  [body(): state.reshape(stack_count, row_count, radix, LANES).transpose(0, 2, 1, 3)]
    ppermute x1, starting transfers between devices: 2.36 us -> 3.48 us  [ocean_slots(): left = lax.ppermute(weighted, 'lat', [(i, i + 1) for i in range(ends)])]
    unnamed x28 -> x21, local copies, waits for them, and re-layouts: 4.36 us -> 3.41 us
    ppermute x15 -> x9, waiting for transfers between devices: 8.25 us -> 7.52 us  [exchange(): lax.ppermute(block, 'lat', [(i, i ^ mask) for i in range(device_count)])]
  transfers between devices with their start and end apart: 17 -> 11, of which waited for: 3 -> 2; matrix products, arithmetic and copies ran while one was open for 0% -> 0% of each run, Pallas kernels for 16% -> 7%
where the time goes in v2:
time: 49.1 us; the launch traced here: 48.7 us
  starting transfers between devices  24.8 us (51%)
  Pallas kernels  9.59 us (20%)
  waiting for transfers between devices  7.53 us (15%)
  local copies, waits for them, and re-layouts  6.05 us (12%)
  between operations  0.77 us (2%)
    ppermute x9, starting transfers between devices, exchange(): lax.ppermute(block, 'lat', [(i, i ^ mask) for i in range(device_count)])  20 us
    ppermute x9, waiting for transfers between devices, exchange(): lax.ppermute(block, 'lat', [(i, i ^ mask) for i in range(device_count)])  7.52 us
    pallas_call x1, Pallas kernels, rest_blocks(): pl.pallas_call(functools.partial(rest_kernel, rows, split, masks), out_sh...  4.53 us
    ppermute x1, starting transfers between devices, ocean_slots(): left = lax.ppermute(weighted, 'lat', [(i, i + 1) for i in range(ends)])  3.48 us
    unnamed x21, local copies, waits for them, and re-layouts  3.41 us
    transpose x1, local copies, waits for them, and re-layouts, body(): state.reshape(stack_count, row_count, radix, LANES).transpose(0, 2, 1, 3)  2.64 us
    pallas_call x1, Pallas kernels, first_blocks(): pl.pallas_call(functools.partial(first_kernel, rows, split, mask), out_sh...  1.81 us
    pallas_call x1, Pallas kernels, place(): pl.pallas_call(functools.partial(place_kernel, len(direct_blocks), masks,...  1.73 us
  transfers between devices with their start and end apart: 11, of which 2 were waited for; matrix products, arithmetic and copies ran while one was open for 0% of the time, Pallas kernels for 7%

profile of v2, /device:TPU:0, one launch (start us, length us, event | category | flops | bytes accessed | tf_op | source)
XLA Modules:
  0.0 48.7 jit_solution(14426978710752731197)
XLA Ops:
  0.6 3.4 %copy.12 = f32[128,2,1152]{0,2,1:T(8,128)} copy(f32[128,2,1152]{2,1,0:T(2,128)} %param.9) | data formatting | bytes 2359296 | tf_op args[0]
  4.0 0.0 copy-start.5
  4.0 0.0 copy-start.6
  4.0 0.0 copy-start.7
  4.0 2.6 %copy.13 = f32[128,9,2,128]{3,2,1,0:T(2,128)S(1)} copy(f32[128,9,2,128]{0,3,1,2:T(8,128)} %bitcast.13) | data formatting | bytes 2359296 | tf_op jit(solution)/shard_map/transpose | solution.py:414
  6.7 0.5 %collective-permute-start = (f32[2304,128]{1,0:T(8,128)S(1)}, f32[2304,128]{1,0:T(8,128)S(1)}, u32[]{:S(2)}, u32[]{:S(2)}) collective-permute-start(f32[2304,128]{1,0:T(8,128)S(1)} %bitcast.10), channel_id=1, source_target_pairs={{0,1},{1,0},{2,3},{3,2},{4,5},{5,4},{6,7},{7,6},{8,9},{9,8},{10,11... | collective-permute-start | bytes 3538952 | tf_op jit(solution)/shard_map/ppermute | solution.py:418
  7.2 2.5 %collective-permute-done.refs_0_ = f32[2304,128]{1,0:T(8,128)S(1)} collective-permute-done((f32[2304,128]{1,0:T(8,128)S(1)}, f32[2304,128]{1,0:T(8,128)S(1)}, u32[]{:S(2)}, u32[]{:S(2)}) %collective-permute-start) | collective-permute-done | bytes 1179680 | tf_op jit(solution)/shard_map/ppermute | solution.py:418
  9.7 4.5 %rest_blocks.1 = (f32[4,8,1152]{2,1,0:T(8,128)S(1)}, f32[4,8,1152]{2,1,0:T(8,128)S(1)}, f32[4,8,1152]{2,1,0:T(8,128)S(1)}, f32[4,8,1152]{2,1,0:T(8,128)S(1)}, f3...) custom-call(f32[2304,128]{1,0:T(8,128)S(1)} %bitcast.11, ...), custom_call_target="tpu_custom_call" | custom-call | tf_op jit(solution)/shard_map/rest_blocks/pallas_call | solution.py:305
  14.3 3.3 %collective-permute-start.1 = (f32[4,8,1152]{2,1,0:T(8,128)S(1)}, f32[4,8,1152]{2,1,0:T(8,128)S(1)}, u32[]{:S(2)}, u32[]{:S(2)}) collective-permute-start(f32[4,8,1152]{2,1,0:T(8,128)S(1)} %get-tuple-element.12), channel_id=1, source_target_pairs={{0,10},{1,11},{2,8},{3,9},{4,14},{5,15},{6,12},{7,13},{8,2},{9,3},... | collective-permute-start | bytes 442376 | tf_op jit(solution)/shard_map/ppermute | solution.py:418
  17.6 1.8 %first_blocks.1 = (f32[2,8,1152]{2,1,0:T(8,128)S(1)}, f32[2,8,1152]{2,1,0:T(8,128)S(1)}) custom-call(f32[2304,128]{1,0:T(8,128)S(1)} %bitcast.12, f32[8,16,16]{2,1,0:T(8,128)S(1)} %copy-done.1, s32[32]{0:T(128)S(1)} %copy-done.6, bf16[2,1152,256]{2,1,0:T(8,128)(2,1)S(1)} %copy-done, f32[48,256]{1,0:T(8,128)S(1)} %copy-done.2), custom_call_target="tpu_custom_call" | custom-call | tf_op jit(solution)/shard_map/first_blocks/pallas_call | solution.py:202
  19.4 0.8 %collective-permute-start.7 = (f32[2,8,1152]{2,1,0:T(8,128)S(1)}, f32[2,8,1152]{2,1,0:T(8,128)S(1)}, u32[]{:S(2)}, u32[]{:S(2)}) collective-permute-start(f32[2,8,1152]{2,1,0:T(8,128)S(1)} %get-tuple-element.19), channel_id=1, source_target_pairs={{0,12},{1,13},{2,14},{3,15},{4,8},{5,9},{6,10},{7,11},{8,4},{9,5},... | collective-permute-start | bytes 221192 | tf_op jit(solution)/shard_map/ppermute | solution.py:418
  20.2 2.3 %collective-permute-start.8 = (f32[2,8,1152]{2,1,0:T(8,128)S(1)}, f32[2,8,1152]{2,1,0:T(8,128)S(1)}, u32[]{:S(2)}, u32[]{:S(2)}) collective-permute-start(f32[2,8,1152]{2,1,0:T(8,128)S(1)} %get-tuple-element.20), channel_id=1, source_target_pairs={{0,13},{1,12},{2,15},{3,14},{4,9},{5,8},{6,11},{7,10},{8,5},{9,4},... | collective-permute-start | bytes 221192 | tf_op jit(solution)/shard_map/ppermute | solution.py:418
  22.5 1.3 %collective-permute-start.10 = (f32[2,4,1152]{2,1,0:T(4,128)S(1)}, f32[2,4,1152]{2,1,0:T(4,128)S(1)}, u32[]{:S(2)}, u32[]{:S(2)}) collective-permute-start(f32[2,4,1152]{2,1,0:T(4,128)S(1)} %get-tuple-element.21.own_ref), channel_id=1, source_target_pairs={{1,0},{2,1},{3,2},{4,3},{5,4},{6,5},{7,6},{8,7},{9,8},{10,9},{11,1... | collective-permute-start | bytes 110600 | tf_op jit(solution)/shard_map/ppermute | solution.py:346
  23.8 3.5 %collective-permute-start.9 = (f32[2,4,1152]{2,1,0:T(4,128)S(1)}, f32[2,4,1152]{2,1,0:T(4,128)S(1)}, u32[]{:S(2)}, u32[]{:S(2)}) collective-permute-start(f32[2,4,1152]{2,1,0:T(4,128)S(1)} %get-tuple-element.21.own_ref), channel_id=1, source_target_pairs={{0,1},{1,2},{2,3},{3,4},{4,5},{5,6},{6,7},{7,8},{8,9},{9,10},{10,1... | collective-permute-start | bytes 110600 | tf_op jit(solution)/shard_map/ppermute | solution.py:345
  27.2 2.7 %collective-permute-start.2 = (f32[4,8,1152]{2,1,0:T(8,128)S(1)}, f32[4,8,1152]{2,1,0:T(8,128)S(1)}, u32[]{:S(2)}, u32[]{:S(2)}) collective-permute-start(f32[4,8,1152]{2,1,0:T(8,128)S(1)} %get-tuple-element.13), channel_id=1, source_target_pairs={{0,14},{1,15},{2,12},{3,13},{4,10},{5,11},{6,8},{7,9},{8,6},{9,7},... | collective-permute-start | bytes 442376 | tf_op jit(solution)/shard_map/ppermute | solution.py:418
  29.9 0.0 collective-permute-done.8.refs_8_
  29.9 3.9 %collective-permute-start.3 = (f32[4,8,1152]{2,1,0:T(8,128)S(1)}, f32[4,8,1152]{2,1,0:T(8,128)S(1)}, u32[]{:S(2)}, u32[]{:S(2)}) collective-permute-start(f32[4,8,1152]{2,1,0:T(8,128)S(1)} %get-tuple-element.14), channel_id=1, source_target_pairs={{0,6},{1,7},{2,4},{3,5},{4,2},{5,3},{6,0},{7,1},{8,14},{9,15},{10,... | collective-permute-start | bytes 442376 | tf_op jit(solution)/shard_map/ppermute | solution.py:418
  33.8 0.0 collective-permute-done.10.right_ref
  33.8 3.2 %collective-permute-start.4 = (f32[4,8,1152]{2,1,0:T(8,128)S(1)}, f32[4,8,1152]{2,1,0:T(8,128)S(1)}, u32[]{:S(2)}, u32[]{:S(2)}) collective-permute-start(f32[4,8,1152]{2,1,0:T(8,128)S(1)} %get-tuple-element.15), channel_id=1, source_target_pairs={{0,8},{1,9},{2,10},{3,11},{4,12},{5,13},{6,14},{7,15},{8,0},{9,1},... | collective-permute-start | bytes 442376 | tf_op jit(solution)/shard_map/ppermute | solution.py:418
  37.0 0.0 collective-permute-done.1.refs_0_
  37.0 3.4 %collective-permute-start.6 = (f32[4,8,1152]{2,1,0:T(8,128)S(1)}, f32[4,8,1152]{2,1,0:T(8,128)S(1)}, u32[]{:S(2)}, u32[]{:S(2)}) collective-permute-start(f32[4,8,1152]{2,1,0:T(8,128)S(1)} %get-tuple-element.17), channel_id=1, source_target_pairs={{0,4},{1,5},{2,6},{3,7},{4,0},{5,1},{6,2},{7,3},{8,12},{9,13},{10,... | collective-permute-start | bytes 442376 | tf_op jit(solution)/shard_map/ppermute | solution.py:418
  40.4 1.5 %ocean.1 = f32[6,4,1152]{2,1,0:T(4,128)} custom-call(s32[17]{0:T(128)} %bounds_ref.1, f32[2,4,1152]{2,1,0:T(4,128)} %copy-done.9, f32[2,4,1152]{2,1,0:T(4,128)} %copy-done.4, f32[2,4,1152]{2,1,0:T(4,128)} %copy-done.8), custom_call_target="tpu_custom_call" | custom-call | tf_op jit(solution)/shard_map/ocean/pallas_call | solution.py:348
  42.0 5.0 %collective-permute-done.4.refs_3_ = f32[4,8,1152]{2,1,0:T(8,128)S(1)} collective-permute-done((f32[4,8,1152]{2,1,0:T(8,128)S(1)}, f32[4,8,1152]{2,1,0:T(8,128)S(1)}, u32[]{:S(2)}, u32[]{:S(2)}) %collective-permute-start.4) | collective-permute-done | bytes 147488 | tf_op jit(solution)/shard_map/ppermute | solution.py:418
  47.0 1.7 %place.1 = f32[2304,128]{1,0:T(8,128)} custom-call(f32[4,8,1152]{2,1,0:T(8,128)S(1)} %collective-permute-done.1.refs_0_, f32[4,8,1152]{2,1,0:T(8,128)S(1)} %collective-permute-done.2.refs_1_, f32[4,8,1152]{2,1,0:T(8,128)S(1)} %collective-permute-done.3.refs_2_, f32[4,8,1152]{2,1,0:T(8,128)S(1)} %collective-permute-done.4.refs_3_, ...), custom_call_target="tpu_custom_call" | custom-call | tf_op jit(solution)/shard_map/place/pallas_call | solution.py:394
  (24 shorter events, 0.1 us)
Async XLA Ops:
  4.0 5.7 %copy-start = (bf16[2,1152,256]{2,1,0:T(8,128)(2,1)S(1)}, bf16[2,1152,256]{2,1,0:T(8,128)(2,1)}, u32[]{:S(2)}) copy-start(bf16[2,1152,256]{2,1,0:T(8,128)(2,1)} %constant.4.clone.refs_6_.table_hbm) | copy-start | bytes 3538948
  4.0 5.7 %copy-start.1 = (f32[8,16,16]{2,1,0:T(8,128)S(1)}, f32[8,16,16]{2,1,0:T(8,128)}, u32[]{:S(2)}) copy-start(f32[8,16,16]{2,1,0:T(8,128)} %mix_ref.1) | copy-start | bytes 24580
  4.0 5.7 %copy-start.2 = (f32[48,256]{1,0:T(8,128)S(1)}, f32[48,256]{1,0:T(8,128)}, u32[]{:S(2)}) copy-start(f32[48,256]{1,0:T(8,128)} %constant.5.clone.refs_7_.row_hbm) | copy-start | bytes 147460
  4.0 5.7 %copy-start.3 = (f32[16,1152]{1,0:T(8,128)S(1)}, f32[16,1152]{1,0:T(8,128)}, u32[]{:S(2)}) copy-start(f32[16,1152]{1,0:T(8,128)} %refs_4_.1) | copy-start | bytes 221188
  4.0 5.7 %copy-start.5 = (f32[4,8]{1,0:T(4,128)S(1)}, f32[4,8]{1,0:T(4,128)}, u32[]{:S(2)}) copy-start(f32[4,8]{1,0:T(4,128)} %refs_3_.1) | copy-start | bytes 388
  4.0 5.7 %copy-start.6 = (s32[32]{0:T(128)S(1)}, s32[32]{0:T(128)}, u32[]{:S(2)}) copy-start(s32[32]{0:T(128)} %mask_hbm.1) | copy-start | bytes 388
  4.0 5.7 %copy-start.7 = (s32[2]{0:T(128)S(1)}, s32[2]{0:T(128)}, u32[]{:S(2)}) copy-start(s32[2]{0:T(128)} %refs_5_.1) | copy-start | bytes 28
  6.7 3.0 %collective-permute-start = (f32[2304,128]{1,0:T(8,128)S(1)}, f32[2304,128]{1,0:T(8,128)S(1)}, u32[]{:S(2)}, u32[]{:S(2)}) collective-permute-start(f32[2304,128]{1,0:T(8,128)S(1)} %bitcast.10), channel_id=1, source_target_pairs={{0,1},{1,0},{2,3},{3,2},{4,5},{5,4},{6,7},{7,6},{8,9},{9,8},{10,11... | collective-permute-start | bytes 3538952 | tf_op jit(solution)/shard_map/ppermute | solution.py:418
  14.3 9.5 %copy-start.4 = (f32[2,4,1152]{2,1,0:T(4,128)}, f32[2,4,1152]{2,1,0:T(4,128)S(1)}, u32[]{:S(2)}) copy-start(f32[2,4,1152]{2,1,0:T(4,128)S(1)} %get-tuple-element.21.own_ref) | copy-start | bytes 110596
  14.3 22.7 %collective-permute-start.1 = (f32[4,8,1152]{2,1,0:T(8,128)S(1)}, f32[4,8,1152]{2,1,0:T(8,128)S(1)}, u32[]{:S(2)}, u32[]{:S(2)}) collective-permute-start(f32[4,8,1152]{2,1,0:T(8,128)S(1)} %get-tuple-element.12), channel_id=1, source_target_pairs={{0,10},{1,11},{2,8},{3,9},{4,14},{5,15},{6,12},{7,13},{8,2},{9,3},... | collective-permute-start | bytes 442376 | tf_op jit(solution)/shard_map/ppermute | solution.py:418
  19.4 7.8 %collective-permute-start.7 = (f32[2,8,1152]{2,1,0:T(8,128)S(1)}, f32[2,8,1152]{2,1,0:T(8,128)S(1)}, u32[]{:S(2)}, u32[]{:S(2)}) collective-permute-start(f32[2,8,1152]{2,1,0:T(8,128)S(1)} %get-tuple-element.19), channel_id=1, source_target_pairs={{0,12},{1,13},{2,14},{3,15},{4,8},{5,9},{6,10},{7,11},{8,4},{9,5},... | collective-permute-start | bytes 221192 | tf_op jit(solution)/shard_map/ppermute | solution.py:418
  20.2 9.7 %collective-permute-start.8 = (f32[2,8,1152]{2,1,0:T(8,128)S(1)}, f32[2,8,1152]{2,1,0:T(8,128)S(1)}, u32[]{:S(2)}, u32[]{:S(2)}) collective-permute-start(f32[2,8,1152]{2,1,0:T(8,128)S(1)} %get-tuple-element.20), channel_id=1, source_target_pairs={{0,13},{1,12},{2,15},{3,14},{4,9},{5,8},{6,11},{7,10},{8,5},{9,4},... | collective-permute-start | bytes 221192 | tf_op jit(solution)/shard_map/ppermute | solution.py:418
  22.5 11.4 %collective-permute-start.10 = (f32[2,4,1152]{2,1,0:T(4,128)S(1)}, f32[2,4,1152]{2,1,0:T(4,128)S(1)}, u32[]{:S(2)}, u32[]{:S(2)}) collective-permute-start(f32[2,4,1152]{2,1,0:T(4,128)S(1)} %get-tuple-element.21.own_ref), channel_id=1, source_target_pairs={{1,0},{2,1},{3,2},{4,3},{5,4},{6,5},{7,6},{8,7},{9,8},{10,9},{11,1... | collective-permute-start | bytes 110600 | tf_op jit(solution)/shard_map/ppermute | solution.py:346
  23.8 13.2 %collective-permute-start.9 = (f32[2,4,1152]{2,1,0:T(4,128)S(1)}, f32[2,4,1152]{2,1,0:T(4,128)S(1)}, u32[]{:S(2)}, u32[]{:S(2)}) collective-permute-start(f32[2,4,1152]{2,1,0:T(4,128)S(1)} %get-tuple-element.21.own_ref), channel_id=1, source_target_pairs={{0,1},{1,2},{2,3},{3,4},{4,5},{5,6},{6,7},{7,8},{8,9},{9,10},{10,1... | collective-permute-start | bytes 110600 | tf_op jit(solution)/shard_map/ppermute | solution.py:345
  27.2 14.7 %collective-permute-start.2 = (f32[4,8,1152]{2,1,0:T(8,128)S(1)}, f32[4,8,1152]{2,1,0:T(8,128)S(1)}, u32[]{:S(2)}, u32[]{:S(2)}) collective-permute-start(f32[4,8,1152]{2,1,0:T(8,128)S(1)} %get-tuple-element.13), channel_id=1, source_target_pairs={{0,14},{1,15},{2,12},{3,13},{4,10},{5,11},{6,8},{7,9},{8,6},{9,7},... | collective-permute-start | bytes 442376 | tf_op jit(solution)/shard_map/ppermute | solution.py:418
  29.9 12.0 %collective-permute-start.3 = (f32[4,8,1152]{2,1,0:T(8,128)S(1)}, f32[4,8,1152]{2,1,0:T(8,128)S(1)}, u32[]{:S(2)}, u32[]{:S(2)}) collective-permute-start(f32[4,8,1152]{2,1,0:T(8,128)S(1)} %get-tuple-element.14), channel_id=1, source_target_pairs={{0,6},{1,7},{2,4},{3,5},{4,2},{5,3},{6,0},{7,1},{8,14},{9,15},{10,... | collective-permute-start | bytes 442376 | tf_op jit(solution)/shard_map/ppermute | solution.py:418
  33.8 6.6 %copy-start.8 = (f32[2,4,1152]{2,1,0:T(4,128)}, f32[2,4,1152]{2,1,0:T(4,128)S(1)}, u32[]{:S(2)}) copy-start(f32[2,4,1152]{2,1,0:T(4,128)S(1)} %collective-permute-done.10.right_ref) | copy-start | bytes 110596
  33.8 13.2 %collective-permute-start.4 = (f32[4,8,1152]{2,1,0:T(8,128)S(1)}, f32[4,8,1152]{2,1,0:T(8,128)S(1)}, u32[]{:S(2)}, u32[]{:S(2)}) collective-permute-start(f32[4,8,1152]{2,1,0:T(8,128)S(1)} %get-tuple-element.15), channel_id=1, source_target_pairs={{0,8},{1,9},{2,10},{3,11},{4,12},{5,13},{6,14},{7,15},{8,0},{9,1},... | collective-permute-start | bytes 442376 | tf_op jit(solution)/shard_map/ppermute | solution.py:418
  37.0 3.4 %copy-start.9 = (f32[2,4,1152]{2,1,0:T(4,128)}, f32[2,4,1152]{2,1,0:T(4,128)S(1)}, u32[]{:S(2)}) copy-start(f32[2,4,1152]{2,1,0:T(4,128)S(1)} %collective-permute-done.9.left_ref) | copy-start | bytes 110596
  37.0 10.0 %collective-permute-start.5 = (f32[4,8,1152]{2,1,0:T(8,128)S(1)}, f32[4,8,1152]{2,1,0:T(8,128)S(1)}, u32[]{:S(2)}, u32[]{:S(2)}) collective-permute-start(f32[4,8,1152]{2,1,0:T(8,128)S(1)} %get-tuple-element.16), channel_id=1, source_target_pairs={{0,2},{1,3},{2,0},{3,1},{4,6},{5,7},{6,4},{7,5},{8,10},{9,11},{10,... | collective-permute-start | bytes 442376 | tf_op jit(solution)/shard_map/ppermute | solution.py:418
  37.0 10.0 %collective-permute-start.6 = (f32[4,8,1152]{2,1,0:T(8,128)S(1)}, f32[4,8,1152]{2,1,0:T(8,128)S(1)}, u32[]{:S(2)}, u32[]{:S(2)}) collective-permute-start(f32[4,8,1152]{2,1,0:T(8,128)S(1)} %get-tuple-element.17), channel_id=1, source_target_pairs={{0,4},{1,5},{2,6},{3,7},{4,0},{5,1},{6,2},{7,3},{8,12},{9,13},{10,... | collective-permute-start | bytes 442376 | tf_op jit(solution)/shard_map/ppermute | solution.py:418

commit v3 on v2

v3 whole, which is shorter than its diff:
```python
import functools

import jax
import jax.numpy as jnp
import numpy as np
from jax import lax
from jax.experimental import pallas as pl
from jax.experimental.layout import Layout, with_layout_constraint
from jax.experimental.pallas import tpu as pltpu
from jax.sharding import PartitionSpec as P

COSCUT = 0.5
LANES = 128
SUBLANES = 8
DIRECT = (6,)
BUNDLES = (5, 7, 3, 4, 1, 2)
F32 = jnp.float32
BF16 = jnp.bfloat16
NORMAL = (((1,), (0,)), ((), ()))
TRANSPOSED = (((1,), (1,)), ((), ()))
VMEM_LIMIT = 48 << 20


def halves(values):
    high = values.astype(BF16)
    return high, (values - high.astype(F32)).astype(BF16)


def split_product(left, right, dims=NORMAL):
    dot = functools.partial(lax.dot_general, dimension_numbers=dims, preferred_element_type=F32)
    return dot(left[0], right[0]) + (dot(left[0], right[1]) + dot(left[1], right[0]))


def np_halves(values):
    values = np.asarray(values, np.float32)
    high = values.astype(jnp.bfloat16)
    return np.stack([high, (values - high.astype(np.float32)).astype(jnp.bfloat16)])


def transform_tables(lon_count, lat_count):
    radix = lon_count // LANES
    steps = radix // 2
    b = np.arange(LANES)[:, None]
    k2 = np.arange(LANES)[None, :]
    table = np.zeros((steps * 2 * LANES + LANES, 2 * LANES))
    for k in range(1, steps + 1):
        angle = 2 * np.pi * ((b * (k + radix * k2)) % lon_count) / lon_count
        c, s = np.cos(angle), np.sin(angle)
        table[(k - 1) * 2 * LANES : k * 2 * LANES] = np.block([[c, -s], [s, c]])
    half = LANES // 2
    angle = 2 * np.pi * ((b * k2) % LANES) / LANES
    table[steps * 2 * LANES :, :LANES] = np.concatenate(
        [np.cos(angle[:, : half + 1]), np.sin(angle[:, 1:half])], axis=1
    )
    wave = np.zeros((steps + 1, 2 * LANES))
    scale = np.full((steps + 1, 2 * LANES), 2.0 / lon_count)
    wave[0, :LANES] = np.concatenate([np.arange(half + 1), np.arange(1, half)]) * radix
    scale[0, [0, half]] = 1.0 / lon_count
    for k in range(1, steps + 1):
        wave[k] = np.tile(k + radix * np.arange(LANES), 2)
    limit = COSCUT**2 * np.sin(np.pi * wave / lon_count) ** 2
    latitude = np.pi * ((np.arange(lat_count) + 0.5) / lat_count - 0.5)
    square = np.repeat(np.cos(latitude)[:, None] ** 2, 2 * LANES, axis=1)
    rows = np.concatenate([limit, scale, square])
    rows = np.pad(rows, ((0, -len(rows) % SUBLANES), (0, 0)))
    return np_halves(table), rows.astype(np.float32)


def filtered(fields, squares, table_ref, row_ref):
    radix = fields.shape[1] // LANES
    half = radix // 2
    height = fields.shape[0] // len(squares)
    parts = [fields[:, a * LANES : (a + 1) * LANES] for a in range(radix)]
    sums = [parts[a] + parts[radix - a] for a in range(1, half + 1)]
    gaps = [parts[a] - parts[radix - a] for a in range(1, half + 1)]

    def pair(k):
        if k == 0:
            rows, width = slice(half * 2 * LANES, half * 2 * LANES + LANES), LANES
        else:
            rows, width = slice((k - 1) * 2 * LANES, k * 2 * LANES), 2 * LANES
        return table_ref[0, rows, :width], table_ref[1, rows, :width]

    def gain(k, width):
        limit = row_ref[k : k + 1, :LANES]
        scale = row_ref[half + 1 + k : half + 2 + k, :LANES]
        groups = [
            jnp.broadcast_to(square / jnp.maximum(square, limit) * scale, (height, LANES))
            for square in squares
        ]
        groups = jnp.concatenate(groups, axis=0)
        return groups if width == LANES else jnp.concatenate([groups, groups], axis=1)

    total = parts[0]
    for value in sums:
        total = total + value
    spectrum = split_product(halves(total), pair(0)) * gain(0, LANES)
    base = split_product(halves(spectrum), pair(0), TRANSPOSED)
    cosines, sines = [], []
    for k in range(1, half + 1):
        real, imag = parts[0], None
        for a in range(1, half + 1):
            angle = 2 * np.pi * (a * k % radix) / radix
            real = real + float(np.cos(angle)) * sums[a - 1]
            term = float(-np.sin(angle)) * gaps[a - 1]
            imag = term if imag is None else imag + term
        both = jnp.concatenate([real, imag], axis=1)
        spectrum = split_product(halves(both), pair(k)) * gain(k, 2 * LANES)
        series = split_product(halves(spectrum), pair(k), TRANSPOSED)
        cosines.append(series[:, :LANES])
        sines.append(series[:, LANES:])
    whole = base
    for value in cosines:
        whole = whole + value
    lower, upper = [], []
    for a in range(1, half + 1):
        even, odd = base, None
        for k in range(1, half + 1):
            angle = 2 * np.pi * (a * k % radix) / radix
            even = even + float(np.cos(angle)) * cosines[k - 1]
            term = float(np.sin(angle)) * sines[k - 1]
            odd = term if odd is None else odd + term
        lower.append(even - odd)
        upper.append(even + odd)
    return jnp.concatenate([whole] + lower + upper[::-1], axis=1)


def filter_blocks(rows, out_refs, mask_ref, table_ref, row_ref):
    part = out_refs[0].shape[1]
    height = len(out_refs) * part
    radix = out_refs[0].shape[2] // LANES
    first_square = 2 * (radix // 2 + 1)
    active = [mask_ref[row] == 1 for row in rows]

    @pl.when(functools.reduce(jnp.logical_or, active))
    def _():
        fields = jnp.concatenate([ref[r] for r in range(len(rows)) for ref in out_refs], axis=0)
        squares = [row_ref[pl.ds(first_square + row, 1), :][:, :LANES] for row in rows]
        smooth = filtered(fields, squares, table_ref, row_ref)
        for r in range(len(rows)):

            @pl.when(active[r])
            def _():
                for i, ref in enumerate(out_refs):
                    start = r * height + i * part
                    ref[r] = smooth[start : start + part]


def field_rows(ref, start, count, r, rows, radix):
    step = rows * radix
    return jnp.concatenate(
        [ref[pl.ds(start * step + t * rows + r, count, stride=step), :] for t in range(radix)], axis=1
    )


def first_kernel(rows, split, masks, state_ref, mix_ref, mask_hbm, table_hbm, row_hbm, *refs):
    outs = split * len(masks)
    out_refs = refs[:outs]
    load, weights_ref, mask_ref, table_ref, row_ref, sems = refs[outs:]
    levels = mix_ref.shape[1]
    part = levels // split
    radix = out_refs[0].shape[2] // LANES
    span = levels * rows * radix
    me = lax.axis_index("lat")
    core = lax.rem(me, split)
    fields = [jnp.bitwise_xor(me // split, mask) for mask in masks]
    loads = [
        pltpu.make_async_copy(
            state_ref.at[pl.ds(pl.multiple_of(field * span, span), span)], load.at[i], sems.at[4 + i]
        )
        for i, field in enumerate(fields)
    ]
    others = [
        pltpu.make_async_copy(mix_ref, weights_ref, sems.at[0]),
        pltpu.make_async_copy(mask_hbm, mask_ref, sems.at[1]),
        pltpu.make_async_copy(row_hbm, row_ref, sems.at[2]),
        pltpu.make_async_copy(table_hbm, table_ref, sems.at[3]),
    ]
    for copy in loads + others:
        copy.start()
    others[0].wait()
    for i, field in enumerate(fields):
        starts = [pl.multiple_of(jnp.bitwise_xor(core, c) * part, part) for c in range(split)]
        weights = halves(
            jnp.concatenate([weights_ref[field, pl.ds(start, part), :] for start in starts], axis=0)
        )
        loads[i].wait()
        for r in range(rows):
            mixed = split_product(weights, halves(field_rows(load.at[i], 0, levels, r, rows, radix)))
            for c in range(split):
                out_refs[i * split + c][r] = mixed[c * part : (c + 1) * part]
    others[1].wait()
    others[2].wait()
    others[3].wait()
    filter_blocks([me * rows + r for r in range(rows)], out_refs, mask_ref, table_ref, row_ref)


def first_blocks(view, vertical_mix, polar_mask, tables, lon, rows, split, masks):
    table, row_table = tables
    levels = vertical_mix.shape[1]
    part = levels // split
    operands = [
        pltpu.with_memory_space_constraint(value, pltpu.HBM)
        for value in (view, vertical_mix, polar_mask, jnp.asarray(table), jnp.asarray(row_table))
    ]
    return pl.pallas_call(
        functools.partial(first_kernel, rows, split, masks),
        out_shape=[pltpu.VMEM((rows, part, lon), F32)] * (split * len(masks)),
        in_specs=[pl.BlockSpec(memory_space=pltpu.HBM)] * len(operands),
        out_specs=[pl.BlockSpec(memory_space=pltpu.VMEM)] * (split * len(masks)),
        scratch_shapes=[
            pltpu.VMEM((len(masks), levels * rows * lon // LANES, LANES), F32),
            pltpu.VMEM(vertical_mix.shape, F32),
            pltpu.SMEM(polar_mask.shape, jnp.int32),
            pltpu.VMEM(table.shape, BF16),
            pltpu.VMEM(row_table.shape, F32),
            pltpu.SemaphoreType.DMA((4 + len(masks),)),
        ],
        compiler_params=pltpu.CompilerParams(vmem_limit_bytes=VMEM_LIMIT),
        name="first_blocks",
    )(*operands)


def spread(values, groups, width, count):
    lane = lax.broadcasted_iota(jnp.int32, (width, width * count), 1)
    repeat = (lax.rem(lane, width) == lax.broadcasted_iota(jnp.int32, lane.shape, 0)).astype(BF16)
    lane_group = lax.broadcasted_iota(jnp.int32, (1, width * count), 1) // width
    keep = jnp.concatenate(
        [
            jnp.broadcast_to((lane_group == group).astype(F32), (height, width * count))
            for group, height in groups
        ],
        axis=0,
    )
    return [
        (jnp.dot(value, repeat, preferred_element_type=F32) * keep).astype(BF16) for value in halves(values)
    ]


def rest_kernel(rows, split, masks, *refs):
    sources = refs[:split]
    refs = refs[split:] if split == 1 else refs[split + 1 :]
    (mix_ref, mask_ref, coupling_ref, fractions_ref, index_ref, table_ref, row_ref) = refs[:7]
    out_refs = refs[7 : 7 + len(masks)]
    flux_ref = refs[7 + len(masks)]
    fields, levels, _ = mix_ref.shape
    part = levels // split
    radix = out_refs[0].shape[2] // LANES
    me = lax.axis_index("lat")
    chip = me // split
    core = lax.rem(me, split)
    chosen = [jnp.bitwise_xor(chip, mask) if split > 1 else mask for mask in masks]
    level_start = pl.multiple_of(core * part, part)
    blocks = [mix_ref[field, pl.ds(level_start, part), :] for field in chosen]
    blocks += [mix_ref[f, levels - 1 : levels, :] for f in range(fields)]
    groups = [(field, part) for field in chosen] + [(f, 1) for f in range(fields)]
    weights = spread(jnp.concatenate(blocks, axis=0), groups, levels, fields)
    height = len(masks) * part
    for i, source in enumerate(sources):
        for r in range(rows):
            right = halves(field_rows(source, 0, fields * levels, r, rows, radix))
            mixed = split_product(weights, right)
            place = r if split == 1 else jnp.bitwise_xor(core, i) * rows + r
            for j, ref in enumerate(out_refs):
                ref[place] = mixed[j * part : (j + 1) * part]
            if i == 0:
                bottom = mixed[height:]
                speed = jnp.sqrt(bottom[0:1] * bottom[0:1] + bottom[1:2] * bottom[1:2] + 1.0)
                flux = split_product(halves(coupling_ref[...]), halves(bottom))
                flux_ref[r] = speed * flux * fractions_ref[pl.ds(index_ref[r], 1), :]
    filter_blocks(
        [chip * split * rows + r for r in range(rows * split)], out_refs, mask_ref, table_ref, row_ref
    )


def rest_blocks(
    views, after, vertical_mix, polar_mask, coupling, fractions, weight_index, tables, lon, rows, masks
):
    split = len(views)
    levels = vertical_mix.shape[1]
    part = levels // split
    vmem = pl.BlockSpec(memory_space=pltpu.VMEM)
    smem = pl.BlockSpec(memory_space=pltpu.SMEM)
    *blocks, weighted = pl.pallas_call(
        functools.partial(rest_kernel, rows, split, masks),
        out_shape=[pltpu.VMEM((rows * split, part, lon), F32)] * len(masks)
        + [pltpu.VMEM((rows, coupling.shape[0], lon), F32)],
        in_specs=[vmem] * split
        + [vmem] * len(after)
        + [vmem, smem, vmem, vmem, smem, vmem, vmem],
        out_specs=[vmem] * (len(masks) + 1),
        compiler_params=pltpu.CompilerParams(vmem_limit_bytes=VMEM_LIMIT),
        name="rest_blocks",
    )(*views, *after, vertical_mix, polar_mask, coupling, fractions, weight_index, *tables)
    return blocks, weighted


def ocean_kernel(lat_count, split, bounds_ref, own_ref, *refs):
    near_refs, out_ref = refs[:-1], refs[-1]
    rows = own_ref.shape[0]
    slots = out_ref.shape[0]
    half = rows // 2
    me = lax.axis_index("lat")
    start = bounds_ref[me] - half
    length = bounds_ref[me + 1] - bounds_ref[me] + 2 * half + 1
    shift = start - (me - 1) * rows
    first, last = ([ref[r] for r in range(rows)] for ref in near_refs)
    if split > 1:
        upper = lax.rem(me, split) == 0
        first, last = (
            [jnp.where(upper, outer, other) for outer, other in zip(last, first)],
            [jnp.where(upper, other, outer) for outer, other in zip(last, first)],
        )
    near = first + [own_ref[r] for r in range(rows)] + last
    for s in range(slots):
        row = start + s
        valid = (s < length) & (row >= 0) & (row < lat_count)
        picked = jnp.zeros_like(near[0])
        for p, value in enumerate(near):
            picked = jnp.where(valid & (shift + s == p), value, picked)
        out_ref[s] = picked


def ocean_slots(weighted, band_bounds, lat_count, device_count, split):
    rows, flux_count, lon = weighted.shape
    ends = device_count - 1
    if split == 2:
        pairs = [(i, i + 1) for i in range(1, ends, 2)]
        near = [
            lax.ppermute(weighted, "lat", [(i, i ^ 1) for i in range(device_count)]),
            lax.ppermute(weighted, "lat", pairs + [(j, i) for i, j in pairs]),
        ]
    else:
        near = [
            lax.ppermute(weighted, "lat", [(i, i + 1) for i in range(ends)]),
            lax.ppermute(weighted, "lat", [(i + 1, i) for i in range(ends)]),
        ]
    vmem = pl.BlockSpec(memory_space=pltpu.VMEM)
    slots = pl.pallas_call(
        functools.partial(ocean_kernel, lat_count, split),
        out_shape=jax.ShapeDtypeStruct((3 * rows, flux_count, lon), F32),
        in_specs=[pl.BlockSpec(memory_space=pltpu.SMEM)] + [vmem] * 3,
        out_specs=vmem,
        name="ocean",
    )(band_bounds, weighted, *near)
    return slots


def place_kernel(split, masks, direct, *refs):
    blocks = len(masks) + split * len(direct)
    in_refs, (out_ref, buffer, sems) = refs[:blocks], refs[-3:]
    part, lon = in_refs[0].shape[1:]
    rows = in_refs[len(masks)].shape[0]
    radix = lon // LANES
    chip_rows = rows * split
    tile = radix * SUBLANES
    span = out_ref.shape[0] // part
    chips = SUBLANES // chip_rows
    me = lax.axis_index("lat")
    chip = me // split
    core = lax.rem(me, split)
    copies = []
    for group in range(span // tile):
        for low in range(chips):
            mask = group * chips + low
            base = jnp.bitwise_xor(lax.rem(chip, chips), low) * chip_rows
            if mask in masks:
                ref = in_refs[masks.index(mask)]
                items = [(ref, r, base + r) for r in range(chip_rows)]
            else:
                first = len(masks) + direct.index(mask) * split
                items = [
                    (in_refs[first + c], r, base + jnp.bitwise_xor(core, c) * rows + r)
                    for c in range(split)
                    for r in range(rows)
                ]
            for ref, index, row in items:
                for t in range(radix):
                    buffer[group, pl.ds(row + t * SUBLANES, part, stride=tile), :] = ref[
                        index, :, t * LANES : (t + 1) * LANES
                    ]
        start = jnp.bitwise_xor(chip // chips, group) * tile
        for f in range(part):
            copy = pltpu.make_async_copy(
                buffer.at[group, pl.ds(f * tile, tile)],
                out_ref.at[pl.ds(pl.multiple_of(f * span + start, SUBLANES), tile)],
                sems.at[group, f],
            )
            copy.start()
            copies.append(copy)
    for copy in copies:
        copy.wait()


def place(bundles, masks, direct_blocks, direct, lat_count, after):
    part, lon = bundles[0].shape[1:]
    rows = direct_blocks[0].shape[0]
    split = len(direct_blocks) // len(direct)
    size = part * lat_count * lon // LANES
    groups = lat_count // SUBLANES
    vmem = pl.BlockSpec(memory_space=pltpu.VMEM)
    out = pl.pallas_call(
        functools.partial(place_kernel, split, masks, direct),
        out_shape=jax.ShapeDtypeStruct((size, LANES), F32),
        in_specs=[vmem] * (len(bundles) + len(direct_blocks)) + [pl.BlockSpec(memory_space=pl.ANY)],
        out_specs=pl.BlockSpec(memory_space=pltpu.HBM),
        scratch_shapes=[
            pltpu.VMEM((groups, size // groups, LANES), F32),
            pltpu.SemaphoreType.DMA((groups, part)),
        ],
        compiler_params=pltpu.CompilerParams(vmem_limit_bytes=VMEM_LIMIT),
        name="place",
    )(*bundles, *direct_blocks, after)
    tiles = out.reshape(part, groups, lon // LANES, SUBLANES, LANES)
    return tiles.transpose(0, 1, 3, 2, 4).reshape(part, lat_count, lon)


def body(device_count, state, vertical_mix, coupling, fractions, weight_index, band_bounds, polar_mask):
    field_count, level_count = vertical_mix.shape[:2]
    stack_count, row_count, lon_count = state.shape
    lat_count = polar_mask.shape[0]
    part = stack_count // device_count
    tables = transform_tables(lon_count, lat_count)
    radix = lon_count // LANES
    blocked = with_layout_constraint(
        state.reshape(stack_count, row_count, radix, LANES), Layout(major_to_minor=(0, 2, 1, 3))
    )
    view = blocked.transpose(0, 2, 1, 3).reshape(-1, LANES)
    surface = (coupling, fractions, weight_index, tables, lon_count, row_count)

    def exchange(block, mask):
        return lax.ppermute(block, "lat", [(i, i ^ mask) for i in range(device_count)])

    if part == SUBLANES and level_count == 2 * part and field_count == len(BUNDLES) + len(DIRECT) + 1:
        split = 2
        sibling = exchange(view, 1)
        first = first_blocks(
            view, vertical_mix, polar_mask, tables, lon_count, row_count, split, DIRECT
        )
        partners = [mask * split + c for mask in DIRECT for c in range(split)]
        direct = [exchange(block, partner) for block, partner in zip(first, partners)]
        masks = BUNDLES + (0,)
        blocks, weighted = rest_blocks((view, sibling), first[:1], vertical_mix, polar_mask, *surface, masks)
        (blocks[0], *direct) = lax.optimization_barrier((blocks[0], *direct))
        moved = [exchange(block, mask * split) for block, mask in zip(blocks, BUNDLES)]
        ocean = ocean_slots(weighted, band_bounds, lat_count, device_count, split)
        state_out = place(moved + [blocks[-1]], masks, direct, DIRECT, lat_count, ocean)
    else:
        masks = tuple(range(field_count))
        blocks, weighted = rest_blocks((view,), (), vertical_mix, polar_mask, *surface, masks)
        stacked = jnp.concatenate(blocks, axis=1)
        moved = lax.all_to_all(stacked, "lat", split_axis=1, concat_axis=0, tiled=True)
        state_out = jnp.transpose(moved, (1, 0, 2))
        ocean = ocean_slots(weighted, band_bounds, lat_count, device_count, 1)
    return (state_out, jnp.transpose(ocean, (1, 0, 2)))


def solution(mesh):
    return jax.shard_map(
        functools.partial(body, mesh.shape["lat"]),
        mesh=mesh,
        in_specs=(P("member", "lat", None), P(), P(), P(), P(("member", "lat")), P(), P()),
        out_specs=(P(("member", "lat"), None, None), P(None, ("member", "lat"), None)),
        check_vma=False,
    )
```

time: 49.1 us -> 39.7 us (0.81)
  starting transfers between devices: 24.8 us -> 20.8 us
  local copies, waits for them, and re-layouts: 6.05 us -> 2.33 us
  waiting for transfers between devices: 7.53 us -> 6.42 us
  Pallas kernels: 9.59 us -> 9.08 us
    ppermute x9, starting transfers between devices: 20 us -> 15.7 us  [exchange(): lax.ppermute(block, 'lat', [(i, i ^ mask) for i in range(device_count)])]
    transpose x1 -> x0, local copies, waits for them, and re-layouts: 2.64 us -> none  [body(): state.reshape(stack_count, row_count, radix, LANES).transpose(0, 2, 1, 3)]
    ppermute x9, waiting for transfers between devices: 7.52 us -> 6.42 us  [exchange(): lax.ppermute(block, 'lat', [(i, i ^ mask) for i in range(device_count)])]
    unnamed x21 -> x24, local copies, waits for them, and re-layouts: 3.41 us -> 2.33 us
    pallas_call x1, Pallas kernels: 4.53 us -> 3.52 us  [rest_blocks(): pl.pallas_call(functools.partial(rest_kernel, rows, split, masks), out_sh...]
    pallas_call x3, Pallas kernels: 5.07 us -> 5.56 us  [the longest x1 2.7 us: first_blocks(): pl.pallas_call(functools.partial(first_kernel, rows, split, masks), out_s...]
  transfers between devices with their start and end apart: 11 -> 11, of which waited for: 2 -> 4; matrix products, arithmetic and copies ran while one was open for 0% -> 0% of each run, Pallas kernels for 7% -> 20%
where the time goes in v3:
time: 39.7 us; the launch traced here: 39.5 us
  starting transfers between devices  20.8 us (52%)
  Pallas kernels  9.08 us (23%)
  waiting for transfers between devices  6.42 us (16%)
  local copies, waits for them, and re-layouts  2.33 us (6%)
  between operations  0.83 us (2%)
    ppermute x9, starting transfers between devices, exchange(): lax.ppermute(block, 'lat', [(i, i ^ mask) for i in range(device_count)])  15.7 us
    ppermute x9, waiting for transfers between devices, exchange(): lax.ppermute(block, 'lat', [(i, i ^ mask) for i in range(device_count)])  6.42 us
    ppermute x1, starting transfers between devices, ocean_slots(): lax.ppermute(weighted, 'lat', [(i, i ^ 1) for i in range(device_count)])  4.41 us
    pallas_call x1, Pallas kernels, rest_blocks(): pl.pallas_call(functools.partial(rest_kernel, rows, split, masks), out_sh...  3.52 us
    pallas_call x1, Pallas kernels, first_blocks(): pl.pallas_call(functools.partial(first_kernel, rows, split, masks), out_s...  2.7 us
    unnamed x24, local copies, waits for them, and re-layouts  2.33 us
    pallas_call x1, Pallas kernels, ocean_slots(): pl.pallas_call(functools.partial(ocean_kernel, lat_count, split), out_sha...  1.53 us
    pallas_call x1, Pallas kernels, place(): pl.pallas_call(functools.partial(place_kernel, split, masks, direct), out...  1.34 us
  transfers between devices with their start and end apart: 11, of which 4 were waited for; matrix products, arithmetic and copies ran while one was open for 0% of the time, Pallas kernels for 20%

profile of v3, /device:TPU:0, one launch (start us, length us, event | category | flops | bytes accessed | tf_op | source)
XLA Modules:
  0.0 39.5 jit_solution(4896444016285538972)
XLA Ops:
  0.6 0.0 copy-start.1
  0.7 0.0 copy-start.4
  0.7 0.5 %collective-permute-start = (f32[2304,128]{1,0:T(8,128)}, f32[2304,128]{1,0:T(8,128)S(1)}, u32[]{:S(2)}, u32[]{:S(2)}) collective-permute-start(f32[2304,128]{1,0:T(8,128)} %bitcast.11), channel_id=1, source_target_pairs={{0,1},{1,0},{2,3},{3,2},{4,5},{5,4},{6,7},{7,6},{8,9},{9,8},{10,11... | collective-permute-start | bytes 3538952 | tf_op jit(solution)/shard_map/ppermute | solution.py:432
  1.2 2.7 %first_blocks.1 = (f32[2,8,1152]{2,1,0:T(8,128)S(1)}, f32[2,8,1152]{2,1,0:T(8,128)S(1)}) custom-call(f32[2304,128]{1,0:T(8,128)} %bitcast.12, f32[8,16,16]{2,1,0:T(8,128)} %refs_3_.1, s32[32]{0:T(128)} %refs_4_.1, bf16[2,1152,256]{2,1,0:T(8,128)(2,1)} %constant.4.clone.table_hbm.refs_8_, f32[48,256]{1,0:T(8,128)} %constant.5.clone.row_hbm.refs_9_), custom_call_target="tpu_custom_call" | custom-call | tf_op jit(solution)/shard_map/first_blocks/pallas_call | solution.py:206
  3.9 3.6 %collective-permute-start.1 = (f32[2,8,1152]{2,1,0:T(8,128)S(1)}, f32[2,8,1152]{2,1,0:T(8,128)S(1)}, u32[]{:S(2)}, u32[]{:S(2)}) collective-permute-start(f32[2,8,1152]{2,1,0:T(8,128)S(1)} %get-tuple-element.15.refs_2_), channel_id=1, source_target_pairs={{0,12},{1,13},{2,14},{3,15},{4,8},{5,9},{6,10},{7,11},{8,4},{9,5},... | collective-permute-start | bytes 221192 | tf_op jit(solution)/shard_map/ppermute | solution.py:432
  7.5 1.1 %collective-permute-start.2 = (f32[2,8,1152]{2,1,0:T(8,128)S(1)}, f32[2,8,1152]{2,1,0:T(8,128)S(1)}, u32[]{:S(2)}, u32[]{:S(2)}) collective-permute-start(f32[2,8,1152]{2,1,0:T(8,128)S(1)} %get-tuple-element.17), channel_id=1, source_target_pairs={{0,13},{1,12},{2,15},{3,14},{4,9},{5,8},{6,11},{7,10},{8,5},{9,4},... | collective-permute-start | bytes 221192 | tf_op jit(solution)/shard_map/ppermute | solution.py:432
  8.7 0.0 copy-start.5
  8.7 0.9 %copy-done.5 = f32[16,1152]{1,0:T(8,128)S(1)} copy-done((f32[16,1152]{1,0:T(8,128)S(1)}, f32[16,1152]{1,0:T(8,128)}, u32[]{:S(2)}) %copy-start.5) | copy-done | bytes 73752
  9.6 3.5 %rest_blocks.1 = (f32[4,8,1152]{2,1,0:T(8,128)S(1)}, f32[4,8,1152]{2,1,0:T(8,128)S(1)}, f32[4,8,1152]{2,1,0:T(8,128)S(1)}, f32[4,8,1152]{2,1,0:T(8,128)S(1)}, f3...) custom-call(f32[2304,128]{1,0:T(8,128)S(1)} %bitcast.13, ...), custom_call_target="tpu_custom_call" | custom-call | tf_op jit(solution)/shard_map/rest_blocks/pallas_call | solution.py:284
  13.1 0.1 collective-permute-done.2.refs_8_
  13.2 0.0 collective-permute-start.3
  13.2 0.7 %collective-permute-start.10 = (f32[2,4,1152]{2,1,0:T(4,128)S(1)}, f32[2,4,1152]{2,1,0:T(4,128)S(1)}, u32[]{:S(2)}, u32[]{:S(2)}) collective-permute-start(f32[2,4,1152]{2,1,0:T(4,128)S(1)} %get-tuple-element.27.own_ref), channel_id=1, source_target_pairs={{1,2},{3,4},{5,6},{7,8},{9,10},{11,12},{13,14},{2,1},{4,3},{6,5},{... | collective-permute-start | bytes 110600 | tf_op jit(solution)/shard_map/ppermute | solution.py:331
  13.9 4.4 %collective-permute-start.9 = (f32[2,4,1152]{2,1,0:T(4,128)S(1)}, f32[2,4,1152]{2,1,0:T(4,128)S(1)}, u32[]{:S(2)}, u32[]{:S(2)}) collective-permute-start(f32[2,4,1152]{2,1,0:T(4,128)S(1)} %get-tuple-element.27.own_ref), channel_id=1, source_target_pairs={{0,1},{1,0},{2,3},{3,2},{4,5},{5,4},{6,7},{7,6},{8,9},{9,8},{10,11... | collective-permute-start | bytes 110600 | tf_op jit(solution)/shard_map/ppermute | solution.py:330
  18.3 1.4 %collective-permute-start.4 = (f32[4,8,1152]{2,1,0:T(8,128)S(1)}, f32[4,8,1152]{2,1,0:T(8,128)S(1)}, u32[]{:S(2)}, u32[]{:S(2)}) collective-permute-start(f32[4,8,1152]{2,1,0:T(8,128)S(1)} %get-tuple-element.19), channel_id=1, source_target_pairs={{0,14},{1,15},{2,12},{3,13},{4,10},{5,11},{6,8},{7,9},{8,6},{9,7},... | collective-permute-start | bytes 442376 | tf_op jit(solution)/shard_map/ppermute | solution.py:432
  19.7 2.4 %collective-permute-start.5 = (f32[4,8,1152]{2,1,0:T(8,128)S(1)}, f32[4,8,1152]{2,1,0:T(8,128)S(1)}, u32[]{:S(2)}, u32[]{:S(2)}) collective-permute-start(f32[4,8,1152]{2,1,0:T(8,128)S(1)} %get-tuple-element.20), channel_id=1, source_target_pairs={{0,6},{1,7},{2,4},{3,5},{4,2},{5,3},{6,0},{7,1},{8,14},{9,15},{10,... | collective-permute-start | bytes 442376 | tf_op jit(solution)/shard_map/ppermute | solution.py:432
  22.1 6.6 %collective-permute-start.6 = (f32[4,8,1152]{2,1,0:T(8,128)S(1)}, f32[4,8,1152]{2,1,0:T(8,128)S(1)}, u32[]{:S(2)}, u32[]{:S(2)}) collective-permute-start(f32[4,8,1152]{2,1,0:T(8,128)S(1)} %get-tuple-element.21), channel_id=1, source_target_pairs={{0,8},{1,9},{2,10},{3,11},{4,12},{5,13},{6,14},{7,15},{8,0},{9,1},... | collective-permute-start | bytes 442376 | tf_op jit(solution)/shard_map/ppermute | solution.py:432
  28.8 0.1 collective-permute-start.8
  28.9 0.5 %copy-done.11 = f32[2,4,1152]{2,1,0:T(4,128)} copy-done((f32[2,4,1152]{2,1,0:T(4,128)}, f32[2,4,1152]{2,1,0:T(4,128)S(1)}, u32[]{:S(2)}) %copy-start.11) | copy-done | bytes 36888
  29.4 1.5 %ocean.1.refs_9_ = f32[6,4,1152]{2,1,0:T(4,128)} custom-call(s32[17]{0:T(128)} %bounds_ref.1, f32[2,4,1152]{2,1,0:T(4,128)} %copy-done.6, f32[2,4,1152]{2,1,0:T(4,128)} %copy-done.11, f32[2,4,1152]{2,1,0:T(4,128)} %copy-done.10), custom_call_target="tpu_custom_call" | custom-call | tf_op jit(solution)/shard_map/ocean/pallas_call | solution.py:339
  30.9 0.4 %collective-permute-done.5.refs_2_ = f32[4,8,1152]{2,1,0:T(8,128)S(1)} collective-permute-done((f32[4,8,1152]{2,1,0:T(8,128)S(1)}, f32[4,8,1152]{2,1,0:T(8,128)S(1)}, u32[]{:S(2)}, u32[]{:S(2)}) %collective-permute-start.5) | collective-permute-done | bytes 147488 | tf_op jit(solution)/shard_map/ppermute | solution.py:432
  31.3 5.5 %collective-permute-done.6.refs_3_ = f32[4,8,1152]{2,1,0:T(8,128)S(1)} collective-permute-done((f32[4,8,1152]{2,1,0:T(8,128)S(1)}, f32[4,8,1152]{2,1,0:T(8,128)S(1)}, u32[]{:S(2)}, u32[]{:S(2)}) %collective-permute-start.6) | collective-permute-done | bytes 147488 | tf_op jit(solution)/shard_map/ppermute | solution.py:432
  36.8 0.5 %collective-permute-done.8.refs_5_ = f32[4,8,1152]{2,1,0:T(8,128)S(1)} collective-permute-done((f32[4,8,1152]{2,1,0:T(8,128)S(1)}, f32[4,8,1152]{2,1,0:T(8,128)S(1)}, u32[]{:S(2)}, u32[]{:S(2)}) %collective-permute-start.8) | collective-permute-done | bytes 147488 | tf_op jit(solution)/shard_map/ppermute | solution.py:432
  37.2 0.9 %copy-done.2 = f32[6,4,1152]{2,1,0:T(4,128)S(1)} copy-done((f32[6,4,1152]{2,1,0:T(4,128)S(1)}, f32[6,4,1152]{2,1,0:T(4,128)}, u32[]{:S(2)}) %copy-start.2) | copy-done | bytes 110616
  38.1 1.3 %place.1 = f32[2304,128]{1,0:T(8,128)} custom-call(f32[4,8,1152]{2,1,0:T(8,128)S(1)} %collective-permute-done.3.refs_0_, f32[4,8,1152]{2,1,0:T(8,128)S(1)} %collective-permute-done.4.refs_1_, f32[4,8,1152]{2,1,0:T(8,128)S(1)} %collective-permute-done.5.refs_2_, f32[4,8,1152]{2,1,0:T(8,128)S(1)} %collective-permute-done.6.refs_3_, ...), custom_call_target="tpu_custom_call" | custom-call | tf_op jit(solution)/shard_map/place/pallas_call | solution.py:402
  (26 shorter events, 0.1 us)
Async XLA Ops:
  0.6 8.0 %copy-start = (f32[128,2,1152]{2,1,0:T(2,128)S(1)}, f32[128,2,1152]{2,1,0:T(2,128)}, u32[]{:S(2)}) copy-start(f32[128,2,1152]{2,1,0:T(2,128)} %param.9) | copy-start | bytes 3538948
  0.6 8.0 %copy-start.1 = (bf16[2,1152,256]{2,1,0:T(8,128)(2,1)S(1)}, bf16[2,1152,256]{2,1,0:T(8,128)(2,1)}, u32[]{:S(2)}) copy-start(bf16[2,1152,256]{2,1,0:T(8,128)(2,1)} %constant.4.clone.table_hbm.refs_8_) | copy-start | bytes 3538948
  0.7 8.0 %copy-start.3 = (f32[8,16,16]{2,1,0:T(8,128)S(1)}, f32[8,16,16]{2,1,0:T(8,128)}, u32[]{:S(2)}) copy-start(f32[8,16,16]{2,1,0:T(8,128)} %refs_3_.1) | copy-start | bytes 24580
  0.7 8.0 %copy-start.4 = (f32[48,256]{1,0:T(8,128)S(1)}, f32[48,256]{1,0:T(8,128)}, u32[]{:S(2)}) copy-start(f32[48,256]{1,0:T(8,128)} %constant.5.clone.row_hbm.refs_9_) | copy-start | bytes 147460
  0.7 8.0 %copy-start.7 = (f32[4,8]{1,0:T(4,128)S(1)}, f32[4,8]{1,0:T(4,128)}, u32[]{:S(2)}) copy-start(f32[4,8]{1,0:T(4,128)} %refs_5_.1) | copy-start | bytes 388
  0.7 8.0 %copy-start.8 = (s32[32]{0:T(128)S(1)}, s32[32]{0:T(128)}, u32[]{:S(2)}) copy-start(s32[32]{0:T(128)} %refs_4_.1) | copy-start | bytes 388
  0.7 8.0 %copy-start.9 = (s32[2]{0:T(128)S(1)}, s32[2]{0:T(128)}, u32[]{:S(2)}) copy-start(s32[2]{0:T(128)} %refs_7_.1) | copy-start | bytes 28
  0.7 7.9 %collective-permute-start = (f32[2304,128]{1,0:T(8,128)}, f32[2304,128]{1,0:T(8,128)S(1)}, u32[]{:S(2)}, u32[]{:S(2)}) collective-permute-start(f32[2304,128]{1,0:T(8,128)} %bitcast.11), channel_id=1, source_target_pairs={{0,1},{1,0},{2,3},{3,2},{4,5},{5,4},{6,7},{7,6},{8,9},{9,8},{10,11... | collective-permute-start | bytes 3538952 | tf_op jit(solution)/shard_map/ppermute | solution.py:432
  3.9 9.2 %collective-permute-start.1 = (f32[2,8,1152]{2,1,0:T(8,128)S(1)}, f32[2,8,1152]{2,1,0:T(8,128)S(1)}, u32[]{:S(2)}, u32[]{:S(2)}) collective-permute-start(f32[2,8,1152]{2,1,0:T(8,128)S(1)} %get-tuple-element.15.refs_2_), channel_id=1, source_target_pairs={{0,12},{1,13},{2,14},{3,15},{4,8},{5,9},{6,10},{7,11},{8,4},{9,5},... | collective-permute-start | bytes 221192 | tf_op jit(solution)/shard_map/ppermute | solution.py:432
  7.5 5.7 %collective-permute-start.2 = (f32[2,8,1152]{2,1,0:T(8,128)S(1)}, f32[2,8,1152]{2,1,0:T(8,128)S(1)}, u32[]{:S(2)}, u32[]{:S(2)}) collective-permute-start(f32[2,8,1152]{2,1,0:T(8,128)S(1)} %get-tuple-element.17), channel_id=1, source_target_pairs={{0,13},{1,12},{2,15},{3,14},{4,9},{5,8},{6,11},{7,10},{8,5},{9,4},... | collective-permute-start | bytes 221192 | tf_op jit(solution)/shard_map/ppermute | solution.py:432
  8.7 0.9 %copy-start.5 = (f32[16,1152]{1,0:T(8,128)S(1)}, f32[16,1152]{1,0:T(8,128)}, u32[]{:S(2)}) copy-start(f32[16,1152]{1,0:T(8,128)} %refs_6_.1) | copy-start | bytes 221188
  13.1 15.7 %copy-start.6 = (f32[2,4,1152]{2,1,0:T(4,128)}, f32[2,4,1152]{2,1,0:T(4,128)S(1)}, u32[]{:S(2)}) copy-start(f32[2,4,1152]{2,1,0:T(4,128)S(1)} %get-tuple-element.27.own_ref) | copy-start | bytes 110596
  13.2 15.6 %collective-permute-start.3 = (f32[4,8,1152]{2,1,0:T(8,128)S(1)}, f32[4,8,1152]{2,1,0:T(8,128)S(1)}, u32[]{:S(2)}, u32[]{:S(2)}) collective-permute-start(f32[4,8,1152]{2,1,0:T(8,128)S(1)} %get-tuple-element.18), channel_id=1, source_target_pairs={{0,10},{1,11},{2,8},{3,9},{4,14},{5,15},{6,12},{7,13},{8,2},{9,3},... | collective-permute-start | bytes 442376 | tf_op jit(solution)/shard_map/ppermute | solution.py:432
  13.2 8.9 %collective-permute-start.10 = (f32[2,4,1152]{2,1,0:T(4,128)S(1)}, f32[2,4,1152]{2,1,0:T(4,128)S(1)}, u32[]{:S(2)}, u32[]{:S(2)}) collective-permute-start(f32[2,4,1152]{2,1,0:T(4,128)S(1)} %get-tuple-element.27.own_ref), channel_id=1, source_target_pairs={{1,2},{3,4},{5,6},{7,8},{9,10},{11,12},{13,14},{2,1},{4,3},{6,5},{... | collective-permute-start | bytes 110600 | tf_op jit(solution)/shard_map/ppermute | solution.py:331
  13.9 14.9 %collective-permute-start.9 = (f32[2,4,1152]{2,1,0:T(4,128)S(1)}, f32[2,4,1152]{2,1,0:T(4,128)S(1)}, u32[]{:S(2)}, u32[]{:S(2)}) collective-permute-start(f32[2,4,1152]{2,1,0:T(4,128)S(1)} %get-tuple-element.27.own_ref), channel_id=1, source_target_pairs={{0,1},{1,0},{2,3},{3,2},{4,5},{5,4},{6,7},{7,6},{8,9},{9,8},{10,11... | collective-permute-start | bytes 110600 | tf_op jit(solution)/shard_map/ppermute | solution.py:330
  18.3 12.6 %collective-permute-start.4 = (f32[4,8,1152]{2,1,0:T(8,128)S(1)}, f32[4,8,1152]{2,1,0:T(8,128)S(1)}, u32[]{:S(2)}, u32[]{:S(2)}) collective-permute-start(f32[4,8,1152]{2,1,0:T(8,128)S(1)} %get-tuple-element.19), channel_id=1, source_target_pairs={{0,14},{1,15},{2,12},{3,13},{4,10},{5,11},{6,8},{7,9},{8,6},{9,7},... | collective-permute-start | bytes 442376 | tf_op jit(solution)/shard_map/ppermute | solution.py:432
  19.7 11.6 %collective-permute-start.5 = (f32[4,8,1152]{2,1,0:T(8,128)S(1)}, f32[4,8,1152]{2,1,0:T(8,128)S(1)}, u32[]{:S(2)}, u32[]{:S(2)}) collective-permute-start(f32[4,8,1152]{2,1,0:T(8,128)S(1)} %get-tuple-element.20), channel_id=1, source_target_pairs={{0,6},{1,7},{2,4},{3,5},{4,2},{5,3},{6,0},{7,1},{8,14},{9,15},{10,... | collective-permute-start | bytes 442376 | tf_op jit(solution)/shard_map/ppermute | solution.py:432
  22.1 6.7 %copy-start.10 = (f32[2,4,1152]{2,1,0:T(4,128)}, f32[2,4,1152]{2,1,0:T(4,128)S(1)}, u32[]{:S(2)}) copy-start(f32[2,4,1152]{2,1,0:T(4,128)S(1)} %collective-permute-done.10.refs_1_) | copy-start | bytes 110596
  22.1 14.7 %collective-permute-start.6 = (f32[4,8,1152]{2,1,0:T(8,128)S(1)}, f32[4,8,1152]{2,1,0:T(8,128)S(1)}, u32[]{:S(2)}, u32[]{:S(2)}) collective-permute-start(f32[4,8,1152]{2,1,0:T(8,128)S(1)} %get-tuple-element.21), channel_id=1, source_target_pairs={{0,8},{1,9},{2,10},{3,11},{4,12},{5,13},{6,14},{7,15},{8,0},{9,1},... | collective-permute-start | bytes 442376 | tf_op jit(solution)/shard_map/ppermute | solution.py:432
  28.7 0.6 %copy-start.11 = (f32[2,4,1152]{2,1,0:T(4,128)}, f32[2,4,1152]{2,1,0:T(4,128)S(1)}, u32[]{:S(2)}) copy-start(f32[2,4,1152]{2,1,0:T(4,128)S(1)} %collective-permute-done.9.refs_0_) | copy-start | bytes 110596
  28.7 8.0 %collective-permute-start.7 = (f32[4,8,1152]{2,1,0:T(8,128)S(1)}, f32[4,8,1152]{2,1,0:T(8,128)S(1)}, u32[]{:S(2)}, u32[]{:S(2)}) collective-permute-start(f32[4,8,1152]{2,1,0:T(8,128)S(1)} %get-tuple-element.22), channel_id=1, source_target_pairs={{0,2},{1,3},{2,0},{3,1},{4,6},{5,7},{6,4},{7,5},{8,10},{9,11},{10,... | collective-permute-start | bytes 442376 | tf_op jit(solution)/shard_map/ppermute | solution.py:432
  28.8 8.5 %collective-permute-start.8 = (f32[4,8,1152]{2,1,0:T(8,128)S(1)}, f32[4,8,1152]{2,1,0:T(8,128)S(1)}, u32[]{:S(2)}, u32[]{:S(2)}) collective-permute-start(f32[4,8,1152]{2,1,0:T(8,128)S(1)} %get-tuple-element.23), channel_id=1, source_target_pairs={{0,4},{1,5},{2,6},{3,7},{4,0},{5,1},{6,2},{7,3},{8,12},{9,13},{10,... | collective-permute-start | bytes 442376 | tf_op jit(solution)/shard_map/ppermute | solution.py:432
  37.2 0.9 %copy-start.2 = (f32[6,4,1152]{2,1,0:T(4,128)S(1)}, f32[6,4,1152]{2,1,0:T(4,128)}, u32[]{:S(2)}) copy-start(f32[6,4,1152]{2,1,0:T(4,128)} %ocean.1.refs_9_) | copy-start | bytes 331780

commit v4 on v3

v4 whole, which is shorter than its diff:
```python
import functools

import jax
import jax.numpy as jnp
import numpy as np
from jax import lax
from jax.experimental import pallas as pl
from jax.experimental.layout import Layout, with_layout_constraint
from jax.experimental.pallas import tpu as pltpu
from jax.sharding import PartitionSpec as P

COSCUT = 0.5
LANES = 128
SUBLANES = 8
STEPS = ((4, 4), (7, 7), (3, 3), (5, 5), (1, 1), (6, 6), (2, 2))
RAW_STEPS = 1
RAW_TIE = 2
HALO_STEP = 9
HALO_SWAP = 0
SWAPS = ((0, 1, 2, 7), (3, 4, 5, 6))
F32 = jnp.float32
BF16 = jnp.bfloat16
NORMAL = (((1,), (0,)), ((), ()))
TRANSPOSED = (((1,), (1,)), ((), ()))
VMEM_LIMIT = 32 << 20
SMALL_LIMIT = 8 << 20


def halves(values):
    high = values.astype(BF16)
    return high, (values - high.astype(F32)).astype(BF16)


def split_product(left, right, dims=NORMAL):
    dot = functools.partial(lax.dot_general, dimension_numbers=dims, preferred_element_type=F32)
    return dot(left[0], right[0]) + (dot(left[0], right[1]) + dot(left[1], right[0]))


def np_halves(values):
    values = np.asarray(values, np.float32)
    high = values.astype(jnp.bfloat16)
    return np.stack([high, (values - high.astype(np.float32)).astype(jnp.bfloat16)])


def transform_tables(lon_count, lat_count):
    radix = lon_count // LANES
    steps = radix // 2
    b = np.arange(LANES)[:, None]
    k2 = np.arange(LANES)[None, :]
    table = np.zeros((steps * 2 * LANES + LANES, 2 * LANES))
    for k in range(1, steps + 1):
        angle = 2 * np.pi * ((b * (k + radix * k2)) % lon_count) / lon_count
        c, s = np.cos(angle), np.sin(angle)
        table[(k - 1) * 2 * LANES : k * 2 * LANES] = np.block([[c, -s], [s, c]])
    half = LANES // 2
    angle = 2 * np.pi * ((b * k2) % LANES) / LANES
    table[steps * 2 * LANES :, :LANES] = np.concatenate(
        [np.cos(angle[:, : half + 1]), np.sin(angle[:, 1:half])], axis=1
    )
    wave = np.zeros((steps + 1, 2 * LANES))
    scale = np.full((steps + 1, 2 * LANES), 2.0 / lon_count)
    wave[0, :LANES] = np.concatenate([np.arange(half + 1), np.arange(1, half)]) * radix
    scale[0, [0, half]] = 1.0 / lon_count
    for k in range(1, steps + 1):
        wave[k] = np.tile(k + radix * np.arange(LANES), 2)
    limit = COSCUT**2 * np.sin(np.pi * wave / lon_count) ** 2
    latitude = np.pi * ((np.arange(lat_count) + 0.5) / lat_count - 0.5)
    square = np.repeat(np.cos(latitude)[:, None] ** 2, 2 * LANES, axis=1)
    rows = np.concatenate([limit, scale, square])
    rows = np.pad(rows, ((0, -len(rows) % SUBLANES), (0, 0)))
    return np_halves(table), rows.astype(np.float32)


def filtered(fields, squares, table_ref, row_ref):
    radix = fields.shape[1] // LANES
    half = radix // 2
    height = fields.shape[0] // len(squares)
    parts = [fields[:, a * LANES : (a + 1) * LANES] for a in range(radix)]
    sums = [parts[a] + parts[radix - a] for a in range(1, half + 1)]
    gaps = [parts[a] - parts[radix - a] for a in range(1, half + 1)]

    def pair(k):
        if k == 0:
            rows, width = slice(half * 2 * LANES, half * 2 * LANES + LANES), LANES
        else:
            rows, width = slice((k - 1) * 2 * LANES, k * 2 * LANES), 2 * LANES
        return table_ref[0, rows, :width], table_ref[1, rows, :width]

    def gain(k, width):
        limit = row_ref[k : k + 1, :LANES]
        scale = row_ref[half + 1 + k : half + 2 + k, :LANES]
        groups = [
            jnp.broadcast_to(square / jnp.maximum(square, limit) * scale, (height, LANES))
            for square in squares
        ]
        groups = jnp.concatenate(groups, axis=0)
        return groups if width == LANES else jnp.concatenate([groups, groups], axis=1)

    total = parts[0]
    for value in sums:
        total = total + value
    spectrum = split_product(halves(total), pair(0)) * gain(0, LANES)
    base = split_product(halves(spectrum), pair(0), TRANSPOSED)
    cosines, sines = [], []
    for k in range(1, half + 1):
        real, imag = parts[0], None
        for a in range(1, half + 1):
            angle = 2 * np.pi * (a * k % radix) / radix
            real = real + float(np.cos(angle)) * sums[a - 1]
            term = float(-np.sin(angle)) * gaps[a - 1]
            imag = term if imag is None else imag + term
        both = jnp.concatenate([real, imag], axis=1)
        spectrum = split_product(halves(both), pair(k)) * gain(k, 2 * LANES)
        series = split_product(halves(spectrum), pair(k), TRANSPOSED)
        cosines.append(series[:, :LANES])
        sines.append(series[:, LANES:])
    whole = base
    for value in cosines:
        whole = whole + value
    lower, upper = [], []
    for a in range(1, half + 1):
        even, odd = base, None
        for k in range(1, half + 1):
            angle = 2 * np.pi * (a * k % radix) / radix
            even = even + float(np.cos(angle)) * cosines[k - 1]
            term = float(np.sin(angle)) * sines[k - 1]
            odd = term if odd is None else odd + term
        lower.append(even - odd)
        upper.append(even + odd)
    return jnp.concatenate([whole] + lower + upper[::-1], axis=1)


def filter_blocks(rows, out_refs, mask_ref, table_ref, row_ref):
    part = out_refs[0].shape[1]
    height = len(out_refs) * part
    radix = out_refs[0].shape[2] // LANES
    first_square = 2 * (radix // 2 + 1)
    active = [mask_ref[row] == 1 for row in rows]

    @pl.when(functools.reduce(jnp.logical_or, active))
    def _():
        fields = jnp.concatenate([ref[r] for r in range(len(rows)) for ref in out_refs], axis=0)
        squares = [row_ref[pl.ds(first_square + row, 1), :][:, :LANES] for row in rows]
        smooth = filtered(fields, squares, table_ref, row_ref)
        for r in range(len(rows)):

            @pl.when(active[r])
            def _():
                for i, ref in enumerate(out_refs):
                    start = r * height + i * part
                    ref[r] = smooth[start : start + part]


def step_mask(chip, step):
    first, second = STEPS[step] if step < len(STEPS) else (0, 0)
    if first == second:
        return first
    if isinstance(chip, int):
        return first if (chip >> 2 ^ chip >> 1) & 1 else second
    return jnp.where(lax.rem(chip // 4 + chip // 2, 2) == 1, first, second)


def field_rows(ref, start, count, r, rows, radix):
    step = rows * radix
    return jnp.concatenate(
        [ref[pl.ds(start * step + t * rows + r, count, stride=step), :] for t in range(radix)], axis=1
    )


def spread(values, groups, width, count):
    lane = lax.broadcasted_iota(jnp.int32, (width, width * count), 1)
    repeat = (lax.rem(lane, width) == lax.broadcasted_iota(jnp.int32, lane.shape, 0)).astype(BF16)
    lane_group = lax.broadcasted_iota(jnp.int32, (1, width * count), 1) // width
    keep = jnp.concatenate(
        [
            jnp.broadcast_to((lane_group == group).astype(F32), (height, width * count))
            for group, height in groups
        ],
        axis=0,
    )
    return [
        (jnp.dot(value, repeat, preferred_element_type=F32) * keep).astype(BF16) for value in halves(values)
    ]


def mix_kernel(rows, split, first, steps, *refs):
    outs = steps + split if split > 1 else steps
    inputs, refs = refs[:8], refs[8:]
    out_refs, flux_ref, refs = refs[:outs], refs[outs], refs[outs + 1 :]
    (load, mix_ref, mask_ref, coupling_ref, fractions_ref, index_ref, table_ref, row_ref, sems) = refs
    copies = [
        pltpu.make_async_copy(source, target, sems.at[i])
        for i, (source, target) in enumerate(zip(inputs, refs[:-1]))
    ]
    for copy in copies:
        copy.start()
    fields, levels, _ = mix_ref.shape
    part = levels // split
    lon = flux_ref.shape[2]
    radix = lon // LANES
    me = lax.axis_index("lat")
    core = lax.rem(me, split)
    blocks = list(out_refs)
    if split > 1:
        blocks = [ref.at[c] for ref in out_refs[:steps] for c in range(split)] + blocks[steps:]
    chosen, weights = [], []
    copies[1].wait()
    for step in range(first, fields):
        field = jnp.bitwise_xor(me // split, step_mask(me // split, step)) if split > 1 else step
        for c in range(split):
            start = pl.multiple_of(jnp.bitwise_xor(core, c) * part, part) if split > 1 else 0
            weights.append(mix_ref[field, pl.ds(start, part), :])
            chosen.append((field, part))
    weights += [mix_ref[f, levels - 1 : levels, :] for f in range(fields)]
    chosen += [(f, 1) for f in range(fields)]
    left = spread(jnp.concatenate(weights, axis=0), chosen, levels, fields)
    copies[0].wait()
    bottoms = []
    for r in range(rows):
        mixed = split_product(left, halves(field_rows(load, 0, fields * levels, r, rows, radix)))
        for j, ref in enumerate(blocks):
            ref[r] = mixed[j * part : (j + 1) * part]
        bottoms.append(mixed[len(blocks) * part :])
    for copy in copies[2:]:
        copy.wait()
    for r, bottom in enumerate(bottoms):
        speed = jnp.sqrt(bottom[0:1] * bottom[0:1] + bottom[1:2] * bottom[1:2] + 1.0)
        flux = split_product(halves(coupling_ref[...]), halves(bottom))
        flux_ref[r] = speed * flux * fractions_ref[pl.ds(index_ref[r], 1), :]
    filter_blocks([me * rows + r for r in range(rows)], blocks, mask_ref, table_ref, row_ref)


def mixed_blocks(
    view, vertical_mix, polar_mask, coupling, fractions, weight_index, tables, lon, rows, split, first, steps
):
    part = vertical_mix.shape[1] // split
    arrays = (view, vertical_mix, polar_mask, coupling, fractions, weight_index) + tuple(
        jnp.asarray(table) for table in tables
    )
    operands = [pltpu.with_memory_space_constraint(value, pltpu.HBM) for value in arrays]
    spaces = [pltpu.SMEM if value.dtype == jnp.int32 else pltpu.VMEM for value in arrays]
    block = (rows, part, lon)
    outs = [pltpu.VMEM((split,) + block if split > 1 else block, F32)] * steps
    outs += [pltpu.VMEM(block, F32)] * (split if split > 1 else 0)
    outs += [pltpu.VMEM((rows, coupling.shape[0], lon), F32)]
    return pl.pallas_call(
        functools.partial(mix_kernel, rows, split, first, steps),
        out_shape=outs,
        in_specs=[pl.BlockSpec(memory_space=pltpu.HBM)] * len(operands),
        out_specs=[pl.BlockSpec(memory_space=pltpu.VMEM)] * len(outs),
        scratch_shapes=[space(value.shape, value.dtype) for space, value in zip(spaces, arrays)]
        + [pltpu.SemaphoreType.DMA((len(arrays),))],
        compiler_params=pltpu.CompilerParams(vmem_limit_bytes=VMEM_LIMIT),
        name="mixed_blocks",
    )(*operands)


def pick_kernel(split, steps, view_ref, *refs):
    out_refs, sems = refs[:-1], refs[-1]
    span = out_refs[0].shape[0]
    chip = lax.axis_index("lat") // split
    copies = []
    for i, step in enumerate(steps):
        start = pl.multiple_of(jnp.bitwise_xor(chip, step_mask(chip, step)) * span, span)
        copies.append(pltpu.make_async_copy(view_ref.at[pl.ds(start, span)], out_refs[i], sems.at[i]))
        copies[-1].start()
    for copy in copies:
        copy.wait()


def raw_fields(view, field_count, split, steps):
    shape = (view.shape[0] // field_count, LANES)
    return pl.pallas_call(
        functools.partial(pick_kernel, split, steps),
        out_shape=[pltpu.VMEM(shape, F32)] * len(steps),
        in_specs=[pl.BlockSpec(memory_space=pltpu.HBM)],
        out_specs=[pl.BlockSpec(memory_space=pltpu.VMEM)] * len(steps),
        scratch_shapes=[pltpu.SemaphoreType.DMA((len(steps),))],
        compiler_params=pltpu.CompilerParams(vmem_limit_bytes=SMALL_LIMIT),
        name="raw_fields",
    )(pltpu.with_memory_space_constraint(view, pltpu.HBM))


def arrived_kernel(rows, split, step, raw_ref, mix_ref, mask_ref, table_ref, row_ref, out_ref):
    levels = mix_ref.shape[1]
    part = levels // split
    radix = out_ref.shape[3] // LANES
    me = lax.axis_index("lat")
    chip = me // split
    core = lax.rem(me, split)
    starts = [pl.multiple_of(jnp.bitwise_xor(core, c) * part, part) for c in range(split)]
    left = halves(jnp.concatenate([mix_ref[chip, pl.ds(start, part), :] for start in starts], axis=0))
    blocks = [out_ref.at[c] for c in range(split)]
    for r in range(rows):
        mixed = split_product(left, halves(field_rows(raw_ref, 0, levels, r, rows, radix)))
        for c in range(split):
            blocks[c][r] = mixed[c * part : (c + 1) * part]
    source = jnp.bitwise_xor(chip, step_mask(chip, step)) * split + core
    filter_blocks([source * rows + r for r in range(rows)], blocks, mask_ref, table_ref, row_ref)


def arrived_blocks(raw, vertical_mix, polar_mask, tables, lon, rows, split, step):
    vmem = pl.BlockSpec(memory_space=pltpu.VMEM)
    return pl.pallas_call(
        functools.partial(arrived_kernel, rows, split, step),
        out_shape=pltpu.VMEM((split, rows, vertical_mix.shape[1] // split, lon), F32),
        in_specs=[vmem, vmem, pl.BlockSpec(memory_space=pltpu.SMEM), vmem, vmem],
        out_specs=vmem,
        compiler_params=pltpu.CompilerParams(vmem_limit_bytes=VMEM_LIMIT),
        name="arrived_blocks",
    )(raw, vertical_mix, polar_mask, *tables)


def collect_kernel(*refs):
    out_ref = refs[-1]
    for i, ref in enumerate(refs[:-1]):
        out_ref[i] = ref[1] if len(ref.shape) == len(out_ref.shape) else ref[...]


def collect(blocks):
    vmem = pl.BlockSpec(memory_space=pltpu.VMEM)
    return pl.pallas_call(
        collect_kernel,
        out_shape=pltpu.VMEM((len(blocks),) + blocks[0].shape[1:], F32),
        in_specs=[vmem] * len(blocks),
        out_specs=vmem,
        compiler_params=pltpu.CompilerParams(vmem_limit_bytes=SMALL_LIMIT),
        name="collect",
    )(*blocks)


def ocean_kernel(lat_count, split, bounds_ref, own_ref, *refs):
    near_refs, out_ref = refs[:-1], refs[-1]
    rows = own_ref.shape[0]
    slots = out_ref.shape[0]
    half = rows // 2
    me = lax.axis_index("lat")
    start = bounds_ref[me] - half
    length = bounds_ref[me + 1] - bounds_ref[me] + 2 * half + 1
    shift = start - (me - 1) * rows
    first, last = ([ref[r] for r in range(rows)] for ref in near_refs)
    if split > 1:
        upper = lax.rem(me, split) == 0
        first, last = (
            [jnp.where(upper, outer, other) for outer, other in zip(last, first)],
            [jnp.where(upper, other, outer) for outer, other in zip(last, first)],
        )
    near = first + [own_ref[r] for r in range(rows)] + last
    for s in range(slots):
        row = start + s
        valid = (s < length) & (row >= 0) & (row < lat_count)
        picked = jnp.zeros_like(near[0])
        for p, value in enumerate(near):
            picked = jnp.where(valid & (shift + s == p), value, picked)
        out_ref[s] = picked


def neighbour_rows(weighted, device_count, split):
    ends = device_count - 1
    if split == 2:
        pairs = [(i, i + 1) for i in range(1, ends, 2)]
        return [
            lax.ppermute(weighted, "lat", [(i, i ^ 1) for i in range(device_count)]),
            lax.ppermute(weighted, "lat", pairs + [(j, i) for i, j in pairs]),
        ]
    return [
        lax.ppermute(weighted, "lat", [(i, i + 1) for i in range(ends)]),
        lax.ppermute(weighted, "lat", [(i + 1, i) for i in range(ends)]),
    ]


def ocean_slots(weighted, near, band_bounds, lat_count, split):
    rows, flux_count, lon = weighted.shape
    vmem = pl.BlockSpec(memory_space=pltpu.VMEM)
    return pl.pallas_call(
        functools.partial(ocean_kernel, lat_count, split),
        out_shape=jax.ShapeDtypeStruct((3 * rows, flux_count, lon), F32),
        in_specs=[pl.BlockSpec(memory_space=pltpu.SMEM)] + [vmem] * 3,
        out_specs=vmem,
        compiler_params=pltpu.CompilerParams(vmem_limit_bytes=SMALL_LIMIT),
        name="ocean",
    )(band_bounds, weighted, *near)


def place_kernel(split, sources, *refs):
    out_ref, buffer, sems = refs[-3:]
    part, lon = refs[0].shape[-2:]
    rows = refs[0].shape[-3]
    radix = lon // LANES
    chip_rows = rows * split
    tile = radix * SUBLANES
    span = out_ref.shape[0] // part
    me = lax.axis_index("lat")
    chip = me // split
    core = lax.rem(me, split)
    groups = chip_rows * len(sources) // SUBLANES
    chips = len(sources) // groups
    step_groups = [{first // chips, second // chips} for first, second in STEPS] + [{0}]
    pending = {group: sum(group in held for held in step_groups) for group in range(groups)}
    copies = []
    for step in [len(STEPS)] + list(range(len(STEPS))):
        source = jnp.bitwise_xor(chip, step_mask(chip, step))
        base = source // chips * (part * tile) + lax.rem(source, chips) * chip_rows
        for c, (operand, index) in enumerate(sources[step]):
            ref = refs[operand] if index is None else refs[operand].at[index]
            for r in range(rows):
                row = base + jnp.bitwise_xor(core, c) * rows + r
                for t in range(radix):
                    buffer[pl.ds(row + t * SUBLANES, part, stride=tile), :] = ref[
                        r, :, t * LANES : (t + 1) * LANES
                    ]
        for group in step_groups[step]:
            pending[group] -= 1
            if pending[group]:
                continue
            place = jnp.bitwise_xor(chip // chips, group)
            for f in range(part):
                copy = pltpu.make_async_copy(
                    buffer.at[pl.ds(pl.multiple_of((place * part + f) * tile, SUBLANES), tile)],
                    out_ref.at[pl.ds(pl.multiple_of(f * span + place * tile, SUBLANES), tile)],
                    sems.at[group, f],
                )
                copy.start()
                copies.append(copy)
    for copy in copies:
        copy.wait()


def place(operands, sources, lat_count, after):
    part, lon = operands[0].shape[-2:]
    size = part * lat_count * lon // LANES
    groups = lat_count // SUBLANES
    vmem = pl.BlockSpec(memory_space=pltpu.VMEM)
    out = pl.pallas_call(
        functools.partial(place_kernel, len(sources[0]), sources),
        out_shape=jax.ShapeDtypeStruct((size, LANES), F32),
        in_specs=[vmem] * len(operands) + [pl.BlockSpec(memory_space=pl.ANY)],
        out_specs=pl.BlockSpec(memory_space=pltpu.HBM),
        scratch_shapes=[pltpu.VMEM((size, LANES), F32), pltpu.SemaphoreType.DMA((groups, part))],
        compiler_params=pltpu.CompilerParams(vmem_limit_bytes=VMEM_LIMIT),
        name="place",
    )(*operands, pltpu.with_memory_space_constraint(after, pltpu.HBM))
    tiles = out.reshape(part, groups, lon // LANES, SUBLANES, LANES)
    return tiles.transpose(0, 1, 3, 2, 4).reshape(part, lat_count, lon)


def body(device_count, state, vertical_mix, coupling, fractions, weight_index, band_bounds, polar_mask):
    field_count, level_count = vertical_mix.shape[:2]
    stack_count, row_count, lon_count = state.shape
    lat_count = polar_mask.shape[0]
    part = stack_count // device_count
    tables = transform_tables(lon_count, lat_count)
    radix = lon_count // LANES
    blocked = with_layout_constraint(
        state.reshape(stack_count, row_count, radix, LANES), Layout(major_to_minor=(0, 2, 1, 3))
    )
    view = blocked.transpose(0, 2, 1, 3).reshape(-1, LANES)
    mixed = functools.partial(
        mixed_blocks,
        view,
        vertical_mix,
        polar_mask,
        coupling,
        fractions,
        weight_index,
        tables,
        lon_count,
        row_count,
    )

    if part == SUBLANES and level_count == 2 * part and field_count == len(STEPS) + 1:
        split = 2
        raw = raw_fields(view, field_count, split, tuple(range(RAW_STEPS)))
        *blocks, near, far, weighted = mixed(split, RAW_STEPS, len(STEPS) - RAW_STEPS)
        neighbours = neighbour_rows(weighted, device_count, split)
        blocks = list(raw) + blocks
        for step, block in enumerate(blocks):
            if step == HALO_STEP:
                block, *neighbours = lax.optimization_barrier((block, *neighbours))
            if step == RAW_TIE:
                block, *blocks[:RAW_STEPS] = lax.optimization_barrier((block, *blocks[:RAW_STEPS]))
            pairs = [(i, i ^ split * step_mask(i // split, step)) for i in range(device_count)]
            blocks[step] = lax.ppermute(block, "lat", pairs)
        for step in range(RAW_STEPS):
            blocks[step] = arrived_blocks(
                blocks[step], vertical_mix, polar_mask, tables, lon_count, row_count, split, step
            )
        operands = blocks + [near]
        sources = [[(step, 0)] for step in range(len(STEPS))] + [[(len(STEPS), None)]]
        for number, group in enumerate(SWAPS):
            if number == HALO_SWAP:
                last = max(step for step in group if step < len(STEPS))
                blocks[last], *neighbours = lax.optimization_barrier((blocks[last], *neighbours))
            held = collect([(blocks + [far])[step] for step in group])
            for i, step in enumerate(group):
                sources[step].append((len(operands), i))
            operands.append(lax.ppermute(held, "lat", [(i, i ^ 1) for i in range(device_count)]))
        ocean = ocean_slots(weighted, neighbours, band_bounds, lat_count, split)
        state_out = place(operands, sources, lat_count, ocean)
    else:
        *blocks, weighted = mixed(1, 0, field_count)
        stacked = jnp.concatenate(blocks, axis=1)
        moved = lax.all_to_all(stacked, "lat", split_axis=1, concat_axis=0, tiled=True)
        state_out = jnp.transpose(moved, (1, 0, 2))
        neighbours = neighbour_rows(weighted, device_count, 1)
        ocean = ocean_slots(weighted, neighbours, band_bounds, lat_count, 1)
    return (state_out, jnp.transpose(ocean, (1, 0, 2)))


def solution(mesh):
    return jax.shard_map(
        functools.partial(body, mesh.shape["lat"]),
        mesh=mesh,
        in_specs=(P("member", "lat", None), P(), P(), P(), P(("member", "lat")), P(), P()),
        out_specs=(P(("member", "lat"), None, None), P(None, ("member", "lat"), None)),
        check_vma=False,
    )
```

time: 39.7 us -> 35.4 us (0.89)
  waiting for transfers between devices: 6.42 us -> 3.4 us
  local copies, waits for them, and re-layouts: 2.33 us -> 0.03 us
  starting transfers between devices: 20.8 us -> 22.3 us
  Pallas kernels: 9.08 us -> 8.53 us
    ppermute x11, waiting for transfers between devices: 6.42 us -> 3.4 us  [the longest x7 3.3 us: body(): blocks[step] = lax.ppermute(block, 'lat', pairs)]
    unnamed x24 -> x10, local copies, waits for them, and re-layouts: 2.33 us -> 0.03 us
    ppermute x11, starting transfers between devices: 20.8 us -> 22.3 us  [the longest x7 18.3 us: body(): blocks[step] = lax.ppermute(block, 'lat', pairs)]
    pallas_call x3 -> x6, Pallas kernels: 7.55 us -> 7.27 us  [the longest x1 4.05 us: mixed_blocks(): pl.pallas_call(functools.partial(mix_kernel, rows, split, first, steps),...]
  transfers between devices with their start and end apart: 11 -> 11, of which waited for: 4 -> 3; matrix products, arithmetic and copies ran while one was open for 0% -> 0% of each run, Pallas kernels for 20% -> 17%
where the time goes in v4:
time: 35.4 us; the launch traced here: 35 us
  starting transfers between devices  22.3 us (63%)
  Pallas kernels  8.53 us (24%)
  waiting for transfers between devices  3.4 us (10%)
  between operations  0.75 us (2%)
    ppermute x7, starting transfers between devices, body(): blocks[step] = lax.ppermute(block, 'lat', pairs)  18.3 us
    pallas_call x1, Pallas kernels, mixed_blocks(): pl.pallas_call(functools.partial(mix_kernel, rows, split, first, steps),...  4.05 us
    ppermute x7, waiting for transfers between devices, body(): blocks[step] = lax.ppermute(block, 'lat', pairs)  3.3 us
    ppermute x1, starting transfers between devices, neighbour_rows(): lax.ppermute(weighted, 'lat', [(i, i ^ 1) for i in range(device_count)])  2.95 us
    pallas_call x1, Pallas kernels, place(): pl.pallas_call(functools.partial(place_kernel, len(sources[0]), sources),...  1.5 us
    pallas_call x1, Pallas kernels, ocean_slots(): pl.pallas_call(functools.partial(ocean_kernel, lat_count, split), out_sha...  1.25 us
    pallas_call x1, Pallas kernels, raw_fields(): pl.pallas_call(functools.partial(pick_kernel, split, steps), out_shape=[p...  0.93 us
    pallas_call x1, Pallas kernels, arrived_blocks(): pl.pallas_call(functools.partial(arrived_kernel, rows, split, step), out_...  0.75 us
  transfers between devices with their start and end apart: 11, of which 3 were waited for; matrix products, arithmetic and copies ran while one was open for 0% of the time, Pallas kernels for 17%

profile of v4, /device:TPU:0, one launch (start us, length us, event | category | flops | bytes accessed | tf_op | source)
XLA Modules:
  0.0 35.0 jit_solution(6918998787674839074)
XLA Ops:
  0.6 0.9 %raw_fields.1 = f32[288,128]{1,0:T(8,128)S(1)} custom-call(f32[2304,128]{1,0:T(8,128)} %bitcast.11), custom_call_target="tpu_custom_call" | custom-call | tf_op jit(solution)/shard_map/raw_fields/pallas_call | solution.py:273
  1.6 0.0 copy-start
  1.6 0.0 copy-start.1
  1.6 0.0 copy-start.2
  1.6 0.0 copy-start.3
  1.6 4.1 %collective-permute-start = (f32[288,128]{1,0:T(8,128)S(1)}, f32[288,128]{1,0:T(8,128)S(1)}, u32[]{:S(2)}, u32[]{:S(2)}) collective-permute-start(f32[288,128]{1,0:T(8,128)S(1)} %raw_fields.1), channel_id=1, source_target_pairs={{0,8},{1,9},{2,10},{3,11},{4,12},{5,13},{6,14},{7,15},{8,0},{9,1},... | collective-permute-start | bytes 442376 | tf_op jit(solution)/shard_map/ppermute | solution.py:483
  5.7 4.0 %mixed_blocks.1 = (f32[2,2,8,1152]{3,2,1,0:T(8,128)S(1)}, f32[2,2,8,1152]{3,2,1,0:T(8,128)S(1)}, f32[2,2,8,1152]{3,2,1,0:T(8,128)S(1)}, f32[2,2,8,1152]{3,2,1,0:...) custom-call(f32[2304,128]{1,0:T(8,128)} %bitcast.12, ...), custom_call_target="tpu_custom_call" | custom-call | tf_op jit(solution)/shard_map/mixed_blocks/pallas_call | solution.py:246
  9.8 0.1 collective-permute-start.3
  9.9 1.6 %collective-permute-start.4 = (f32[2,2,8,1152]{3,2,1,0:T(8,128)S(1)}, f32[2,2,8,1152]{3,2,1,0:T(8,128)S(1)}, u32[]{:S(2)}, u32[]{:S(2)}) collective-permute-start(f32[2,2,8,1152]{3,2,1,0:T(8,128)S(1)} %get-tuple-element.21), channel_id=1, source_target_pairs={{0,2},{1,3},{2,0},{3,1},{4,6},{5,7},{6,4},{7,5},{8,10},{9,11},{10,... | collective-permute-start | bytes 442376 | tf_op jit(solution)/shard_map/ppermute | solution.py:483
  11.4 2.1 %collective-permute-start.5 = (f32[2,2,8,1152]{3,2,1,0:T(8,128)S(1)}, f32[2,2,8,1152]{3,2,1,0:T(8,128)S(1)}, u32[]{:S(2)}, u32[]{:S(2)}) collective-permute-start(f32[2,2,8,1152]{3,2,1,0:T(8,128)S(1)} %get-tuple-element.22), channel_id=1, source_target_pairs={{0,12},{1,13},{2,14},{3,15},{4,8},{5,9},{6,10},{7,11},{8,4},{9,5},... | collective-permute-start | bytes 442376 | tf_op jit(solution)/shard_map/ppermute | solution.py:483
  13.6 1.2 %collective-permute-start.6 = (f32[2,2,8,1152]{3,2,1,0:T(8,128)S(1)}, f32[2,2,8,1152]{3,2,1,0:T(8,128)S(1)}, u32[]{:S(2)}, u32[]{:S(2)}) collective-permute-start(f32[2,2,8,1152]{3,2,1,0:T(8,128)S(1)} %get-tuple-element.23), channel_id=1, source_target_pairs={{0,4},{1,5},{2,6},{3,7},{4,0},{5,1},{6,2},{7,3},{8,12},{9,13},{10,... | collective-permute-start | bytes 442376 | tf_op jit(solution)/shard_map/ppermute | solution.py:483
  14.8 6.1 %collective-permute-start.2 = (f32[2,2,8,1152]{3,2,1,0:T(8,128)S(1)}, f32[2,2,8,1152]{3,2,1,0:T(8,128)S(1)}, u32[]{:S(2)}, u32[]{:S(2)}) collective-permute-start(f32[2,2,8,1152]{3,2,1,0:T(8,128)S(1)} %get-tuple-element.19), channel_id=1, source_target_pairs={{0,6},{1,7},{2,4},{3,5},{4,2},{5,3},{6,0},{7,1},{8,14},{9,15},{10,... | collective-permute-start | bytes 442376 | tf_op jit(solution)/shard_map/ppermute | solution.py:483
  20.9 2.8 %collective-permute-done.3.refs_0_.refs_3_ = f32[2,2,8,1152]{3,2,1,0:T(8,128)S(1)} collective-permute-done((f32[2,2,8,1152]{3,2,1,0:T(8,128)S(1)}, f32[2,2,8,1152]{3,2,1,0:T(8,128)S(1)}, u32[]{:S(2)}, u32[]{:S(2)}) %collective-permute-start.3) | collective-permute-done | bytes 147488 | tf_op jit(solution)/shard_map/ppermute | solution.py:483
  23.7 3.1 %collective-permute-start.1 = (f32[2,2,8,1152]{3,2,1,0:T(8,128)S(1)}, f32[2,2,8,1152]{3,2,1,0:T(8,128)S(1)}, u32[]{:S(2)}, u32[]{:S(2)}) collective-permute-start(f32[2,2,8,1152]{3,2,1,0:T(8,128)S(1)} %get-tuple-element.18), channel_id=1, source_target_pairs={{0,14},{1,15},{2,12},{3,13},{4,10},{5,11},{6,8},{7,9},{8,6},{9,7},... | collective-permute-start | bytes 442376 | tf_op jit(solution)/shard_map/ppermute | solution.py:483
  26.8 0.7 %collective-permute-start.8 = (f32[2,4,1152]{2,1,0:T(4,128)S(1)}, f32[2,4,1152]{2,1,0:T(4,128)S(1)}, u32[]{:S(2)}, u32[]{:S(2)}) collective-permute-start(f32[2,4,1152]{2,1,0:T(4,128)S(1)} %get-tuple-element.25.own_ref), channel_id=1, source_target_pairs={{1,2},{3,4},{5,6},{7,8},{9,10},{11,12},{13,14},{2,1},{4,3},{6,5},{... | collective-permute-start | bytes 110600 | tf_op jit(solution)/shard_map/ppermute | solution.py:364
  27.5 2.9 %collective-permute-start.7 = (f32[2,4,1152]{2,1,0:T(4,128)S(1)}, f32[2,4,1152]{2,1,0:T(4,128)S(1)}, u32[]{:S(2)}, u32[]{:S(2)}) collective-permute-start(f32[2,4,1152]{2,1,0:T(4,128)S(1)} %get-tuple-element.25.own_ref), channel_id=1, source_target_pairs={{0,1},{1,0},{2,3},{3,2},{4,5},{5,4},{6,7},{7,6},{8,9},{9,8},{10,11... | collective-permute-start | bytes 110600 | tf_op jit(solution)/shard_map/ppermute | solution.py:363
  30.4 0.8 %arrived_blocks.1.refs_0_ = f32[2,2,8,1152]{3,2,1,0:T(8,128)S(1)} custom-call(f32[288,128]{1,0:T(8,128)S(1)} %collective-permute-done.raw_ref, f32[8,16,16]{2,1,0:T(8,128)S(1)} %copy-done.1, s32[32]{0:T(128)S(1)} %copy-done.3, bf16[2,1152,256]{2,1,0:T(8,128)(2,1)S(1)} %copy-done, f32[48,256]{1,0:T(8,128)S(1)} %copy-done.2), custom_call_target="tpu_custom_call" | custom-call | tf_op jit(solution)/shard_map/arrived_blocks/pallas_call | solution.py:304
  31.2 0.0 copy-start.4
  31.2 0.1 collective-permute-start.10
  31.3 0.4 %collective-permute-done.2.refs_2_ = f32[2,2,8,1152]{3,2,1,0:T(8,128)S(1)} collective-permute-done((f32[2,2,8,1152]{3,2,1,0:T(8,128)S(1)}, f32[2,2,8,1152]{3,2,1,0:T(8,128)S(1)}, u32[]{:S(2)}, u32[]{:S(2)}) %collective-permute-start.2) | collective-permute-done | bytes 147488 | tf_op jit(solution)/shard_map/ppermute | solution.py:483
  31.8 0.3 collective-permute-start.9
  32.1 1.3 %ocean.1.refs_10_ = f32[6,4,1152]{2,1,0:T(4,128)} custom-call(s32[17]{0:T(128)S(1)} %copy-done.4, f32[2,4,1152]{2,1,0:T(4,128)S(1)} %get-tuple-element.25.own_ref, f32[2,4,1152]{2,1,0:T(4,128)S(1)} %collective-permute-done.7.refs_0_, f32[2,4,1152]{2,1,0:T(4,128)S(1)} %collective-permute-done.8.refs_1_), custom_call_target="tpu_custom_call" | custom-call | tf_op jit(solution)/shard_map/ocean/pallas_call | solution.py:375
  33.4 0.1 collective-permute-done.9.refs_8_
  33.5 1.5 %place.1 = f32[2304,128]{1,0:T(8,128)} custom-call(f32[2,2,8,1152]{3,2,1,0:T(8,128)S(1)} %arrived_blocks.1.refs_0_, f32[2,2,8,1152]{3,2,1,0:T(8,128)S(1)} %collective-permute-done.1.refs_1_, f32[2,2,8,1152]{3,2,1,0:T(8,128)S(1)} %collective-permute-done.2.refs_2_, f32[2,2,8,1152]{3,2,1,0:T(8,128)S(1)} %collective-permute-done.3.refs_0_.refs_3_, ...), custom_call_target="tpu_custom_call" | custom-call | tf_op jit(solution)/shard_map/place/pallas_call | solution.py:434
  (15 shorter events, 0.1 us)
Async XLA Ops:
  1.6 28.8 %copy-start = (bf16[2,1152,256]{2,1,0:T(8,128)(2,1)S(1)}, bf16[2,1152,256]{2,1,0:T(8,128)(2,1)}, u32[]{:S(2)}) copy-start(bf16[2,1152,256]{2,1,0:T(8,128)(2,1)} %constant.4.clone.refs_6_.table_ref) | copy-start | bytes 3538948
  1.6 28.8 %copy-start.1 = (f32[8,16,16]{2,1,0:T(8,128)S(1)}, f32[8,16,16]{2,1,0:T(8,128)}, u32[]{:S(2)}) copy-start(f32[8,16,16]{2,1,0:T(8,128)} %mix_ref.1) | copy-start | bytes 24580
  1.6 28.8 %copy-start.2 = (f32[48,256]{1,0:T(8,128)S(1)}, f32[48,256]{1,0:T(8,128)}, u32[]{:S(2)}) copy-start(f32[48,256]{1,0:T(8,128)} %constant.5.clone.refs_7_.row_ref) | copy-start | bytes 147460
  1.6 28.8 %copy-start.3 = (s32[32]{0:T(128)S(1)}, s32[32]{0:T(128)}, u32[]{:S(2)}) copy-start(s32[32]{0:T(128)} %mask_ref.1) | copy-start | bytes 388
  1.6 13.2 %collective-permute-start = (f32[288,128]{1,0:T(8,128)S(1)}, f32[288,128]{1,0:T(8,128)S(1)}, u32[]{:S(2)}, u32[]{:S(2)}) collective-permute-start(f32[288,128]{1,0:T(8,128)S(1)} %raw_fields.1), channel_id=1, source_target_pairs={{0,8},{1,9},{2,10},{3,11},{4,12},{5,13},{6,14},{7,15},{8,0},{9,1},... | collective-permute-start | bytes 442376 | tf_op jit(solution)/shard_map/ppermute | solution.py:483
  9.8 13.9 %collective-permute-start.3 = (f32[2,2,8,1152]{3,2,1,0:T(8,128)S(1)}, f32[2,2,8,1152]{3,2,1,0:T(8,128)S(1)}, u32[]{:S(2)}, u32[]{:S(2)}) collective-permute-start(f32[2,2,8,1152]{3,2,1,0:T(8,128)S(1)} %get-tuple-element.20), channel_id=1, source_target_pairs={{0,10},{1,11},{2,8},{3,9},{4,14},{5,15},{6,12},{7,13},{8,2},{9,3},... | collective-permute-start | bytes 442376 | tf_op jit(solution)/shard_map/ppermute | solution.py:483
  9.9 16.9 %collective-permute-start.4 = (f32[2,2,8,1152]{3,2,1,0:T(8,128)S(1)}, f32[2,2,8,1152]{3,2,1,0:T(8,128)S(1)}, u32[]{:S(2)}, u32[]{:S(2)}) collective-permute-start(f32[2,2,8,1152]{3,2,1,0:T(8,128)S(1)} %get-tuple-element.21), channel_id=1, source_target_pairs={{0,2},{1,3},{2,0},{3,1},{4,6},{5,7},{6,4},{7,5},{8,10},{9,11},{10,... | collective-permute-start | bytes 442376 | tf_op jit(solution)/shard_map/ppermute | solution.py:483
  11.4 16.0 %collective-permute-start.5 = (f32[2,2,8,1152]{3,2,1,0:T(8,128)S(1)}, f32[2,2,8,1152]{3,2,1,0:T(8,128)S(1)}, u32[]{:S(2)}, u32[]{:S(2)}) collective-permute-start(f32[2,2,8,1152]{3,2,1,0:T(8,128)S(1)} %get-tuple-element.22), channel_id=1, source_target_pairs={{0,12},{1,13},{2,14},{3,15},{4,8},{5,9},{6,10},{7,11},{8,4},{9,5},... | collective-permute-start | bytes 442376 | tf_op jit(solution)/shard_map/ppermute | solution.py:483
  13.6 17.6 %collective-permute-start.6 = (f32[2,2,8,1152]{3,2,1,0:T(8,128)S(1)}, f32[2,2,8,1152]{3,2,1,0:T(8,128)S(1)}, u32[]{:S(2)}, u32[]{:S(2)}) collective-permute-start(f32[2,2,8,1152]{3,2,1,0:T(8,128)S(1)} %get-tuple-element.23), channel_id=1, source_target_pairs={{0,4},{1,5},{2,6},{3,7},{4,0},{5,1},{6,2},{7,3},{8,12},{9,13},{10,... | collective-permute-start | bytes 442376 | tf_op jit(solution)/shard_map/ppermute | solution.py:483
  14.8 17.0 %collective-permute-start.2 = (f32[2,2,8,1152]{3,2,1,0:T(8,128)S(1)}, f32[2,2,8,1152]{3,2,1,0:T(8,128)S(1)}, u32[]{:S(2)}, u32[]{:S(2)}) collective-permute-start(f32[2,2,8,1152]{3,2,1,0:T(8,128)S(1)} %get-tuple-element.19), channel_id=1, source_target_pairs={{0,6},{1,7},{2,4},{3,5},{4,2},{5,3},{6,0},{7,1},{8,14},{9,15},{10,... | collective-permute-start | bytes 442376 | tf_op jit(solution)/shard_map/ppermute | solution.py:483
  23.7 8.1 %collective-permute-start.1 = (f32[2,2,8,1152]{3,2,1,0:T(8,128)S(1)}, f32[2,2,8,1152]{3,2,1,0:T(8,128)S(1)}, u32[]{:S(2)}, u32[]{:S(2)}) collective-permute-start(f32[2,2,8,1152]{3,2,1,0:T(8,128)S(1)} %get-tuple-element.18), channel_id=1, source_target_pairs={{0,14},{1,15},{2,12},{3,13},{4,10},{5,11},{6,8},{7,9},{8,6},{9,7},... | collective-permute-start | bytes 442376 | tf_op jit(solution)/shard_map/ppermute | solution.py:483
  26.8 4.5 %collective-permute-start.8 = (f32[2,4,1152]{2,1,0:T(4,128)S(1)}, f32[2,4,1152]{2,1,0:T(4,128)S(1)}, u32[]{:S(2)}, u32[]{:S(2)}) collective-permute-start(f32[2,4,1152]{2,1,0:T(4,128)S(1)} %get-tuple-element.25.own_ref), channel_id=1, source_target_pairs={{1,2},{3,4},{5,6},{7,8},{9,10},{11,12},{13,14},{2,1},{4,3},{6,5},{... | collective-permute-start | bytes 110600 | tf_op jit(solution)/shard_map/ppermute | solution.py:364
  27.5 3.9 %collective-permute-start.7 = (f32[2,4,1152]{2,1,0:T(4,128)S(1)}, f32[2,4,1152]{2,1,0:T(4,128)S(1)}, u32[]{:S(2)}, u32[]{:S(2)}) collective-permute-start(f32[2,4,1152]{2,1,0:T(4,128)S(1)} %get-tuple-element.25.own_ref), channel_id=1, source_target_pairs={{0,1},{1,0},{2,3},{3,2},{4,5},{5,4},{6,7},{7,6},{8,9},{9,8},{10,11... | collective-permute-start | bytes 110600 | tf_op jit(solution)/shard_map/ppermute | solution.py:363
  31.2 0.9 %copy-start.4 = (s32[17]{0:T(128)S(1)}, s32[17]{0:T(128)}, u32[]{:S(2)}) copy-start(s32[17]{0:T(128)} %bounds_ref.1) | copy-start | bytes 208
  31.2 2.1 %collective-permute-start.10 = (f32[4,2,8,1152]{3,2,1,0:T(8,128)S(1)}, f32[4,2,8,1152]{3,2,1,0:T(8,128)S(1)}, u32[]{:S(2)}, u32[]{:S(2)}) collective-permute-start(f32[4,2,8,1152]{3,2,1,0:T(8,128)S(1)} %collect.3), channel_id=1, source_target_pairs={{0,1},{1,0},{2,3},{3,2},{4,5},{5,4},{6,7},{7,6},{8,9},{9,8},{10,11... | collective-permute-start | bytes 884744 | tf_op jit(solution)/shard_map/ppermute | solution.py:497
  31.8 1.6 %collective-permute-start.9 = (f32[4,2,8,1152]{3,2,1,0:T(8,128)S(1)}, f32[4,2,8,1152]{3,2,1,0:T(8,128)S(1)}, u32[]{:S(2)}, u32[]{:S(2)}) collective-permute-start(f32[4,2,8,1152]{3,2,1,0:T(8,128)S(1)} %collect.2), channel_id=1, source_target_pairs={{0,1},{1,0},{2,3},{3,2},{4,5},{5,4},{6,7},{7,6},{8,9},{9,8},{10,11... | collective-permute-start | bytes 884744 | tf_op jit(solution)/shard_map/ppermute | solution.py:497

commit v5 on v4

--- a/solution.py
+++ b/solution.py
@@ -12,12 +12,10 @@
 COSCUT = 0.5
 LANES = 128
 SUBLANES = 8
-STEPS = ((4, 4), (7, 7), (3, 3), (5, 5), (1, 1), (6, 6), (2, 2))
-RAW_STEPS = 1
-RAW_TIE = 2
-HALO_STEP = 9
-HALO_SWAP = 0
-SWAPS = ((0, 1, 2, 7), (3, 4, 5, 6))
+STEPS = ((4, 4), (6, 6), (1, 1), (5, 5), (2, 2), (3, 3), (7, 7))
+CORE, OUTER, FAR = 8, 9, 10
+ORDER = (0, 1, 2, 3, 4, 5, 6, OUTER, CORE, FAR)
+WINDOW = 5
 F32 = jnp.float32
 BF16 = jnp.bfloat16
 NORMAL = (((1,), (0,)), ((), ()))
@@ -183,11 +181,12 @@
     ]
 
 
-def mix_kernel(rows, split, first, steps, *refs):
-    outs = steps + split if split > 1 else steps
-    inputs, refs = refs[:8], refs[8:]
-    out_refs, flux_ref, refs = refs[:outs], refs[outs], refs[outs + 1 :]
-    (load, mix_ref, mask_ref, coupling_ref, fractions_ref, index_ref, table_ref, row_ref, sems) = refs
+def mix_kernel(rows, split, first, *refs):
+    inputs, siblings, refs = refs[:9], refs[9 : 8 + split], refs[8 + split :]
+    outs = len(refs) - 12
+    out_refs, (flux_ref, pick_ref), refs = refs[:outs], refs[outs : outs + 2], refs[outs + 2 :]
+    (load, mix_ref, mask_ref, bounds_ref, coupling_ref, fractions_ref, index_ref) = refs[:7]
+    table_ref, row_ref, sems = refs[7:]
     copies = [
         pltpu.make_async_copy(source, target, sems.at[i])
         for i, (source, target) in enumerate(zip(inputs, refs[:-1]))
@@ -199,60 +198,71 @@
     lon = flux_ref.shape[2]
     radix = lon // LANES
     me = lax.axis_index("lat")
+    chip = me // split
     core = lax.rem(me, split)
-    blocks = list(out_refs)
-    if split > 1:
-        blocks = [ref.at[c] for ref in out_refs[:steps] for c in range(split)] + blocks[steps:]
     chosen, weights = [], []
     copies[1].wait()
+    start = pl.multiple_of(core * part, part)
     for step in range(first, fields):
-        field = jnp.bitwise_xor(me // split, step_mask(me // split, step)) if split > 1 else step
-        for c in range(split):
-            start = pl.multiple_of(jnp.bitwise_xor(core, c) * part, part) if split > 1 else 0
-            weights.append(mix_ref[field, pl.ds(start, part), :])
-            chosen.append((field, part))
+        field = jnp.bitwise_xor(chip, step_mask(chip, step)) if split > 1 else step
+        weights.append(mix_ref[field, pl.ds(start, part), :])
+        chosen.append((field, part))
     weights += [mix_ref[f, levels - 1 : levels, :] for f in range(fields)]
     chosen += [(f, 1) for f in range(fields)]
     left = spread(jnp.concatenate(weights, axis=0), chosen, levels, fields)
     copies[0].wait()
     bottoms = []
-    for r in range(rows):
-        mixed = split_product(left, halves(field_rows(load, 0, fields * levels, r, rows, radix)))
-        for j, ref in enumerate(blocks):
-            ref[r] = mixed[j * part : (j + 1) * part]
-        bottoms.append(mixed[len(blocks) * part :])
+    for i, source in enumerate([load] + list(siblings)):
+        for r in range(rows):
+            mixed = split_product(left, halves(field_rows(source, 0, fields * levels, r, rows, radix)))
+            row = jnp.bitwise_xor(core, i) * rows + r if split > 1 else r
+            for j, ref in enumerate(out_refs):
+                ref[row] = mixed[j * part : (j + 1) * part]
+            if i == 0:
+                bottoms.append(mixed[outs * part :])
     for copy in copies[2:]:
         copy.wait()
     for r, bottom in enumerate(bottoms):
         speed = jnp.sqrt(bottom[0:1] * bottom[0:1] + bottom[1:2] * bottom[1:2] + 1.0)
         flux = split_product(halves(coupling_ref[...]), halves(bottom))
         flux_ref[r] = speed * flux * fractions_ref[pl.ds(index_ref[r], 1), :]
-    filter_blocks([me * rows + r for r in range(rows)], blocks, mask_ref, table_ref, row_ref)
+    first_row = bounds_ref[me] - rows // 2
+    length = bounds_ref[me + 1] - first_row + rows // 2 + 1
+    for s in range(3 * rows):
+        row = first_row + s
+        valid = (s < length) & (row >= 0) & (row < mask_ref.shape[0])
+        pick_ref[s] = jnp.full(pick_ref.shape[1:], jnp.where(valid, row - (me - 1) * rows, -1))
+    filter_blocks(
+        [chip * split * rows + r for r in range(split * rows)], out_refs, mask_ref, table_ref, row_ref
+    )
 
 
 def mixed_blocks(
-    view, vertical_mix, polar_mask, coupling, fractions, weight_index, tables, lon, rows, split, first, steps
+    view, vertical_mix, polar_mask, band_bounds, coupling, fractions, weight_index, tables, lon, rows, siblings, first
 ):
-    part = vertical_mix.shape[1] // split
-    arrays = (view, vertical_mix, polar_mask, coupling, fractions, weight_index) + tuple(
+    split = 1 + len(siblings)
+    fields, levels, _ = vertical_mix.shape
+    arrays = (view, vertical_mix, polar_mask, band_bounds, coupling, fractions, weight_index) + tuple(
         jnp.asarray(table) for table in tables
     )
     operands = [pltpu.with_memory_space_constraint(value, pltpu.HBM) for value in arrays]
     spaces = [pltpu.SMEM if value.dtype == jnp.int32 else pltpu.VMEM for value in arrays]
-    block = (rows, part, lon)
-    outs = [pltpu.VMEM((split,) + block if split > 1 else block, F32)] * steps
-    outs += [pltpu.VMEM(block, F32)] * (split if split > 1 else 0)
-    outs += [pltpu.VMEM((rows, coupling.shape[0], lon), F32)]
+    outs = [pltpu.VMEM((rows * split, levels // split, lon), F32)] * (fields - first)
+    outs += [
+        pltpu.VMEM((rows, coupling.shape[0], lon), F32),
+        pltpu.VMEM((3 * rows, coupling.shape[0], LANES), jnp.int32),
+    ]
     return pl.pallas_call(
-        functools.partial(mix_kernel, rows, split, first, steps),
+        functools.partial(mix_kernel, rows, split, first),
         out_shape=outs,
-        in_specs=[pl.BlockSpec(memory_space=pltpu.HBM)] * len(operands),
+        in_specs=[pl.BlockSpec(memory_space=pltpu.HBM)] * len(operands)
+        + [pl.BlockSpec(memory_space=pltpu.VMEM)] * len(siblings),
         out_specs=[pl.BlockSpec(memory_space=pltpu.VMEM)] * len(outs),
         scratch_shapes=[space(value.shape, value.dtype) for space, value in zip(spaces, arrays)]
         + [pltpu.SemaphoreType.DMA((len(arrays),))],
         compiler_params=pltpu.CompilerParams(vmem_limit_bytes=VMEM_LIMIT),
         name="mixed_blocks",
-    )(*operands)
+    )(*operands, *siblings)
 
 
 def pick_kernel(split, steps, view_ref, *refs):
@@ -281,16 +291,15 @@
     )(pltpu.with_memory_space_constraint(view, pltpu.HBM))
 
 
-def arrived_kernel(rows, split, step, raw_ref, mix_ref, mask_ref, table_ref, row_ref, out_ref):
+def arrived_kernel(rows, split, step, raw_ref, mix_ref, mask_ref, table_ref, row_ref, *blocks):
     levels = mix_ref.shape[1]
     part = levels // split
-    radix = out_ref.shape[3] // LANES
+    radix = blocks[0].shape[2] // LANES
     me = lax.axis_index("lat")
     chip = me // split
     core = lax.rem(me, split)
     starts = [pl.multiple_of(jnp.bitwise_xor(core, c) * part, part) for c in range(split)]
     left = halves(jnp.concatenate([mix_ref[chip, pl.ds(start, part), :] for start in starts], axis=0))
-    blocks = [out_ref.at[c] for c in range(split)]
     for r in range(rows):
         mixed = split_product(left, halves(field_rows(raw_ref, 0, levels, r, rows, radix)))
         for c in range(split):
@@ -303,89 +312,60 @@
     vmem = pl.BlockSpec(memory_space=pltpu.VMEM)
     return pl.pallas_call(
         functools.partial(arrived_kernel, rows, split, step),
-        out_shape=pltpu.VMEM((split, rows, vertical_mix.shape[1] // split, lon), F32),
+        out_shape=[pltpu.VMEM((rows, vertical_mix.shape[1] // split, lon), F32)] * split,
         in_specs=[vmem, vmem, pl.BlockSpec(memory_space=pltpu.SMEM), vmem, vmem],
-        out_specs=vmem,
+        out_specs=[vmem] * split,
         compiler_params=pltpu.CompilerParams(vmem_limit_bytes=VMEM_LIMIT),
         name="arrived_blocks",
     )(raw, vertical_mix, polar_mask, *tables)
 
 
-def collect_kernel(*refs):
-    out_ref = refs[-1]
-    for i, ref in enumerate(refs[:-1]):
-        out_ref[i] = ref[1] if len(ref.shape) == len(out_ref.shape) else ref[...]
-
-
-def collect(blocks):
-    vmem = pl.BlockSpec(memory_space=pltpu.VMEM)
-    return pl.pallas_call(
-        collect_kernel,
-        out_shape=pltpu.VMEM((len(blocks),) + blocks[0].shape[1:], F32),
-        in_specs=[vmem] * len(blocks),
-        out_specs=vmem,
-        compiler_params=pltpu.CompilerParams(vmem_limit_bytes=SMALL_LIMIT),
-        name="collect",
-    )(*blocks)
-
-
-def ocean_kernel(lat_count, split, bounds_ref, own_ref, *refs):
-    near_refs, out_ref = refs[:-1], refs[-1]
+def fill_slots(split, pick_ref, own_ref, first_ref, last_ref, out_ref):
+    slots, flux_count, lon = out_ref.shape
     rows = own_ref.shape[0]
-    slots = out_ref.shape[0]
-    half = rows // 2
-    me = lax.axis_index("lat")
-    start = bounds_ref[me] - half
-    length = bounds_ref[me + 1] - bounds_ref[me] + 2 * half + 1
-    shift = start - (me - 1) * rows
-    first, last = ([ref[r] for r in range(rows)] for ref in near_refs)
-    if split > 1:
-        upper = lax.rem(me, split) == 0
-        first, last = (
-            [jnp.where(upper, outer, other) for outer, other in zip(last, first)],
-            [jnp.where(upper, other, outer) for outer, other in zip(last, first)],
-        )
-    near = first + [own_ref[r] for r in range(rows)] + last
-    for s in range(slots):
-        row = start + s
-        valid = (s < length) & (row >= 0) & (row < lat_count)
-        picked = jnp.zeros_like(near[0])
-        for p, value in enumerate(near):
-            picked = jnp.where(valid & (shift + s == p), value, picked)
-        out_ref[s] = picked
-
-
-def neighbour_rows(weighted, device_count, split):
+    upper = lax.rem(lax.axis_index("lat"), split) == 0
+    for t in range(lon // LANES):
+        lanes = slice(t * LANES, (t + 1) * LANES)
+        first, last = ([ref[r, :, lanes] for r in range(rows)] for ref in (first_ref, last_ref))
+        if split > 1:
+            first, last = (
+                [jnp.where(upper, outer, other) for outer, other in zip(last, first)],
+                [jnp.where(upper, other, outer) for outer, other in zip(last, first)],
+            )
+        near = first + [own_ref[r, :, lanes] for r in range(rows)] + last
+        for s in range(slots):
+            pick = pick_ref[s]
+            picked = jnp.zeros((flux_count, LANES), F32)
+            for p, value in enumerate(near):
+                picked = jnp.where(pick == p, value, picked)
+            out_ref[s, :, lanes] = picked
+
+
+def neighbour_rows(weighted, device_count):
     ends = device_count - 1
-    if split == 2:
-        pairs = [(i, i + 1) for i in range(1, ends, 2)]
-        return [
-            lax.ppermute(weighted, "lat", [(i, i ^ 1) for i in range(device_count)]),
-            lax.ppermute(weighted, "lat", pairs + [(j, i) for i, j in pairs]),
-        ]
     return [
         lax.ppermute(weighted, "lat", [(i, i + 1) for i in range(ends)]),
         lax.ppermute(weighted, "lat", [(i + 1, i) for i in range(ends)]),
     ]
 
 
-def ocean_slots(weighted, near, band_bounds, lat_count, split):
-    rows, flux_count, lon = weighted.shape
+def ocean_slots(picks, weighted, near):
     vmem = pl.BlockSpec(memory_space=pltpu.VMEM)
     return pl.pallas_call(
-        functools.partial(ocean_kernel, lat_count, split),
-        out_shape=jax.ShapeDtypeStruct((3 * rows, flux_count, lon), F32),
-        in_specs=[pl.BlockSpec(memory_space=pltpu.SMEM)] + [vmem] * 3,
+        functools.partial(fill_slots, 1),
+        out_shape=jax.ShapeDtypeStruct(picks.shape[:2] + weighted.shape[2:], F32),
+        in_specs=[vmem] * 4,
         out_specs=vmem,
         compiler_params=pltpu.CompilerParams(vmem_limit_bytes=SMALL_LIMIT),
         name="ocean",
-    )(band_bounds, weighted, *near)
+    )(picks, weighted, *near)
 
 
 def place_kernel(split, sources, *refs):
-    out_ref, buffer, sems = refs[-3:]
-    part, lon = refs[0].shape[-2:]
-    rows = refs[0].shape[-3]
+    out_ref, ocean_ref, buffer, slots, sems, slots_sem = refs[-6:]
+    surface = refs[-10:-6]
+    part, lon = refs[0].shape[1:]
+    rows = surface[1].shape[0]
     radix = lon // LANES
     chip_rows = rows * split
     tile = radix * SUBLANES
@@ -401,10 +381,10 @@
     for step in [len(STEPS)] + list(range(len(STEPS))):
         source = jnp.bitwise_xor(chip, step_mask(chip, step))
         base = source // chips * (part * tile) + lax.rem(source, chips) * chip_rows
-        for c, (operand, index) in enumerate(sources[step]):
-            ref = refs[operand] if index is None else refs[operand].at[index]
-            for r in range(rows):
-                row = base + jnp.bitwise_xor(core, c) * rows + r
+        for c, operand in enumerate(sources[step]):
+            ref = refs[operand]
+            for r in range(ref.shape[0]):
+                row = base + (r if len(sources[step]) == 1 else jnp.bitwise_xor(core, c) * rows + r)
                 for t in range(radix):
                     buffer[pl.ds(row + t * SUBLANES, part, stride=tile), :] = ref[
                         r, :, t * LANES : (t + 1) * LANES
@@ -422,26 +402,35 @@
                 )
                 copy.start()
                 copies.append(copy)
+    fill_slots(split, *surface, slots)
+    copies.append(pltpu.make_async_copy(slots, ocean_ref, slots_sem))
+    copies[-1].start()
     for copy in copies:
         copy.wait()
 
 
-def place(operands, sources, lat_count, after):
-    part, lon = operands[0].shape[-2:]
+def place(operands, sources, lat_count, surface):
+    part, lon = operands[0].shape[1:]
     size = part * lat_count * lon // LANES
     groups = lat_count // SUBLANES
     vmem = pl.BlockSpec(memory_space=pltpu.VMEM)
-    out = pl.pallas_call(
-        functools.partial(place_kernel, len(sources[0]), sources),
-        out_shape=jax.ShapeDtypeStruct((size, LANES), F32),
-        in_specs=[vmem] * len(operands) + [pl.BlockSpec(memory_space=pl.ANY)],
-        out_specs=pl.BlockSpec(memory_space=pltpu.HBM),
-        scratch_shapes=[pltpu.VMEM((size, LANES), F32), pltpu.SemaphoreType.DMA((groups, part))],
+    slots = surface[0].shape[:2] + (lon,)
+    out, ocean = pl.pallas_call(
+        functools.partial(place_kernel, 2, sources),
+        out_shape=[jax.ShapeDtypeStruct((size, LANES), F32), jax.ShapeDtypeStruct(slots, F32)],
+        in_specs=[vmem] * (len(operands) + len(surface)),
+        out_specs=[pl.BlockSpec(memory_space=pltpu.HBM)] * 2,
+        scratch_shapes=[
+            pltpu.VMEM((size, LANES), F32),
+            pltpu.VMEM(slots, F32),
+            pltpu.SemaphoreType.DMA((groups, part)),
+            pltpu.SemaphoreType.DMA,
+        ],
         compiler_params=pltpu.CompilerParams(vmem_limit_bytes=VMEM_LIMIT),
         name="place",
-    )(*operands, pltpu.with_memory_space_constraint(after, pltpu.HBM))
+    )(*operands, *surface)
     tiles = out.reshape(part, groups, lon // LANES, SUBLANES, LANES)
-    return tiles.transpose(0, 1, 3, 2, 4).reshape(part, lat_count, lon)
+    return tiles.transpose(0, 1, 3, 2, 4).reshape(part, lat_count, lon), ocean
 
 
 def body(device_count, state, vertical_mix, coupling, fractions, weight_index, band_bounds, polar_mask):
@@ -460,6 +449,7 @@
         view,
         vertical_mix,
         polar_mask,
+        band_bounds,
         coupling,
         fractions,
         weight_index,
@@ -470,40 +460,36 @@
 
     if part == SUBLANES and level_count == 2 * part and field_count == len(STEPS) + 1:
         split = 2
-        raw = raw_fields(view, field_count, split, tuple(range(RAW_STEPS)))
-        *blocks, near, far, weighted = mixed(split, RAW_STEPS, len(STEPS) - RAW_STEPS)
-        neighbours = neighbour_rows(weighted, device_count, split)
-        blocks = list(raw) + blocks
-        for step, block in enumerate(blocks):
-            if step == HALO_STEP:
-                block, *neighbours = lax.optimization_barrier((block, *neighbours))
-            if step == RAW_TIE:
-                block, *blocks[:RAW_STEPS] = lax.optimization_barrier((block, *blocks[:RAW_STEPS]))
-            pairs = [(i, i ^ split * step_mask(i // split, step)) for i in range(device_count)]
-            blocks[step] = lax.ppermute(block, "lat", pairs)
-        for step in range(RAW_STEPS):
-            blocks[step] = arrived_blocks(
-                blocks[step], vertical_mix, polar_mask, tables, lon_count, row_count, split, step
-            )
-        operands = blocks + [near]
-        sources = [[(step, 0)] for step in range(len(STEPS))] + [[(len(STEPS), None)]]
-        for number, group in enumerate(SWAPS):
-            if number == HALO_SWAP:
-                last = max(step for step in group if step < len(STEPS))
-                blocks[last], *neighbours = lax.optimization_barrier((blocks[last], *neighbours))
-            held = collect([(blocks + [far])[step] for step in group])
-            for i, step in enumerate(group):
-                sources[step].append((len(operands), i))
-            operands.append(lax.ppermute(held, "lat", [(i, i ^ 1) for i in range(device_count)]))
-        ocean = ocean_slots(weighted, neighbours, band_bounds, lat_count, split)
-        state_out = place(operands, sources, lat_count, ocean)
+        swap = [(i, i ^ 1) for i in range(device_count)]
+        sibling = lax.ppermute(view, "lat", swap)
+        raw = raw_fields(view, field_count, split, (0,))
+        *blocks, weighted, picks = mixed((sibling,), 1)
+        blocks = dict(enumerate(list(raw) + blocks))
+        pairs = [(i, i + 1) for i in range(1, device_count - 1, 2)]
+        pairs = {CORE: swap, OUTER: pairs + [(j, i) for i, j in pairs], FAR: swap}
+        blocks |= {CORE: weighted, OUTER: weighted}
+        for step in range(len(STEPS)):
+            pairs[step] = [(i, i ^ split * step_mask(i // split, step)) for i in range(device_count)]
+        for place_in_order, item in enumerate(ORDER):
+            if item == FAR:
+                blocks[0], blocks[FAR] = arrived_blocks(
+                    blocks[0], vertical_mix, polar_mask, tables, lon_count, row_count, split, 0
+                )
+            if place_in_order >= WINDOW:
+                earlier = ORDER[place_in_order - WINDOW]
+                blocks[item], blocks[earlier] = lax.optimization_barrier((blocks[item], blocks[earlier]))
+            blocks[item] = lax.ppermute(blocks[item], "lat", pairs[item])
+        operands = [blocks[step] for step in range(len(STEPS) + 1)] + [blocks[FAR]]
+        sources = [[0, len(STEPS) + 1]] + [[step] for step in range(1, len(STEPS) + 1)]
+        surface = (picks, weighted, blocks[CORE], blocks[OUTER])
+        state_out, ocean = place(operands, sources, lat_count, surface)
     else:
-        *blocks, weighted = mixed(1, 0, field_count)
+        *blocks, weighted, picks = mixed((), 0)
         stacked = jnp.concatenate(blocks, axis=1)
         moved = lax.all_to_all(stacked, "lat", split_axis=1, concat_axis=0, tiled=True)
         state_out = jnp.transpose(moved, (1, 0, 2))
-        neighbours = neighbour_rows(weighted, device_count, 1)
-        ocean = ocean_slots(weighted, neighbours, band_bounds, lat_count, 1)
+        neighbours = neighbour_rows(weighted, device_count)
+        ocean = ocean_slots(picks, weighted, neighbours)
     return (state_out, jnp.transpose(ocean, (1, 0, 2)))
 
 

time: 35.4 us -> 34.4 us (0.972)
  waiting for transfers between devices: 3.4 us -> 10.4 us
  starting transfers between devices: 22.3 us -> 15.8 us
  Pallas kernels: 8.53 us -> 7.29 us
    ppermute x11, waiting for transfers between devices: 3.4 us -> 10.4 us  [the longest x10 10.4 us: body(): blocks[item] = lax.ppermute(blocks[item], 'lat', pairs[item])]
    ppermute x11, starting transfers between devices: 22.3 us -> 15.8 us  [the longest x10 15.3 us: body(): blocks[item] = lax.ppermute(blocks[item], 'lat', pairs[item])]
    pallas_call x5 -> x2, Pallas kernels: 6.84 us -> 5.62 us  [the longest x1 4.08 us: mixed_blocks(): pl.pallas_call(functools.partial(mix_kernel, rows, split, first), out_sha...]
  transfers between devices with their start and end apart: 11 -> 11, of which waited for: 3 -> 5; matrix products, arithmetic and copies ran while one was open for 0% -> 0% of each run, Pallas kernels for 17% -> 17%
where the time goes in v5:
time: 34.4 us; the launch traced here: 34.2 us
  starting transfers between devices  15.8 us (46%)
  waiting for transfers between devices  10.4 us (30%)
  Pallas kernels  7.29 us (21%)
  between operations  0.73 us (2%)
    ppermute x10, starting transfers between devices, body(): blocks[item] = lax.ppermute(blocks[item], 'lat', pairs[item])  15.3 us
    ppermute x10, waiting for transfers between devices, body(): blocks[item] = lax.ppermute(blocks[item], 'lat', pairs[item])  10.4 us
    pallas_call x1, Pallas kernels, mixed_blocks(): pl.pallas_call(functools.partial(mix_kernel, rows, split, first), out_sha...  4.08 us
    pallas_call x1, Pallas kernels, place(): pl.pallas_call(functools.partial(place_kernel, 2, sources), out_shape=[ja...  1.54 us
    pallas_call x1, Pallas kernels, raw_fields(): pl.pallas_call(functools.partial(pick_kernel, split, steps), out_shape=[p...  0.92 us
    pallas_call x1, Pallas kernels, arrived_blocks(): pl.pallas_call(functools.partial(arrived_kernel, rows, split, step), out_...  0.75 us
  transfers between devices with their start and end apart: 11, of which 5 were waited for; matrix products, arithmetic and copies ran while one was open for 0% of the time, Pallas kernels for 17%

profile of v5, /device:TPU:0, one launch (start us, length us, event | category | flops | bytes accessed | tf_op | source)
XLA Modules:
  0.0 34.2 jit_solution(16830754308734746085)
XLA Ops:
  0.6 0.5 %collective-permute-start = (f32[2304,128]{1,0:T(8,128)}, f32[2304,128]{1,0:T(8,128)S(1)}, u32[]{:S(2)}, u32[]{:S(2)}) collective-permute-start(f32[2304,128]{1,0:T(8,128)} %bitcast.11), channel_id=1, source_target_pairs={{0,1},{1,0},{2,3},{3,2},{4,5},{5,4},{6,7},{7,6},{8,9},{9,8},{10,11... | collective-permute-start | bytes 3538952 | tf_op jit(solution)/shard_map/ppermute | solution.py:464
  1.1 0.9 %raw_fields.1 = f32[288,128]{1,0:T(8,128)S(1)} custom-call(f32[2304,128]{1,0:T(8,128)} %bitcast.12), custom_call_target="tpu_custom_call" | custom-call | tf_op jit(solution)/shard_map/raw_fields/pallas_call | solution.py:283
  2.1 0.0 copy-start
  2.1 0.0 copy-start.1
  2.1 0.0 copy-start.2
  2.1 0.0 copy-start.3
  2.1 3.7 %collective-permute-start.1 = (f32[288,128]{1,0:T(8,128)S(1)}, f32[288,128]{1,0:T(8,128)S(1)}, u32[]{:S(2)}, u32[]{:S(2)}) collective-permute-start(f32[288,128]{1,0:T(8,128)S(1)} %raw_fields.1), channel_id=1, source_target_pairs={{0,8},{1,9},{2,10},{3,11},{4,12},{5,13},{6,14},{7,15},{8,0},{9,1},... | collective-permute-start | bytes 442376 | tf_op jit(solution)/shard_map/ppermute | solution.py:481
  5.8 4.1 %mixed_blocks.1 = (f32[4,8,1152]{2,1,0:T(8,128)S(1)}, f32[4,8,1152]{2,1,0:T(8,128)S(1)}, f32[4,8,1152]{2,1,0:T(8,128)S(1)}, f32[4,8,1152]{2,1,0:T(8,128)S(1)}, f...) custom-call(f32[2304,128]{1,0:T(8,128)} %bitcast.13, ...), custom_call_target="tpu_custom_call" | custom-call | tf_op jit(solution)/shard_map/mixed_blocks/pallas_call | solution.py:255
  9.9 3.0 %collective-permute-start.2 = (f32[4,8,1152]{2,1,0:T(8,128)S(1)}, f32[4,8,1152]{2,1,0:T(8,128)S(1)}, u32[]{:S(2)}, u32[]{:S(2)}) collective-permute-start(f32[4,8,1152]{2,1,0:T(8,128)S(1)} %get-tuple-element.29), channel_id=1, source_target_pairs={{0,12},{1,13},{2,14},{3,15},{4,8},{5,9},{6,10},{7,11},{8,4},{9,5},... | collective-permute-start | bytes 442376 | tf_op jit(solution)/shard_map/ppermute | solution.py:481
  12.9 0.0 collective-permute-start.5
  12.9 1.6 %collective-permute-start.3 = (f32[4,8,1152]{2,1,0:T(8,128)S(1)}, f32[4,8,1152]{2,1,0:T(8,128)S(1)}, u32[]{:S(2)}, u32[]{:S(2)}) collective-permute-start(f32[4,8,1152]{2,1,0:T(8,128)S(1)} %get-tuple-element.32), channel_id=1, source_target_pairs={{0,2},{1,3},{2,0},{3,1},{4,6},{5,7},{6,4},{7,5},{8,10},{9,11},{10,... | collective-permute-start | bytes 442376 | tf_op jit(solution)/shard_map/ppermute | solution.py:481
  14.5 1.3 %collective-permute-start.4 = (f32[4,8,1152]{2,1,0:T(8,128)S(1)}, f32[4,8,1152]{2,1,0:T(8,128)S(1)}, u32[]{:S(2)}, u32[]{:S(2)}) collective-permute-start(f32[4,8,1152]{2,1,0:T(8,128)S(1)} %get-tuple-element.34), channel_id=1, source_target_pairs={{0,10},{1,11},{2,8},{3,9},{4,14},{5,15},{6,12},{7,13},{8,2},{9,3},... | collective-permute-start | bytes 442376 | tf_op jit(solution)/shard_map/ppermute | solution.py:481
  15.8 0.9 %collective-permute-start.6 = (f32[4,8,1152]{2,1,0:T(8,128)S(1)}, f32[4,8,1152]{2,1,0:T(8,128)S(1)}, u32[]{:S(2)}, u32[]{:S(2)}) collective-permute-start(f32[4,8,1152]{2,1,0:T(8,128)S(1)} %get-tuple-element.39), channel_id=1, source_target_pairs={{0,6},{1,7},{2,4},{3,5},{4,2},{5,3},{6,0},{7,1},{8,14},{9,15},{10,... | collective-permute-start | bytes 442376 | tf_op jit(solution)/shard_map/ppermute | solution.py:481
  16.8 1.7 %collective-permute-done.2.refs_1_ = f32[4,8,1152]{2,1,0:T(8,128)S(1)} collective-permute-done((f32[4,8,1152]{2,1,0:T(8,128)S(1)}, f32[4,8,1152]{2,1,0:T(8,128)S(1)}, u32[]{:S(2)}, u32[]{:S(2)}) %collective-permute-start.2) | collective-permute-done | bytes 147488 | tf_op jit(solution)/shard_map/ppermute | solution.py:481
  18.5 4.0 %collective-permute-start.7 = (f32[4,8,1152]{2,1,0:T(8,128)S(1)}, f32[4,8,1152]{2,1,0:T(8,128)S(1)}, u32[]{:S(2)}, u32[]{:S(2)}) collective-permute-start(f32[4,8,1152]{2,1,0:T(8,128)S(1)} %get-tuple-element.40), channel_id=1, source_target_pairs={{0,14},{1,15},{2,12},{3,13},{4,10},{5,11},{6,8},{7,9},{8,6},{9,7},... | collective-permute-start | bytes 442376 | tf_op jit(solution)/shard_map/ppermute | solution.py:481
  22.5 0.8 %arrived_blocks.1 = (f32[2,8,1152]{2,1,0:T(8,128)S(1)}, f32[2,8,1152]{2,1,0:T(8,128)S(1)}) custom-call(f32[288,128]{1,0:T(8,128)S(1)} %collective-permute-done.1.raw_ref, f32[8,16,16]{2,1,0:T(8,128)S(1)} %copy-done.1, s32[32]{0:T(128)S(1)} %copy-done.3, bf16[2,1152,256]{2,1,0:T(8,128)(2,1)S(1)} %copy-done, f32[48,256]{1,0:T(8,128)S(1)} %copy-done.2), custom_call_target="tpu_custom_call" | custom-call | tf_op jit(solution)/shard_map/arrived_blocks/pallas_call | solution.py:313
  23.3 0.0 collective-permute-done.5.refs_4_
  23.3 0.1 collective-permute-start.8
  23.4 0.7 %collective-permute-start.10 = (f32[2,4,1152]{2,1,0:T(4,128)S(1)}, f32[2,4,1152]{2,1,0:T(4,128)S(1)}, u32[]{:S(2)}, u32[]{:S(2)}) collective-permute-start(f32[2,4,1152]{2,1,0:T(4,128)S(1)} %get-tuple-element.45.refs_10_), channel_id=1, source_target_pairs={{1,2},{3,4},{5,6},{7,8},{9,10},{11,12},{13,14},{2,1},{4,3},{6,5},{... | collective-permute-start | bytes 110600 | tf_op jit(solution)/shard_map/ppermute | solution.py:481
  24.0 3.5 %collective-permute-done.4.refs_3_ = f32[4,8,1152]{2,1,0:T(8,128)S(1)} collective-permute-done((f32[4,8,1152]{2,1,0:T(8,128)S(1)}, f32[4,8,1152]{2,1,0:T(8,128)S(1)}, u32[]{:S(2)}, u32[]{:S(2)}) %collective-permute-start.4) | collective-permute-done | bytes 147488 | tf_op jit(solution)/shard_map/ppermute | solution.py:481
  27.5 0.7 %collective-permute-done.6.refs_5_ = f32[4,8,1152]{2,1,0:T(8,128)S(1)} collective-permute-done((f32[4,8,1152]{2,1,0:T(8,128)S(1)}, f32[4,8,1152]{2,1,0:T(8,128)S(1)}, u32[]{:S(2)}, u32[]{:S(2)}) %collective-permute-start.6) | collective-permute-done | bytes 147488 | tf_op jit(solution)/shard_map/ppermute | solution.py:481
  28.2 0.5 %collective-permute-done.9.refs_11_ = f32[2,4,1152]{2,1,0:T(4,128)S(1)} collective-permute-done((f32[2,4,1152]{2,1,0:T(4,128)S(1)}, f32[2,4,1152]{2,1,0:T(4,128)S(1)}, u32[]{:S(2)}, u32[]{:S(2)}) %collective-permute-start.9) | collective-permute-done | bytes 36896 | tf_op jit(solution)/shard_map/ppermute | solution.py:481
  28.7 4.0 %collective-permute-done.7.refs_6_ = f32[4,8,1152]{2,1,0:T(8,128)S(1)} collective-permute-done((f32[4,8,1152]{2,1,0:T(8,128)S(1)}, f32[4,8,1152]{2,1,0:T(8,128)S(1)}, u32[]{:S(2)}, u32[]{:S(2)}) %collective-permute-start.7) | collective-permute-done | bytes 147488 | tf_op jit(solution)/shard_map/ppermute | solution.py:481
  32.7 1.5 %place.1 = (f32[2304,128]{1,0:T(8,128)}, f32[6,4,1152]{2,1,0:T(4,128)}) custom-call(f32[2,8,1152]{2,1,0:T(8,128)S(1)} %get-tuple-element.27.refs_0_, f32[4,8,1152]{2,1,0:T(8,128)S(1)} %collective-permute-done.2.refs_1_, f32[4,8,1152]{2,1,0:T(8,128)S(1)} %collective-permute-done.3.refs_2_, f32[4,8,1152]{2,1,0:T(8,128)S(1)} %collective-permute-done.4.refs_3_, ...), custom_call_target="tpu_custom_call" | custom-call | tf_op jit(solution)/shard_map/place/pallas_call | solution.py:418
  (10 shorter events, 0.0 us)
Async XLA Ops:
  0.6 5.2 %collective-permute-start = (f32[2304,128]{1,0:T(8,128)}, f32[2304,128]{1,0:T(8,128)S(1)}, u32[]{:S(2)}, u32[]{:S(2)}) collective-permute-start(f32[2304,128]{1,0:T(8,128)} %bitcast.11), channel_id=1, source_target_pairs={{0,1},{1,0},{2,3},{3,2},{4,5},{5,4},{6,7},{7,6},{8,9},{9,8},{10,11... | collective-permute-start | bytes 3538952 | tf_op jit(solution)/shard_map/ppermute | solution.py:464
  2.1 20.4 %copy-start = (bf16[2,1152,256]{2,1,0:T(8,128)(2,1)S(1)}, bf16[2,1152,256]{2,1,0:T(8,128)(2,1)}, u32[]{:S(2)}) copy-start(bf16[2,1152,256]{2,1,0:T(8,128)(2,1)} %constant.4.clone.refs_7_.table_ref) | copy-start | bytes 3538948
  2.1 20.4 %copy-start.1 = (f32[8,16,16]{2,1,0:T(8,128)S(1)}, f32[8,16,16]{2,1,0:T(8,128)}, u32[]{:S(2)}) copy-start(f32[8,16,16]{2,1,0:T(8,128)} %mix_ref.1) | copy-start | bytes 24580
  2.1 20.4 %copy-start.2 = (f32[48,256]{1,0:T(8,128)S(1)}, f32[48,256]{1,0:T(8,128)}, u32[]{:S(2)}) copy-start(f32[48,256]{1,0:T(8,128)} %constant.5.clone.refs_8_.row_ref) | copy-start | bytes 147460
  2.1 20.4 %copy-start.3 = (s32[32]{0:T(128)S(1)}, s32[32]{0:T(128)}, u32[]{:S(2)}) copy-start(s32[32]{0:T(128)} %mask_ref.1) | copy-start | bytes 388
  2.1 13.7 %collective-permute-start.1 = (f32[288,128]{1,0:T(8,128)S(1)}, f32[288,128]{1,0:T(8,128)S(1)}, u32[]{:S(2)}, u32[]{:S(2)}) collective-permute-start(f32[288,128]{1,0:T(8,128)S(1)} %raw_fields.1), channel_id=1, source_target_pairs={{0,8},{1,9},{2,10},{3,11},{4,12},{5,13},{6,14},{7,15},{8,0},{9,1},... | collective-permute-start | bytes 442376 | tf_op jit(solution)/shard_map/ppermute | solution.py:481
  9.9 8.6 %collective-permute-start.2 = (f32[4,8,1152]{2,1,0:T(8,128)S(1)}, f32[4,8,1152]{2,1,0:T(8,128)S(1)}, u32[]{:S(2)}, u32[]{:S(2)}) collective-permute-start(f32[4,8,1152]{2,1,0:T(8,128)S(1)} %get-tuple-element.29), channel_id=1, source_target_pairs={{0,12},{1,13},{2,14},{3,15},{4,8},{5,9},{6,10},{7,11},{8,4},{9,5},... | collective-permute-start | bytes 442376 | tf_op jit(solution)/shard_map/ppermute | solution.py:481
  12.9 10.3 %collective-permute-start.5 = (f32[4,8,1152]{2,1,0:T(8,128)S(1)}, f32[4,8,1152]{2,1,0:T(8,128)S(1)}, u32[]{:S(2)}, u32[]{:S(2)}) collective-permute-start(f32[4,8,1152]{2,1,0:T(8,128)S(1)} %get-tuple-element.37), channel_id=1, source_target_pairs={{0,4},{1,5},{2,6},{3,7},{4,0},{5,1},{6,2},{7,3},{8,12},{9,13},{10,... | collective-permute-start | bytes 442376 | tf_op jit(solution)/shard_map/ppermute | solution.py:481
  12.9 10.4 %collective-permute-start.3 = (f32[4,8,1152]{2,1,0:T(8,128)S(1)}, f32[4,8,1152]{2,1,0:T(8,128)S(1)}, u32[]{:S(2)}, u32[]{:S(2)}) collective-permute-start(f32[4,8,1152]{2,1,0:T(8,128)S(1)} %get-tuple-element.32), channel_id=1, source_target_pairs={{0,2},{1,3},{2,0},{3,1},{4,6},{5,7},{6,4},{7,5},{8,10},{9,11},{10,... | collective-permute-start | bytes 442376 | tf_op jit(solution)/shard_map/ppermute | solution.py:481
  14.5 13.0 %collective-permute-start.4 = (f32[4,8,1152]{2,1,0:T(8,128)S(1)}, f32[4,8,1152]{2,1,0:T(8,128)S(1)}, u32[]{:S(2)}, u32[]{:S(2)}) collective-permute-start(f32[4,8,1152]{2,1,0:T(8,128)S(1)} %get-tuple-element.34), channel_id=1, source_target_pairs={{0,10},{1,11},{2,8},{3,9},{4,14},{5,15},{6,12},{7,13},{8,2},{9,3},... | collective-permute-start | bytes 442376 | tf_op jit(solution)/shard_map/ppermute | solution.py:481
  15.8 12.4 %collective-permute-start.6 = (f32[4,8,1152]{2,1,0:T(8,128)S(1)}, f32[4,8,1152]{2,1,0:T(8,128)S(1)}, u32[]{:S(2)}, u32[]{:S(2)}) collective-permute-start(f32[4,8,1152]{2,1,0:T(8,128)S(1)} %get-tuple-element.39), channel_id=1, source_target_pairs={{0,6},{1,7},{2,4},{3,5},{4,2},{5,3},{6,0},{7,1},{8,14},{9,15},{10,... | collective-permute-start | bytes 442376 | tf_op jit(solution)/shard_map/ppermute | solution.py:481
  18.5 14.2 %collective-permute-start.7 = (f32[4,8,1152]{2,1,0:T(8,128)S(1)}, f32[4,8,1152]{2,1,0:T(8,128)S(1)}, u32[]{:S(2)}, u32[]{:S(2)}) collective-permute-start(f32[4,8,1152]{2,1,0:T(8,128)S(1)} %get-tuple-element.40), channel_id=1, source_target_pairs={{0,14},{1,15},{2,12},{3,13},{4,10},{5,11},{6,8},{7,9},{8,6},{9,7},... | collective-permute-start | bytes 442376 | tf_op jit(solution)/shard_map/ppermute | solution.py:481
  23.3 5.5 %collective-permute-start.8 = (f32[2,8,1152]{2,1,0:T(8,128)S(1)}, f32[2,8,1152]{2,1,0:T(8,128)S(1)}, u32[]{:S(2)}, u32[]{:S(2)}) collective-permute-start(f32[2,8,1152]{2,1,0:T(8,128)S(1)} %get-tuple-element.42), channel_id=1, source_target_pairs={{0,1},{1,0},{2,3},{3,2},{4,5},{5,4},{6,7},{7,6},{8,9},{9,8},{10,11... | collective-permute-start | bytes 221192 | tf_op jit(solution)/shard_map/ppermute | solution.py:481
  23.4 4.9 %collective-permute-start.10 = (f32[2,4,1152]{2,1,0:T(4,128)S(1)}, f32[2,4,1152]{2,1,0:T(4,128)S(1)}, u32[]{:S(2)}, u32[]{:S(2)}) collective-permute-start(f32[2,4,1152]{2,1,0:T(4,128)S(1)} %get-tuple-element.45.refs_10_), channel_id=1, source_target_pairs={{1,2},{3,4},{5,6},{7,8},{9,10},{11,12},{13,14},{2,1},{4,3},{6,5},{... | collective-permute-start | bytes 110600 | tf_op jit(solution)/shard_map/ppermute | solution.py:481
  27.5 1.2 %collective-permute-start.9 = (f32[2,4,1152]{2,1,0:T(4,128)S(1)}, f32[2,4,1152]{2,1,0:T(4,128)S(1)}, u32[]{:S(2)}, u32[]{:S(2)}) collective-permute-start(f32[2,4,1152]{2,1,0:T(4,128)S(1)} %get-tuple-element.45.refs_10_), channel_id=1, source_target_pairs={{0,1},{1,0},{2,3},{3,2},{4,5},{5,4},{6,7},{7,6},{8,9},{9,8},{10,11... | collective-permute-start | bytes 110600 | tf_op jit(solution)/shard_map/ppermute | solution.py:481

commit v6 on v5

--- a/solution.py
+++ b/solution.py
@@ -12,7 +12,7 @@
 COSCUT = 0.5
 LANES = 128
 SUBLANES = 8
-STEPS = ((4, 4), (6, 6), (1, 1), (5, 5), (2, 2), (3, 3), (7, 7))
+STEPS = (6, 4, 3, 5, 1, 2, 7)
 CORE, OUTER, FAR = 8, 9, 10
 ORDER = (0, 1, 2, 3, 4, 5, 6, OUTER, CORE, FAR)
 WINDOW = 5
@@ -149,13 +149,8 @@
                     ref[r] = smooth[start : start + part]
 
 
-def step_mask(chip, step):
-    first, second = STEPS[step] if step < len(STEPS) else (0, 0)
-    if first == second:
-        return first
-    if isinstance(chip, int):
-        return first if (chip >> 2 ^ chip >> 1) & 1 else second
-    return jnp.where(lax.rem(chip // 4 + chip // 2, 2) == 1, first, second)
+def partner(chip, step):
+    return chip ^ STEPS[step] if step < len(STEPS) else chip
 
 
 def field_rows(ref, start, count, r, rows, radix):
@@ -204,7 +199,7 @@
     copies[1].wait()
     start = pl.multiple_of(core * part, part)
     for step in range(first, fields):
-        field = jnp.bitwise_xor(chip, step_mask(chip, step)) if split > 1 else step
+        field = partner(chip, step) if split > 1 else step
         weights.append(mix_ref[field, pl.ds(start, part), :])
         chosen.append((field, part))
     weights += [mix_ref[f, levels - 1 : levels, :] for f in range(fields)]
@@ -271,7 +266,7 @@
     chip = lax.axis_index("lat") // split
     copies = []
     for i, step in enumerate(steps):
-        start = pl.multiple_of(jnp.bitwise_xor(chip, step_mask(chip, step)) * span, span)
+        start = pl.multiple_of(partner(chip, step) * span, span)
         copies.append(pltpu.make_async_copy(view_ref.at[pl.ds(start, span)], out_refs[i], sems.at[i]))
         copies[-1].start()
     for copy in copies:
@@ -304,7 +299,7 @@
         mixed = split_product(left, halves(field_rows(raw_ref, 0, levels, r, rows, radix)))
         for c in range(split):
             blocks[c][r] = mixed[c * part : (c + 1) * part]
-    source = jnp.bitwise_xor(chip, step_mask(chip, step)) * split + core
+    source = partner(chip, step) * split + core
     filter_blocks([source * rows + r for r in range(rows)], blocks, mask_ref, table_ref, row_ref)
 
 
@@ -369,17 +364,16 @@
     radix = lon // LANES
     chip_rows = rows * split
     tile = radix * SUBLANES
-    span = out_ref.shape[0] // part
     me = lax.axis_index("lat")
     chip = me // split
     core = lax.rem(me, split)
     groups = chip_rows * len(sources) // SUBLANES
     chips = len(sources) // groups
-    step_groups = [{first // chips, second // chips} for first, second in STEPS] + [{0}]
-    pending = {group: sum(group in held for held in step_groups) for group in range(groups)}
+    step_groups = [mask // chips for mask in STEPS] + [0]
+    pending = [step_groups.count(group) for group in range(groups)]
     copies = []
     for step in [len(STEPS)] + list(range(len(STEPS))):
-        source = jnp.bitwise_xor(chip, step_mask(chip, step))
+        source = partner(chip, step)
         base = source // chips * (part * tile) + lax.rem(source, chips) * chip_rows
         for c, operand in enumerate(sources[step]):
             ref = refs[operand]
@@ -389,19 +383,19 @@
                     buffer[pl.ds(row + t * SUBLANES, part, stride=tile), :] = ref[
                         r, :, t * LANES : (t + 1) * LANES
                     ]
-        for group in step_groups[step]:
-            pending[group] -= 1
-            if pending[group]:
-                continue
+        group = step_groups[step]
+        pending[group] -= 1
+        if not pending[group]:
             place = jnp.bitwise_xor(chip // chips, group)
-            for f in range(part):
-                copy = pltpu.make_async_copy(
-                    buffer.at[pl.ds(pl.multiple_of((place * part + f) * tile, SUBLANES), tile)],
-                    out_ref.at[pl.ds(pl.multiple_of(f * span + place * tile, SUBLANES), tile)],
-                    sems.at[group, f],
-                )
-                copy.start()
-                copies.append(copy)
+            copy = pltpu.make_async_copy(
+                buffer.at[pl.ds(pl.multiple_of(place * part * tile, SUBLANES), part * tile)].reshape(
+                    part, tile, LANES
+                ),
+                out_ref.at[:, pl.ds(pl.multiple_of(place * tile, SUBLANES), tile)],
+                sems.at[group],
+            )
+            copy.start()
+            copies.append(copy)
     fill_slots(split, *surface, slots)
     copies.append(pltpu.make_async_copy(slots, ocean_ref, slots_sem))
     copies[-1].start()
@@ -417,13 +411,16 @@
     slots = surface[0].shape[:2] + (lon,)
     out, ocean = pl.pallas_call(
         functools.partial(place_kernel, 2, sources),
-        out_shape=[jax.ShapeDtypeStruct((size, LANES), F32), jax.ShapeDtypeStruct(slots, F32)],
+        out_shape=[
+            jax.ShapeDtypeStruct((part, size // part, LANES), F32),
+            jax.ShapeDtypeStruct(slots, F32),
+        ],
         in_specs=[vmem] * (len(operands) + len(surface)),
         out_specs=[pl.BlockSpec(memory_space=pltpu.HBM)] * 2,
         scratch_shapes=[
             pltpu.VMEM((size, LANES), F32),
             pltpu.VMEM(slots, F32),
-            pltpu.SemaphoreType.DMA((groups, part)),
+            pltpu.SemaphoreType.DMA((groups,)),
             pltpu.SemaphoreType.DMA,
         ],
         compiler_params=pltpu.CompilerParams(vmem_limit_bytes=VMEM_LIMIT),
@@ -469,7 +466,7 @@
         pairs = {CORE: swap, OUTER: pairs + [(j, i) for i, j in pairs], FAR: swap}
         blocks |= {CORE: weighted, OUTER: weighted}
         for step in range(len(STEPS)):
-            pairs[step] = [(i, i ^ split * step_mask(i // split, step)) for i in range(device_count)]
+            pairs[step] = [(i, split * partner(i // split, step) + i % split) for i in range(device_count)]
         for place_in_order, item in enumerate(ORDER):
             if item == FAR:
                 blocks[0], blocks[FAR] = arrived_blocks(

time: 34.4 us -> 33.6 us (0.977)
  the two profiles are of different devices: /device:TPU:0 before, /device:TPU:9 now
where the time goes in v6:
time: 33.6 us; the launch traced here: 33.4 us
  starting transfers between devices  20.9 us (62%)
  waiting for transfers between devices  6.37 us (19%)
  Pallas kernels  5.42 us (16%)
  between operations  0.72 us (2%)
    ppermute x10, starting transfers between devices, body(): blocks[item] = lax.ppermute(blocks[item], 'lat', pairs[item])  20.1 us
    ppermute x10, waiting for transfers between devices, body(): blocks[item] = lax.ppermute(blocks[item], 'lat', pairs[item])  6.03 us
    pallas_call x1, Pallas kernels, mixed_blocks(): pl.pallas_call(functools.partial(mix_kernel, rows, split, first), out_sha...  2.43 us
    pallas_call x1, Pallas kernels, place(): pl.pallas_call(functools.partial(place_kernel, 2, sources), out_shape=[ja...  1.32 us
    pallas_call x1, Pallas kernels, raw_fields(): pl.pallas_call(functools.partial(pick_kernel, split, steps), out_shape=[p...  0.92 us
    pallas_call x1, Pallas kernels, arrived_blocks(): pl.pallas_call(functools.partial(arrived_kernel, rows, split, step), out_...  0.75 us
    ppermute x1, starting transfers between devices, body(): sibling = lax.ppermute(view, 'lat', swap)  0.74 us
  transfers between devices with their start and end apart: 11, of which 4 were waited for; matrix products, arithmetic and copies ran while one was open for 0% of the time, Pallas kernels for 12%

profile of v6, /device:TPU:9, one launch (start us, length us, event | category | flops | bytes accessed | tf_op | source)
XLA Modules:
  0.0 33.4 jit_solution(6841954180155457896)
XLA Ops:
  0.6 0.7 %collective-permute-start = (f32[2304,128]{1,0:T(8,128)}, f32[2304,128]{1,0:T(8,128)S(1)}, u32[]{:S(2)}, u32[]{:S(2)}) collective-permute-start(f32[2304,128]{1,0:T(8,128)} %bitcast.11), channel_id=1, source_target_pairs={{0,1},{1,0},{2,3},{3,2},{4,5},{5,4},{6,7},{7,6},{8,9},{9,8},{10,11... | collective-permute-start | bytes 3538952 | tf_op jit(solution)/shard_map/ppermute | solution.py:461
  1.4 0.9 %raw_fields.1 = f32[288,128]{1,0:T(8,128)S(1)} custom-call(f32[2304,128]{1,0:T(8,128)} %bitcast.12), custom_call_target="tpu_custom_call" | custom-call | tf_op jit(solution)/shard_map/raw_fields/pallas_call | solution.py:278
  2.3 0.0 copy-start
  2.3 0.0 copy-start.1
  2.3 0.0 copy-start.2
  2.3 0.0 copy-start.3
  2.3 1.4 %collective-permute-start.1 = (f32[288,128]{1,0:T(8,128)S(1)}, f32[288,128]{1,0:T(8,128)S(1)}, u32[]{:S(2)}, u32[]{:S(2)}) collective-permute-start(f32[288,128]{1,0:T(8,128)S(1)} %raw_fields.1), channel_id=1, source_target_pairs={{0,12},{1,13},{2,14},{3,15},{4,8},{5,9},{6,10},{7,11},{8,4},{9,5},... | collective-permute-start | bytes 442376 | tf_op jit(solution)/shard_map/ppermute | solution.py:478
  3.7 0.3 %collective-permute-done.refs_9_ = f32[2304,128]{1,0:T(8,128)S(1)} collective-permute-done((f32[2304,128]{1,0:T(8,128)}, f32[2304,128]{1,0:T(8,128)S(1)}, u32[]{:S(2)}, u32[]{:S(2)}) %collective-permute-start) | collective-permute-done | bytes 1179680 | tf_op jit(solution)/shard_map/ppermute | solution.py:461
  4.1 2.4 %mixed_blocks.1 = (f32[4,8,1152]{2,1,0:T(8,128)S(1)}, f32[4,8,1152]{2,1,0:T(8,128)S(1)}, f32[4,8,1152]{2,1,0:T(8,128)S(1)}, f32[4,8,1152]{2,1,0:T(8,128)S(1)}, f...) custom-call(f32[2304,128]{1,0:T(8,128)} %bitcast.13, ...), custom_call_target="tpu_custom_call" | custom-call | tf_op jit(solution)/shard_map/mixed_blocks/pallas_call | solution.py:250
  6.5 4.0 %collective-permute-start.2 = (f32[4,8,1152]{2,1,0:T(8,128)S(1)}, f32[4,8,1152]{2,1,0:T(8,128)S(1)}, u32[]{:S(2)}, u32[]{:S(2)}) collective-permute-start(f32[4,8,1152]{2,1,0:T(8,128)S(1)} %get-tuple-element.29), channel_id=1, source_target_pairs={{0,8},{1,9},{2,10},{3,11},{4,12},{5,13},{6,14},{7,15},{8,0},{9,1},... | collective-permute-start | bytes 442376 | tf_op jit(solution)/shard_map/ppermute | solution.py:478
  10.5 1.3 %collective-permute-start.5 = (f32[4,8,1152]{2,1,0:T(8,128)S(1)}, f32[4,8,1152]{2,1,0:T(8,128)S(1)}, u32[]{:S(2)}, u32[]{:S(2)}) collective-permute-start(f32[4,8,1152]{2,1,0:T(8,128)S(1)} %get-tuple-element.37), channel_id=1, source_target_pairs={{0,2},{1,3},{2,0},{3,1},{4,6},{5,7},{6,4},{7,5},{8,10},{9,11},{10,... | collective-permute-start | bytes 442376 | tf_op jit(solution)/shard_map/ppermute | solution.py:478
  11.8 2.7 %collective-permute-start.4 = (f32[4,8,1152]{2,1,0:T(8,128)S(1)}, f32[4,8,1152]{2,1,0:T(8,128)S(1)}, u32[]{:S(2)}, u32[]{:S(2)}) collective-permute-start(f32[4,8,1152]{2,1,0:T(8,128)S(1)} %get-tuple-element.34), channel_id=1, source_target_pairs={{0,10},{1,11},{2,8},{3,9},{4,14},{5,15},{6,12},{7,13},{8,2},{9,3},... | collective-permute-start | bytes 442376 | tf_op jit(solution)/shard_map/ppermute | solution.py:478
  14.6 3.2 %collective-permute-done.2.refs_1_ = f32[4,8,1152]{2,1,0:T(8,128)S(1)} collective-permute-done((f32[4,8,1152]{2,1,0:T(8,128)S(1)}, f32[4,8,1152]{2,1,0:T(8,128)S(1)}, u32[]{:S(2)}, u32[]{:S(2)}) %collective-permute-start.2) | collective-permute-done | bytes 147488 | tf_op jit(solution)/shard_map/ppermute | solution.py:478
  17.7 1.1 %collective-permute-start.7 = (f32[4,8,1152]{2,1,0:T(8,128)S(1)}, f32[4,8,1152]{2,1,0:T(8,128)S(1)}, u32[]{:S(2)}, u32[]{:S(2)}) collective-permute-start(f32[4,8,1152]{2,1,0:T(8,128)S(1)} %get-tuple-element.40), channel_id=1, source_target_pairs={{0,14},{1,15},{2,12},{3,13},{4,10},{5,11},{6,8},{7,9},{8,6},{9,7},... | collective-permute-start | bytes 442376 | tf_op jit(solution)/shard_map/ppermute | solution.py:478
  18.9 0.8 %arrived_blocks.1 = (f32[2,8,1152]{2,1,0:T(8,128)S(1)}, f32[2,8,1152]{2,1,0:T(8,128)S(1)}) custom-call(f32[288,128]{1,0:T(8,128)S(1)} %collective-permute-done.1.raw_ref, f32[8,16,16]{2,1,0:T(8,128)S(1)} %copy-done.1, s32[32]{0:T(128)S(1)} %copy-done.3, bf16[2,1152,256]{2,1,0:T(8,128)(2,1)S(1)} %copy-done, f32[48,256]{1,0:T(8,128)S(1)} %copy-done.2), custom_call_target="tpu_custom_call" | custom-call | tf_op jit(solution)/shard_map/arrived_blocks/pallas_call | solution.py:308
  19.6 2.7 %collective-permute-start.8 = (f32[2,8,1152]{2,1,0:T(8,128)S(1)}, f32[2,8,1152]{2,1,0:T(8,128)S(1)}, u32[]{:S(2)}, u32[]{:S(2)}) collective-permute-start(f32[2,8,1152]{2,1,0:T(8,128)S(1)} %get-tuple-element.42), channel_id=1, source_target_pairs={{0,1},{1,0},{2,3},{3,2},{4,5},{5,4},{6,7},{7,6},{8,9},{9,8},{10,11... | collective-permute-start | bytes 221192 | tf_op jit(solution)/shard_map/ppermute | solution.py:478
  22.3 0.0 collective-permute-done.3.refs_2_
  22.3 3.9 %collective-permute-start.10 = (f32[2,4,1152]{2,1,0:T(4,128)S(1)}, f32[2,4,1152]{2,1,0:T(4,128)S(1)}, u32[]{:S(2)}, u32[]{:S(2)}) collective-permute-start(f32[2,4,1152]{2,1,0:T(4,128)S(1)} %get-tuple-element.45.refs_10_), channel_id=1, source_target_pairs={{1,2},{3,4},{5,6},{7,8},{9,10},{11,12},{13,14},{2,1},{4,3},{6,5},{... | collective-permute-start | bytes 110600 | tf_op jit(solution)/shard_map/ppermute | solution.py:478
  26.2 0.0 collective-permute-done.4.refs_3_
  26.2 3.0 %collective-permute-start.9 = (f32[2,4,1152]{2,1,0:T(4,128)S(1)}, f32[2,4,1152]{2,1,0:T(4,128)S(1)}, u32[]{:S(2)}, u32[]{:S(2)}) collective-permute-start(f32[2,4,1152]{2,1,0:T(4,128)S(1)} %get-tuple-element.45.refs_10_), channel_id=1, source_target_pairs={{0,1},{1,0},{2,3},{3,2},{4,5},{5,4},{6,7},{7,6},{8,9},{9,8},{10,11... | collective-permute-start | bytes 110600 | tf_op jit(solution)/shard_map/ppermute | solution.py:478
  29.2 0.9 %collective-permute-done.9.refs_11_ = f32[2,4,1152]{2,1,0:T(4,128)S(1)} collective-permute-done((f32[2,4,1152]{2,1,0:T(4,128)S(1)}, f32[2,4,1152]{2,1,0:T(4,128)S(1)}, u32[]{:S(2)}, u32[]{:S(2)}) %collective-permute-start.9) | collective-permute-done | bytes 36896 | tf_op jit(solution)/shard_map/ppermute | solution.py:478
  30.1 0.0 collective-permute-done.8.refs_8_
  30.1 2.0 %collective-permute-done.7.refs_6_ = f32[4,8,1152]{2,1,0:T(8,128)S(1)} collective-permute-done((f32[4,8,1152]{2,1,0:T(8,128)S(1)}, f32[4,8,1152]{2,1,0:T(8,128)S(1)}, u32[]{:S(2)}, u32[]{:S(2)}) %collective-permute-start.7) | collective-permute-done | bytes 147488 | tf_op jit(solution)/shard_map/ppermute | solution.py:478
  32.1 1.3 %place.1 = (f32[8,288,128]{2,1,0:T(8,128)}, f32[6,4,1152]{2,1,0:T(4,128)}) custom-call(f32[2,8,1152]{2,1,0:T(8,128)S(1)} %get-tuple-element.27.refs_0_, f32[4,8,1152]{2,1,0:T(8,128)S(1)} %collective-permute-done.2.refs_1_, f32[4,8,1152]{2,1,0:T(8,128)S(1)} %collective-permute-done.3.refs_2_, f32[4,8,1152]{2,1,0:T(8,128)S(1)} %collective-permute-done.4.refs_3_, ...), custom_call_target="tpu_custom_call" | custom-call | tf_op jit(solution)/shard_map/place/pallas_call | solution.py:412
  (10 shorter events, 0.0 us)
Async XLA Ops:
  0.6 3.4 %collective-permute-start = (f32[2304,128]{1,0:T(8,128)}, f32[2304,128]{1,0:T(8,128)S(1)}, u32[]{:S(2)}, u32[]{:S(2)}) collective-permute-start(f32[2304,128]{1,0:T(8,128)} %bitcast.11), channel_id=1, source_target_pairs={{0,1},{1,0},{2,3},{3,2},{4,5},{5,4},{6,7},{7,6},{8,9},{9,8},{10,11... | collective-permute-start | bytes 3538952 | tf_op jit(solution)/shard_map/ppermute | solution.py:461
  2.3 16.6 %copy-start = (bf16[2,1152,256]{2,1,0:T(8,128)(2,1)S(1)}, bf16[2,1152,256]{2,1,0:T(8,128)(2,1)}, u32[]{:S(2)}) copy-start(bf16[2,1152,256]{2,1,0:T(8,128)(2,1)} %constant.4.clone.refs_7_.table_ref) | copy-start | bytes 3538948
  2.3 16.6 %copy-start.1 = (f32[8,16,16]{2,1,0:T(8,128)S(1)}, f32[8,16,16]{2,1,0:T(8,128)}, u32[]{:S(2)}) copy-start(f32[8,16,16]{2,1,0:T(8,128)} %mix_ref.1) | copy-start | bytes 24580
  2.3 16.5 %copy-start.2 = (f32[48,256]{1,0:T(8,128)S(1)}, f32[48,256]{1,0:T(8,128)}, u32[]{:S(2)}) copy-start(f32[48,256]{1,0:T(8,128)} %constant.5.clone.refs_8_.row_ref) | copy-start | bytes 147460
  2.3 16.5 %copy-start.3 = (s32[32]{0:T(128)S(1)}, s32[32]{0:T(128)}, u32[]{:S(2)}) copy-start(s32[32]{0:T(128)} %mask_ref.1) | copy-start | bytes 388
  2.3 12.2 %collective-permute-start.1 = (f32[288,128]{1,0:T(8,128)S(1)}, f32[288,128]{1,0:T(8,128)S(1)}, u32[]{:S(2)}, u32[]{:S(2)}) collective-permute-start(f32[288,128]{1,0:T(8,128)S(1)} %raw_fields.1), channel_id=1, source_target_pairs={{0,12},{1,13},{2,14},{3,15},{4,8},{5,9},{6,10},{7,11},{8,4},{9,5},... | collective-permute-start | bytes 442376 | tf_op jit(solution)/shard_map/ppermute | solution.py:478
  6.5 11.2 %collective-permute-start.2 = (f32[4,8,1152]{2,1,0:T(8,128)S(1)}, f32[4,8,1152]{2,1,0:T(8,128)S(1)}, u32[]{:S(2)}, u32[]{:S(2)}) collective-permute-start(f32[4,8,1152]{2,1,0:T(8,128)S(1)} %get-tuple-element.29), channel_id=1, source_target_pairs={{0,8},{1,9},{2,10},{3,11},{4,12},{5,13},{6,14},{7,15},{8,0},{9,1},... | collective-permute-start | bytes 442376 | tf_op jit(solution)/shard_map/ppermute | solution.py:478
  10.5 9.1 %collective-permute-start.5 = (f32[4,8,1152]{2,1,0:T(8,128)S(1)}, f32[4,8,1152]{2,1,0:T(8,128)S(1)}, u32[]{:S(2)}, u32[]{:S(2)}) collective-permute-start(f32[4,8,1152]{2,1,0:T(8,128)S(1)} %get-tuple-element.37), channel_id=1, source_target_pairs={{0,2},{1,3},{2,0},{3,1},{4,6},{5,7},{6,4},{7,5},{8,10},{9,11},{10,... | collective-permute-start | bytes 442376 | tf_op jit(solution)/shard_map/ppermute | solution.py:478
  11.8 10.5 %collective-permute-start.3 = (f32[4,8,1152]{2,1,0:T(8,128)S(1)}, f32[4,8,1152]{2,1,0:T(8,128)S(1)}, u32[]{:S(2)}, u32[]{:S(2)}) collective-permute-start(f32[4,8,1152]{2,1,0:T(8,128)S(1)} %get-tuple-element.32), channel_id=1, source_target_pairs={{0,6},{1,7},{2,4},{3,5},{4,2},{5,3},{6,0},{7,1},{8,14},{9,15},{10,... | collective-permute-start | bytes 442376 | tf_op jit(solution)/shard_map/ppermute | solution.py:478
  11.8 14.4 %collective-permute-start.4 = (f32[4,8,1152]{2,1,0:T(8,128)S(1)}, f32[4,8,1152]{2,1,0:T(8,128)S(1)}, u32[]{:S(2)}, u32[]{:S(2)}) collective-permute-start(f32[4,8,1152]{2,1,0:T(8,128)S(1)} %get-tuple-element.34), channel_id=1, source_target_pairs={{0,10},{1,11},{2,8},{3,9},{4,14},{5,15},{6,12},{7,13},{8,2},{9,3},... | collective-permute-start | bytes 442376 | tf_op jit(solution)/shard_map/ppermute | solution.py:478
  14.6 14.7 %collective-permute-start.6 = (f32[4,8,1152]{2,1,0:T(8,128)S(1)}, f32[4,8,1152]{2,1,0:T(8,128)S(1)}, u32[]{:S(2)}, u32[]{:S(2)}) collective-permute-start(f32[4,8,1152]{2,1,0:T(8,128)S(1)} %get-tuple-element.39), channel_id=1, source_target_pairs={{0,4},{1,5},{2,6},{3,7},{4,0},{5,1},{6,2},{7,3},{8,12},{9,13},{10,... | collective-permute-start | bytes 442376 | tf_op jit(solution)/shard_map/ppermute | solution.py:478
  17.7 14.4 %collective-permute-start.7 = (f32[4,8,1152]{2,1,0:T(8,128)S(1)}, f32[4,8,1152]{2,1,0:T(8,128)S(1)}, u32[]{:S(2)}, u32[]{:S(2)}) collective-permute-start(f32[4,8,1152]{2,1,0:T(8,128)S(1)} %get-tuple-element.40), channel_id=1, source_target_pairs={{0,14},{1,15},{2,12},{3,13},{4,10},{5,11},{6,8},{7,9},{8,6},{9,7},... | collective-permute-start | bytes 442376 | tf_op jit(solution)/shard_map/ppermute | solution.py:478
  19.6 10.5 %collective-permute-start.8 = (f32[2,8,1152]{2,1,0:T(8,128)S(1)}, f32[2,8,1152]{2,1,0:T(8,128)S(1)}, u32[]{:S(2)}, u32[]{:S(2)}) collective-permute-start(f32[2,8,1152]{2,1,0:T(8,128)S(1)} %get-tuple-element.42), channel_id=1, source_target_pairs={{0,1},{1,0},{2,3},{3,2},{4,5},{5,4},{6,7},{7,6},{8,9},{9,8},{10,11... | collective-permute-start | bytes 221192 | tf_op jit(solution)/shard_map/ppermute | solution.py:478
  22.3 6.9 %collective-permute-start.10 = (f32[2,4,1152]{2,1,0:T(4,128)S(1)}, f32[2,4,1152]{2,1,0:T(4,128)S(1)}, u32[]{:S(2)}, u32[]{:S(2)}) collective-permute-start(f32[2,4,1152]{2,1,0:T(4,128)S(1)} %get-tuple-element.45.refs_10_), channel_id=1, source_target_pairs={{1,2},{3,4},{5,6},{7,8},{9,10},{11,12},{13,14},{2,1},{4,3},{6,5},{... | collective-permute-start | bytes 110600 | tf_op jit(solution)/shard_map/ppermute | solution.py:478
  26.2 3.9 %collective-permute-start.9 = (f32[2,4,1152]{2,1,0:T(4,128)S(1)}, f32[2,4,1152]{2,1,0:T(4,128)S(1)}, u32[]{:S(2)}, u32[]{:S(2)}) collective-permute-start(f32[2,4,1152]{2,1,0:T(4,128)S(1)} %get-tuple-element.45.refs_10_), channel_id=1, source_target_pairs={{0,1},{1,0},{2,3},{3,2},{4,5},{5,4},{6,7},{7,6},{8,9},{9,8},{10,11... | collective-permute-start | bytes 110600 | tf_op jit(solution)/shard_map/ppermute | solution.py:478

commit v7 on v6

--- a/solution.py
+++ b/solution.py
@@ -12,7 +12,7 @@
 COSCUT = 0.5
 LANES = 128
 SUBLANES = 8
-STEPS = (6, 4, 3, 5, 1, 2, 7)
+STEPS = (6, 7, 2, 5, 1, 3, 4)
 CORE, OUTER, FAR = 8, 9, 10
 ORDER = (0, 1, 2, 3, 4, 5, 6, OUTER, CORE, FAR)
 WINDOW = 5

time: 33.6 us -> 33.2 us (0.988)
  the two profiles are of different devices: /device:TPU:9 before, /device:TPU:0 now
where the time goes in v7:
time: 33.2 us; the launch traced here: 33 us
  starting transfers between devices  15.7 us (47%)
  waiting for transfers between devices  9.55 us (29%)
  Pallas kernels  7.05 us (21%)
  between operations  0.71 us (2%)
    ppermute x10, starting transfers between devices, body(): blocks[item] = lax.ppermute(blocks[item], 'lat', pairs[item])  15.2 us
    ppermute x10, waiting for transfers between devices, body(): blocks[item] = lax.ppermute(blocks[item], 'lat', pairs[item])  9.55 us
    pallas_call x1, Pallas kernels, mixed_blocks(): pl.pallas_call(functools.partial(mix_kernel, rows, split, first), out_sha...  4.1 us
    pallas_call x1, Pallas kernels, place(): pl.pallas_call(functools.partial(place_kernel, 2, sources), out_shape=[ja...  1.28 us
    pallas_call x1, Pallas kernels, raw_fields(): pl.pallas_call(functools.partial(pick_kernel, split, steps), out_shape=[p...  0.92 us
    pallas_call x1, Pallas kernels, arrived_blocks(): pl.pallas_call(functools.partial(arrived_kernel, rows, split, step), out_...  0.75 us
  transfers between devices with their start and end apart: 11, of which 5 were waited for; matrix products, arithmetic and copies ran while one was open for 0% of the time, Pallas kernels for 17%

profile of v7, /device:TPU:0, one launch (start us, length us, event | category | flops | bytes accessed | tf_op | source)
XLA Modules:
  0.0 33.0 jit_solution(11572971847593019252)
XLA Ops:
  0.6 0.5 %collective-permute-start = (f32[2304,128]{1,0:T(8,128)}, f32[2304,128]{1,0:T(8,128)S(1)}, u32[]{:S(2)}, u32[]{:S(2)}) collective-permute-start(f32[2304,128]{1,0:T(8,128)} %bitcast.11), channel_id=1, source_target_pairs={{0,1},{1,0},{2,3},{3,2},{4,5},{5,4},{6,7},{7,6},{8,9},{9,8},{10,11... | collective-permute-start | bytes 3538952 | tf_op jit(solution)/shard_map/ppermute | solution.py:461
  1.1 0.9 %raw_fields.1 = f32[288,128]{1,0:T(8,128)S(1)} custom-call(f32[2304,128]{1,0:T(8,128)} %bitcast.12), custom_call_target="tpu_custom_call" | custom-call | tf_op jit(solution)/shard_map/raw_fields/pallas_call | solution.py:278
  2.1 0.0 copy-start
  2.1 0.0 copy-start.1
  2.1 0.0 copy-start.2
  2.1 0.0 copy-start.3
  2.1 4.7 %collective-permute-start.1 = (f32[288,128]{1,0:T(8,128)S(1)}, f32[288,128]{1,0:T(8,128)S(1)}, u32[]{:S(2)}, u32[]{:S(2)}) collective-permute-start(f32[288,128]{1,0:T(8,128)S(1)} %raw_fields.1), channel_id=1, source_target_pairs={{0,12},{1,13},{2,14},{3,15},{4,8},{5,9},{6,10},{7,11},{8,4},{9,5},... | collective-permute-start | bytes 442376 | tf_op jit(solution)/shard_map/ppermute | solution.py:478
  6.8 0.0 collective-permute-done.refs_9_
  6.8 4.1 %mixed_blocks.1 = (f32[4,8,1152]{2,1,0:T(8,128)S(1)}, f32[4,8,1152]{2,1,0:T(8,128)S(1)}, f32[4,8,1152]{2,1,0:T(8,128)S(1)}, f32[4,8,1152]{2,1,0:T(8,128)S(1)}, f...) custom-call(f32[2304,128]{1,0:T(8,128)} %bitcast.13, ...), custom_call_target="tpu_custom_call" | custom-call | tf_op jit(solution)/shard_map/mixed_blocks/pallas_call | solution.py:250
  10.9 3.0 %collective-permute-start.2 = (f32[4,8,1152]{2,1,0:T(8,128)S(1)}, f32[4,8,1152]{2,1,0:T(8,128)S(1)}, u32[]{:S(2)}, u32[]{:S(2)}) collective-permute-start(f32[4,8,1152]{2,1,0:T(8,128)S(1)} %get-tuple-element.29), channel_id=1, source_target_pairs={{0,14},{1,15},{2,12},{3,13},{4,10},{5,11},{6,8},{7,9},{8,6},{9,7},... | collective-permute-start | bytes 442376 | tf_op jit(solution)/shard_map/ppermute | solution.py:478
  13.9 0.5 %collective-permute-start.5 = (f32[4,8,1152]{2,1,0:T(8,128)S(1)}, f32[4,8,1152]{2,1,0:T(8,128)S(1)}, u32[]{:S(2)}, u32[]{:S(2)}) collective-permute-start(f32[4,8,1152]{2,1,0:T(8,128)S(1)} %get-tuple-element.37), channel_id=1, source_target_pairs={{0,2},{1,3},{2,0},{3,1},{4,6},{5,7},{6,4},{7,5},{8,10},{9,11},{10,... | collective-permute-start | bytes 442376 | tf_op jit(solution)/shard_map/ppermute | solution.py:478
  14.4 0.0 collective-permute-start.3
  14.4 3.3 %collective-permute-start.4 = (f32[4,8,1152]{2,1,0:T(8,128)S(1)}, f32[4,8,1152]{2,1,0:T(8,128)S(1)}, u32[]{:S(2)}, u32[]{:S(2)}) collective-permute-start(f32[4,8,1152]{2,1,0:T(8,128)S(1)} %get-tuple-element.34), channel_id=1, source_target_pairs={{0,10},{1,11},{2,8},{3,9},{4,14},{5,15},{6,12},{7,13},{8,2},{9,3},... | collective-permute-start | bytes 442376 | tf_op jit(solution)/shard_map/ppermute | solution.py:478
  17.8 0.0 collective-permute-done.1.raw_ref
  17.8 2.7 %collective-permute-done.2.refs_1_ = f32[4,8,1152]{2,1,0:T(8,128)S(1)} collective-permute-done((f32[4,8,1152]{2,1,0:T(8,128)S(1)}, f32[4,8,1152]{2,1,0:T(8,128)S(1)}, u32[]{:S(2)}, u32[]{:S(2)}) %collective-permute-start.2) | collective-permute-done | bytes 147488 | tf_op jit(solution)/shard_map/ppermute | solution.py:478
  20.4 2.5 %collective-permute-start.7 = (f32[4,8,1152]{2,1,0:T(8,128)S(1)}, f32[4,8,1152]{2,1,0:T(8,128)S(1)}, u32[]{:S(2)}, u32[]{:S(2)}) collective-permute-start(f32[4,8,1152]{2,1,0:T(8,128)S(1)} %get-tuple-element.40), channel_id=1, source_target_pairs={{0,8},{1,9},{2,10},{3,11},{4,12},{5,13},{6,14},{7,15},{8,0},{9,1},... | collective-permute-start | bytes 442376 | tf_op jit(solution)/shard_map/ppermute | solution.py:478
  22.9 0.8 %arrived_blocks.1 = (f32[2,8,1152]{2,1,0:T(8,128)S(1)}, f32[2,8,1152]{2,1,0:T(8,128)S(1)}) custom-call(f32[288,128]{1,0:T(8,128)S(1)} %collective-permute-done.1.raw_ref, f32[8,16,16]{2,1,0:T(8,128)S(1)} %copy-done.1, s32[32]{0:T(128)S(1)} %copy-done.3, bf16[2,1152,256]{2,1,0:T(8,128)(2,1)S(1)} %copy-done, f32[48,256]{1,0:T(8,128)S(1)} %copy-done.2), custom_call_target="tpu_custom_call" | custom-call | tf_op jit(solution)/shard_map/arrived_blocks/pallas_call | solution.py:308
  23.7 1.0 %collective-permute-done.5.refs_4_ = f32[4,8,1152]{2,1,0:T(8,128)S(1)} collective-permute-done((f32[4,8,1152]{2,1,0:T(8,128)S(1)}, f32[4,8,1152]{2,1,0:T(8,128)S(1)}, u32[]{:S(2)}, u32[]{:S(2)}) %collective-permute-start.5) | collective-permute-done | bytes 147488 | tf_op jit(solution)/shard_map/ppermute | solution.py:478
  24.7 1.9 %collective-permute-done.3.refs_2_ = f32[4,8,1152]{2,1,0:T(8,128)S(1)} collective-permute-done((f32[4,8,1152]{2,1,0:T(8,128)S(1)}, f32[4,8,1152]{2,1,0:T(8,128)S(1)}, u32[]{:S(2)}, u32[]{:S(2)}) %collective-permute-start.3) | collective-permute-done | bytes 147488 | tf_op jit(solution)/shard_map/ppermute | solution.py:478
  26.6 0.7 %collective-permute-start.10 = (f32[2,4,1152]{2,1,0:T(4,128)S(1)}, f32[2,4,1152]{2,1,0:T(4,128)S(1)}, u32[]{:S(2)}, u32[]{:S(2)}) collective-permute-start(f32[2,4,1152]{2,1,0:T(4,128)S(1)} %get-tuple-element.45.refs_10_), channel_id=1, source_target_pairs={{1,2},{3,4},{5,6},{7,8},{9,10},{11,12},{13,14},{2,1},{4,3},{6,5},{... | collective-permute-start | bytes 110600 | tf_op jit(solution)/shard_map/ppermute | solution.py:478
  27.3 0.5 %collective-permute-done.4.refs_3_ = f32[4,8,1152]{2,1,0:T(8,128)S(1)} collective-permute-done((f32[4,8,1152]{2,1,0:T(8,128)S(1)}, f32[4,8,1152]{2,1,0:T(8,128)S(1)}, u32[]{:S(2)}, u32[]{:S(2)}) %collective-permute-start.4) | collective-permute-done | bytes 147488 | tf_op jit(solution)/shard_map/ppermute | solution.py:478
  27.8 0.5 %collective-permute-start.9 = (f32[2,4,1152]{2,1,0:T(4,128)S(1)}, f32[2,4,1152]{2,1,0:T(4,128)S(1)}, u32[]{:S(2)}, u32[]{:S(2)}) collective-permute-start(f32[2,4,1152]{2,1,0:T(4,128)S(1)} %get-tuple-element.45.refs_10_), channel_id=1, source_target_pairs={{0,1},{1,0},{2,3},{3,2},{4,5},{5,4},{6,7},{7,6},{8,9},{9,8},{10,11... | collective-permute-start | bytes 110600 | tf_op jit(solution)/shard_map/ppermute | solution.py:478
  28.3 3.4 %collective-permute-done.6.refs_5_ = f32[4,8,1152]{2,1,0:T(8,128)S(1)} collective-permute-done((f32[4,8,1152]{2,1,0:T(8,128)S(1)}, f32[4,8,1152]{2,1,0:T(8,128)S(1)}, u32[]{:S(2)}, u32[]{:S(2)}) %collective-permute-start.6) | collective-permute-done | bytes 147488 | tf_op jit(solution)/shard_map/ppermute | solution.py:478
  31.7 1.3 %place.1 = (f32[8,288,128]{2,1,0:T(8,128)}, f32[6,4,1152]{2,1,0:T(4,128)}) custom-call(f32[2,8,1152]{2,1,0:T(8,128)S(1)} %get-tuple-element.27.refs_0_, f32[4,8,1152]{2,1,0:T(8,128)S(1)} %collective-permute-done.2.refs_1_, f32[4,8,1152]{2,1,0:T(8,128)S(1)} %collective-permute-done.3.refs_2_, f32[4,8,1152]{2,1,0:T(8,128)S(1)} %collective-permute-done.4.refs_3_, ...), custom_call_target="tpu_custom_call" | custom-call | tf_op jit(solution)/shard_map/place/pallas_call | solution.py:412
  (10 shorter events, 0.0 us)
Async XLA Ops:
  0.6 6.2 %collective-permute-start = (f32[2304,128]{1,0:T(8,128)}, f32[2304,128]{1,0:T(8,128)S(1)}, u32[]{:S(2)}, u32[]{:S(2)}) collective-permute-start(f32[2304,128]{1,0:T(8,128)} %bitcast.11), channel_id=1, source_target_pairs={{0,1},{1,0},{2,3},{3,2},{4,5},{5,4},{6,7},{7,6},{8,9},{9,8},{10,11... | collective-permute-start | bytes 3538952 | tf_op jit(solution)/shard_map/ppermute | solution.py:461
  2.1 20.8 %copy-start = (bf16[2,1152,256]{2,1,0:T(8,128)(2,1)S(1)}, bf16[2,1152,256]{2,1,0:T(8,128)(2,1)}, u32[]{:S(2)}) copy-start(bf16[2,1152,256]{2,1,0:T(8,128)(2,1)} %constant.4.clone.refs_7_.table_ref) | copy-start | bytes 3538948
  2.1 20.8 %copy-start.1 = (f32[8,16,16]{2,1,0:T(8,128)S(1)}, f32[8,16,16]{2,1,0:T(8,128)}, u32[]{:S(2)}) copy-start(f32[8,16,16]{2,1,0:T(8,128)} %mix_ref.1) | copy-start | bytes 24580
  2.1 20.8 %copy-start.2 = (f32[48,256]{1,0:T(8,128)S(1)}, f32[48,256]{1,0:T(8,128)}, u32[]{:S(2)}) copy-start(f32[48,256]{1,0:T(8,128)} %constant.5.clone.refs_8_.row_ref) | copy-start | bytes 147460
  2.1 20.8 %copy-start.3 = (s32[32]{0:T(128)S(1)}, s32[32]{0:T(128)}, u32[]{:S(2)}) copy-start(s32[32]{0:T(128)} %mask_ref.1) | copy-start | bytes 388
  2.1 15.6 %collective-permute-start.1 = (f32[288,128]{1,0:T(8,128)S(1)}, f32[288,128]{1,0:T(8,128)S(1)}, u32[]{:S(2)}, u32[]{:S(2)}) collective-permute-start(f32[288,128]{1,0:T(8,128)S(1)} %raw_fields.1), channel_id=1, source_target_pairs={{0,12},{1,13},{2,14},{3,15},{4,8},{5,9},{6,10},{7,11},{8,4},{9,5},... | collective-permute-start | bytes 442376 | tf_op jit(solution)/shard_map/ppermute | solution.py:478
  10.9 9.5 %collective-permute-start.2 = (f32[4,8,1152]{2,1,0:T(8,128)S(1)}, f32[4,8,1152]{2,1,0:T(8,128)S(1)}, u32[]{:S(2)}, u32[]{:S(2)}) collective-permute-start(f32[4,8,1152]{2,1,0:T(8,128)S(1)} %get-tuple-element.29), channel_id=1, source_target_pairs={{0,14},{1,15},{2,12},{3,13},{4,10},{5,11},{6,8},{7,9},{8,6},{9,7},... | collective-permute-start | bytes 442376 | tf_op jit(solution)/shard_map/ppermute | solution.py:478
  13.9 10.8 %collective-permute-start.5 = (f32[4,8,1152]{2,1,0:T(8,128)S(1)}, f32[4,8,1152]{2,1,0:T(8,128)S(1)}, u32[]{:S(2)}, u32[]{:S(2)}) collective-permute-start(f32[4,8,1152]{2,1,0:T(8,128)S(1)} %get-tuple-element.37), channel_id=1, source_target_pairs={{0,2},{1,3},{2,0},{3,1},{4,6},{5,7},{6,4},{7,5},{8,10},{9,11},{10,... | collective-permute-start | bytes 442376 | tf_op jit(solution)/shard_map/ppermute | solution.py:478
  14.4 12.2 %collective-permute-start.3 = (f32[4,8,1152]{2,1,0:T(8,128)S(1)}, f32[4,8,1152]{2,1,0:T(8,128)S(1)}, u32[]{:S(2)}, u32[]{:S(2)}) collective-permute-start(f32[4,8,1152]{2,1,0:T(8,128)S(1)} %get-tuple-element.32), channel_id=1, source_target_pairs={{0,4},{1,5},{2,6},{3,7},{4,0},{5,1},{6,2},{7,3},{8,12},{9,13},{10,... | collective-permute-start | bytes 442376 | tf_op jit(solution)/shard_map/ppermute | solution.py:478
  14.4 13.4 %collective-permute-start.4 = (f32[4,8,1152]{2,1,0:T(8,128)S(1)}, f32[4,8,1152]{2,1,0:T(8,128)S(1)}, u32[]{:S(2)}, u32[]{:S(2)}) collective-permute-start(f32[4,8,1152]{2,1,0:T(8,128)S(1)} %get-tuple-element.34), channel_id=1, source_target_pairs={{0,10},{1,11},{2,8},{3,9},{4,14},{5,15},{6,12},{7,13},{8,2},{9,3},... | collective-permute-start | bytes 442376 | tf_op jit(solution)/shard_map/ppermute | solution.py:478
  17.8 13.9 %collective-permute-start.6 = (f32[4,8,1152]{2,1,0:T(8,128)S(1)}, f32[4,8,1152]{2,1,0:T(8,128)S(1)}, u32[]{:S(2)}, u32[]{:S(2)}) collective-permute-start(f32[4,8,1152]{2,1,0:T(8,128)S(1)} %get-tuple-element.39), channel_id=1, source_target_pairs={{0,6},{1,7},{2,4},{3,5},{4,2},{5,3},{6,0},{7,1},{8,14},{9,15},{10,... | collective-permute-start | bytes 442376 | tf_op jit(solution)/shard_map/ppermute | solution.py:478
  20.4 11.3 %collective-permute-start.7 = (f32[4,8,1152]{2,1,0:T(8,128)S(1)}, f32[4,8,1152]{2,1,0:T(8,128)S(1)}, u32[]{:S(2)}, u32[]{:S(2)}) collective-permute-start(f32[4,8,1152]{2,1,0:T(8,128)S(1)} %get-tuple-element.40), channel_id=1, source_target_pairs={{0,8},{1,9},{2,10},{3,11},{4,12},{5,13},{6,14},{7,15},{8,0},{9,1},... | collective-permute-start | bytes 442376 | tf_op jit(solution)/shard_map/ppermute | solution.py:478
  24.7 7.0 %collective-permute-start.8 = (f32[2,8,1152]{2,1,0:T(8,128)S(1)}, f32[2,8,1152]{2,1,0:T(8,128)S(1)}, u32[]{:S(2)}, u32[]{:S(2)}) collective-permute-start(f32[2,8,1152]{2,1,0:T(8,128)S(1)} %get-tuple-element.42), channel_id=1, source_target_pairs={{0,1},{1,0},{2,3},{3,2},{4,5},{5,4},{6,7},{7,6},{8,9},{9,8},{10,11... | collective-permute-start | bytes 221192 | tf_op jit(solution)/shard_map/ppermute | solution.py:478
  26.6 5.1 %collective-permute-start.10 = (f32[2,4,1152]{2,1,0:T(4,128)S(1)}, f32[2,4,1152]{2,1,0:T(4,128)S(1)}, u32[]{:S(2)}, u32[]{:S(2)}) collective-permute-start(f32[2,4,1152]{2,1,0:T(4,128)S(1)} %get-tuple-element.45.refs_10_), channel_id=1, source_target_pairs={{1,2},{3,4},{5,6},{7,8},{9,10},{11,12},{13,14},{2,1},{4,3},{6,5},{... | collective-permute-start | bytes 110600 | tf_op jit(solution)/shard_map/ppermute | solution.py:478
  27.8 3.9 %collective-permute-start.9 = (f32[2,4,1152]{2,1,0:T(4,128)S(1)}, f32[2,4,1152]{2,1,0:T(4,128)S(1)}, u32[]{:S(2)}, u32[]{:S(2)}) collective-permute-start(f32[2,4,1152]{2,1,0:T(4,128)S(1)} %get-tuple-element.45.refs_10_), channel_id=1, source_target_pairs={{0,1},{1,0},{2,3},{3,2},{4,5},{5,4},{6,7},{7,6},{8,9},{9,8},{10,11... | collective-permute-start | bytes 110600 | tf_op jit(solution)/shard_map/ppermute | solution.py:478
